TPU v7x, 32 devices: a whole 2x2x4 slice. The times are simulated.
32 devices in a mesh: tm: 8 (over z, y), fsdp: 4 (over x, core).
Axes of the slice: x: 2, y: 2, z: 4, core: 2. Of those that a mesh axis runs over, the one named last changes fastest.
Arguments:
- queries: bfloat16 [32, 128, 12, 128], P('tm', 'fsdp'), may hold values from -5 to 5
- key_states: bfloat16 [32, 128, 12, 128], P('tm', 'fsdp'), may hold values from -5 to 5
- value_states: bfloat16 [32, 128, 12, 128], P('tm', 'fsdp'), may hold values from -6 to 6
- out_grad: bfloat16 [32, 128, 3072], P('tm', 'fsdp'), may hold values from -6 to 6
- out_proj: bfloat16 [1536, 3072], P('fsdp'), may hold values from -0.109375 to 0.109375
Outputs:
- query_grad: bfloat16 [32, 128, 12, 128], P('tm', 'fsdp')
- key_grad: bfloat16 [32, 128, 12, 128], P('tm', 'fsdp')
- value_grad: bfloat16 [32, 128, 12, 128], P('tm', 'fsdp')
All inputs are finite; a program needn't handle non-finite values.
Results may differ from a plain program's by a relative error of at most 0.03.
Values may be sent and summed in bfloat16 or wider, within the bound.
No kernel may reach another device: no remote copies, remote signals or barrier semaphores. Data moves between devices by JAX's collectives and lax.ppermute only.
A program may use at most 64 MiB of HBM per device.

v0:
```python
import jax
import jax.numpy as jnp
from jax import lax
from jax.sharding import PartitionSpec as P


def attend_back(query_block, key_block, value_block, grad_block):
    score_scale = query_block.shape[-1] ** (-0.5)
    scores = (
        jnp.einsum("fphd,gphd->phfg", query_block, key_block, preferred_element_type=jnp.float32)
        * score_scale
    )
    peak = jnp.max(scores, axis=-1, keepdims=True)
    expo = jnp.exp(scores - peak)
    probs = expo / jnp.sum(expo, axis=-1, keepdims=True)
    probs_b = probs.astype(jnp.bfloat16)
    attn_out = jnp.einsum(
        "phfg,gphd->fphd", probs_b, value_block, preferred_element_type=jnp.float32
    )
    row_delta = jnp.einsum("fphd,fphd->phf", grad_block.astype(jnp.float32), attn_out)
    dprobs = jnp.einsum(
        "fphd,gphd->phfg", grad_block, value_block, preferred_element_type=jnp.float32
    )
    dscores = (probs * (dprobs - row_delta[..., None])).astype(jnp.bfloat16)
    query_grad = (
        jnp.einsum("phfg,gphd->fphd", dscores, key_block, preferred_element_type=jnp.float32)
        * score_scale
    ).astype(jnp.bfloat16)
    key_grad = (
        jnp.einsum("phfg,fphd->gphd", dscores, query_block, preferred_element_type=jnp.float32)
        * score_scale
    ).astype(jnp.bfloat16)
    value_grad = jnp.einsum(
        "phfg,fphd->gphd", probs_b, grad_block, preferred_element_type=jnp.float32
    ).astype(jnp.bfloat16)
    return (query_grad, key_grad, value_grad)


def send_back(grads):
    return (
        lax.all_to_all(grads[0], "tm", split_axis=0, concat_axis=1, tiled=True),
        lax.all_to_all(grads[1], "tm", split_axis=0, concat_axis=1, tiled=True),
        lax.all_to_all(grads[2], "tm", split_axis=0, concat_axis=1, tiled=True),
    )


def body(queries, key_states, value_states, out_grad, out_proj):
    frames_dev, pos_dev, heads, head_size = queries.shape
    width = out_grad.shape[-1]
    flat = out_grad.reshape(frames_dev * pos_dev, width)
    grad_flat = lax.dot_general(
        flat,
        lax.all_gather(out_proj, "fsdp", axis=0, tiled=True),
        (((1,), (1,)), ((), ())),
        preferred_element_type=jnp.float32,
    ).astype(jnp.bfloat16)
    grad_attn = grad_flat.reshape(frames_dev, pos_dev, heads, head_size)
    results = send_back(
        attend_back(
            lax.all_to_all(queries, "tm", split_axis=1, concat_axis=0, tiled=True),
            lax.all_to_all(key_states, "tm", split_axis=1, concat_axis=0, tiled=True),
            lax.all_to_all(value_states, "tm", split_axis=1, concat_axis=0, tiled=True),
            lax.all_to_all(grad_attn, "tm", split_axis=1, concat_axis=0, tiled=True),
        )
    )
    return (results[0], results[1], results[2])


def solution(mesh):
    return jax.shard_map(
        body,
        mesh=mesh,
        in_specs=(
            P("tm", "fsdp", None, None),
            P("tm", "fsdp", None, None),
            P("tm", "fsdp", None, None),
            P("tm", "fsdp", None),
            P("fsdp", None),
        ),
        out_specs=(
            P("tm", "fsdp", None, None),
            P("tm", "fsdp", None, None),
            P("tm", "fsdp", None, None),
        ),
        check_vma=False,
    )
```

profile of v0, /device:TPU:0, one launch (start us, length us, event | category | flops | bytes accessed | tf_op | source)
XLA Modules:
  0.0 161.0 jit_solution(13516207489371691894)
XLA Ops:
  7.2 0.0 copy-start
  7.2 0.0 all-gather.2.cloned.1.call-start
  7.2 0.7 all-gather.2.cloned.1.call-update
  7.9 2.0 %copy.43 = bf16[4,32,12,128]{3,2,0,1:T(8,128)(2,1)} copy(bf16[4,32,12,128]{3,1,2,0:T(8,128)(2,1)} %param.5) | data formatting | bytes 786432 | tf_op args[0]
  9.9 7.3 %all-to-all-start = ((bf16[4,32,12,128]{3,2,0,1:T(8,128)(2,1)}), bf16[4,32,12,128]{3,2,0,1:T(8,128)(2,1)S(1)}, u32[]{:S(2)}, u32[]{:S(2)}) async-start(bf16[4,32,12,128]{3,2,0,1:T(8,128)(2,1)} %copy.43), calls=%async_computation | async-start | bytes 1048576 | tf_op jit(solution)/shard_map/all_to_all | solution.py:60
  17.2 2.0 %copy.45 = bf16[4,32,12,128]{3,2,0,1:T(8,128)(2,1)} copy(bf16[4,32,12,128]{3,1,2,0:T(8,128)(2,1)} %param.6) | data formatting | bytes 786432 | tf_op args[1]
  19.2 12.5 %all-to-all-done = bf16[4,32,12,128]{3,2,0,1:T(8,128)(2,1)S(1)} async-done(((bf16[4,32,12,128]{3,2,0,1:T(8,128)(2,1)}), bf16[4,32,12,128]{3,2,0,1:T(8,128)(2,1)S(1)}, u32[]{:S(2)}, u32[]{:S(2)}) %all-to-all-start) | async-done | bytes 393248 | tf_op jit(solution)/shard_map/all_to_all | solution.py:60
  31.7 3.6 %all-to-all-start.1 = ((bf16[4,32,12,128]{3,2,0,1:T(8,128)(2,1)}), bf16[4,32,12,128]{3,2,0,1:T(8,128)(2,1)S(1)}, u32[]{:S(2)}, u32[]{:S(2)}) async-start(bf16[4,32,12,128]{3,2,0,1:T(8,128)(2,1)} %copy.45), calls=%async_computation.1 | async-start | bytes 1048576 | tf_op jit(solution)/shard_map/all_to_all | solution.py:61
  35.3 2.0 %copy.49 = bf16[4,32,12,128]{3,2,0,1:T(8,128)(2,1)} copy(bf16[4,32,12,128]{3,1,2,0:T(8,128)(2,1)} %param.7) | data formatting | bytes 786432 | tf_op args[2]
  37.3 12.7 %all-to-all-done.1 = bf16[4,32,12,128]{3,2,0,1:T(8,128)(2,1)S(1)} async-done(((bf16[4,32,12,128]{3,2,0,1:T(8,128)(2,1)}), bf16[4,32,12,128]{3,2,0,1:T(8,128)(2,1)S(1)}, u32[]{:S(2)}, u32[]{:S(2)}) %all-to-all-start.1) | async-done | bytes 393248 | tf_op jit(solution)/shard_map/all_to_all | solution.py:61
  50.0 3.6 %all-to-all-start.3 = ((bf16[4,32,12,128]{3,2,0,1:T(8,128)(2,1)}), bf16[4,32,12,128]{3,2,0,1:T(8,128)(2,1)S(1)}, u32[]{:S(2)}, u32[]{:S(2)}) async-start(bf16[4,32,12,128]{3,2,0,1:T(8,128)(2,1)} %copy.49), calls=%async_computation.3 | async-start | bytes 1048576 | tf_op jit(solution)/shard_map/all_to_all | solution.py:62
  53.6 22.9 %all-gather.2.cloned.1.call-done = bf16[1536,3072]{1,0:T(8,128)(2,1)} async-done(((bf16[384,3072]{1,0:T(8,128)(2,1)}), bf16[1536,3072]{1,0:T(8,128)(2,1)}) %all-gather.2.cloned.1.call-update) | async-done | bytes 9437200 | tf_op jit(solution)/shard_map/all_gather | solution.py:53
  76.5 0.0 copy-done
  76.5 6.9 %convolution_convert_fusion = bf16[128,1536]{1,0:T(8,128)(2,1)S(1)} fusion(bf16[128,3072]{1,0:T(8,128)(2,1)S(1)} %bitcast.52, bf16[1536,3072]{1,0:T(8,128)(2,1)} %all-gather.2.cloned.1.call-done), kind=kOutput, calls=%fused_computation.1 | convolution fusion | flops 1208156160 | bytes 10616832 | tf_op jit(solution)/shard_map/dot_general | solution.py:51
  83.5 0.3 reshape.16
  83.7 1.1 copy.47
  84.8 0.0 all-to-all-done.3
  84.8 5.5 %all-to-all-start.2 = ((bf16[4,32,12,128]{3,0,2,1:T(4,128)(2,1)}), bf16[4,32,12,128]{3,0,2,1:T(4,128)(2,1)S(1)}, u32[]{:S(2)}, u32[]{:S(2)}) async-start(bf16[4,32,12,128]{3,0,2,1:T(4,128)(2,1)} %copy.47), calls=%async_computation.2 | async-start | bytes 786432 | tf_op jit(solution)/shard_map/all_to_all | solution.py:63
  90.3 0.2 copy.44
  90.5 0.2 copy.46
  90.6 0.2 copy.50
  90.8 1.3 fusion.16
  92.1 10.3 %all-to-all-done.2 = bf16[4,32,12,128]{3,0,2,1:T(4,128)(2,1)S(1)} async-done(((bf16[4,32,12,128]{3,0,2,1:T(4,128)(2,1)}), bf16[4,32,12,128]{3,0,2,1:T(4,128)(2,1)S(1)}, u32[]{:S(2)}, u32[]{:S(2)}) %all-to-all-start.2) | async-done | bytes 393248 | tf_op jit(solution)/shard_map/all_to_all | solution.py:63
  102.4 0.1 copy.48
  102.6 1.6 %fusion.7 = f32[4,12,32]{2,1,0:T(8,128)S(1)} fusion(bf16[32,4,12,128]{3,0,2,1:T(8,128)(2,1)S(1)} %bitcast.64, bf16[4,12,32,128]{3,2,1,0:T(8,128)(2,1)S(1)} %bitcast.66, f32[4,12,32,32]{2,3,1,0:T(8,128)} %get-tuple-element.4, f32[4,12,32]{2,1,0:T(8,128)S(1)} %get-tuple-element.3), kind=kOutput, calls=%fused_computation.14 | convolution fusion | flops 13269504 | bytes 995328 | tf_op jit(solution)/shard_map/phfg,gphd->fphd/dot_general | solution.py:17
  104.2 1.5 fusion.4
  105.7 0.2 fusion.9
  105.9 1.1 copy.56
  107.0 3.6 %all-to-all-start.5 = ((bf16[32,4,12,128]{3,1,2,0:T(4,128)(2,1)}), bf16[32,4,12,128]{3,1,2,0:T(4,128)(2,1)S(1)}, u32[]{:S(2)}, u32[]{:S(2)}) async-start(bf16[32,4,12,128]{3,1,2,0:T(4,128)(2,1)} %copy.56), calls=%async_computation.5 | async-start | bytes 786432 | tf_op jit(solution)/shard_map/all_to_all | solution.py:42
  110.6 0.3 fusion.10
  110.9 1.1 copy.54
  112.0 10.5 %all-to-all-done.5 = bf16[32,4,12,128]{3,1,2,0:T(4,128)(2,1)S(1)} async-done(((bf16[32,4,12,128]{3,1,2,0:T(4,128)(2,1)}), bf16[32,4,12,128]{3,1,2,0:T(4,128)(2,1)S(1)}, u32[]{:S(2)}, u32[]{:S(2)}) %all-to-all-start.5) | async-done | bytes 393248 | tf_op jit(solution)/shard_map/all_to_all | solution.py:42
  122.5 3.6 %all-to-all-start.4 = ((bf16[32,4,12,128]{3,1,2,0:T(4,128)(2,1)}), bf16[32,4,12,128]{3,1,2,0:T(4,128)(2,1)S(1)}, u32[]{:S(2)}, u32[]{:S(2)}) async-start(bf16[32,4,12,128]{3,1,2,0:T(4,128)(2,1)} %copy.54), calls=%async_computation.4 | async-start | bytes 786432 | tf_op jit(solution)/shard_map/all_to_all | solution.py:41
  126.1 1.4 fusion.8
  127.5 1.1 copy.58
  128.6 9.3 %all-to-all-done.4 = bf16[32,4,12,128]{3,1,2,0:T(4,128)(2,1)S(1)} async-done(((bf16[32,4,12,128]{3,1,2,0:T(4,128)(2,1)}), bf16[32,4,12,128]{3,1,2,0:T(4,128)(2,1)S(1)}, u32[]{:S(2)}, u32[]{:S(2)}) %all-to-all-start.4) | async-done | bytes 393248 | tf_op jit(solution)/shard_map/all_to_all | solution.py:41
  137.9 3.6 %all-to-all-start.6 = ((bf16[32,4,12,128]{3,1,2,0:T(4,128)(2,1)}), bf16[32,4,12,128]{3,1,2,0:T(4,128)(2,1)S(1)}, u32[]{:S(2)}, u32[]{:S(2)}) async-start(bf16[32,4,12,128]{3,1,2,0:T(4,128)(2,1)} %copy.58), calls=%async_computation.6 | async-start | bytes 786432 | tf_op jit(solution)/shard_map/all_to_all | solution.py:43
  141.5 0.9 copy.57
  142.4 0.9 copy.55
  143.3 9.9 %all-to-all-done.6 = bf16[32,4,12,128]{3,1,2,0:T(4,128)(2,1)S(1)} async-done(((bf16[32,4,12,128]{3,1,2,0:T(4,128)(2,1)}), bf16[32,4,12,128]{3,1,2,0:T(4,128)(2,1)S(1)}, u32[]{:S(2)}, u32[]{:S(2)}) %all-to-all-start.6) | async-done | bytes 393248 | tf_op jit(solution)/shard_map/all_to_all | solution.py:43
  153.2 0.9 copy.59
Async XLA Ops:
  7.2 69.4 %copy-start = (bf16[4,32,3072]{2,1,0:T(8,128)(2,1)S(1)}, bf16[4,32,3072]{2,1,0:T(8,128)(2,1)}, u32[]{:S(2)}) copy-start(bf16[4,32,3072]{2,1,0:T(8,128)(2,1)} %param.8) | copy-start | bytes 2359300
  7.2 69.4 %all-gather.2.cloned.1.call-start = ((), (), s32[]{:S(2)}) async-start(), calls=%async_computation.7 | async-start | bytes 11796480 | tf_op jit(solution)/shard_map/all_gather | solution.py:53
  9.9 21.8 %all-to-all-start = ((bf16[4,32,12,128]{3,2,0,1:T(8,128)(2,1)}), bf16[4,32,12,128]{3,2,0,1:T(8,128)(2,1)S(1)}, u32[]{:S(2)}, u32[]{:S(2)}) async-start(bf16[4,32,12,128]{3,2,0,1:T(8,128)(2,1)} %copy.43), calls=%async_computation | async-start | bytes 1048576 | tf_op jit(solution)/shard_map/all_to_all | solution.py:60
  31.7 18.3 %all-to-all-start.1 = ((bf16[4,32,12,128]{3,2,0,1:T(8,128)(2,1)}), bf16[4,32,12,128]{3,2,0,1:T(8,128)(2,1)S(1)}, u32[]{:S(2)}, u32[]{:S(2)}) async-start(bf16[4,32,12,128]{3,2,0,1:T(8,128)(2,1)} %copy.45), calls=%async_computation.1 | async-start | bytes 1048576 | tf_op jit(solution)/shard_map/all_to_all | solution.py:61
  50.0 34.8 %all-to-all-start.3 = ((bf16[4,32,12,128]{3,2,0,1:T(8,128)(2,1)}), bf16[4,32,12,128]{3,2,0,1:T(8,128)(2,1)S(1)}, u32[]{:S(2)}, u32[]{:S(2)}) async-start(bf16[4,32,12,128]{3,2,0,1:T(8,128)(2,1)} %copy.49), calls=%async_computation.3 | async-start | bytes 1048576 | tf_op jit(solution)/shard_map/all_to_all | solution.py:62
  84.8 17.6 %all-to-all-start.2 = ((bf16[4,32,12,128]{3,0,2,1:T(4,128)(2,1)}), bf16[4,32,12,128]{3,0,2,1:T(4,128)(2,1)S(1)}, u32[]{:S(2)}, u32[]{:S(2)}) async-start(bf16[4,32,12,128]{3,0,2,1:T(4,128)(2,1)} %copy.47), calls=%async_computation.2 | async-start | bytes 786432 | tf_op jit(solution)/shard_map/all_to_all | solution.py:63
  107.0 15.5 %all-to-all-start.5 = ((bf16[32,4,12,128]{3,1,2,0:T(4,128)(2,1)}), bf16[32,4,12,128]{3,1,2,0:T(4,128)(2,1)S(1)}, u32[]{:S(2)}, u32[]{:S(2)}) async-start(bf16[32,4,12,128]{3,1,2,0:T(4,128)(2,1)} %copy.56), calls=%async_computation.5 | async-start | bytes 786432 | tf_op jit(solution)/shard_map/all_to_all | solution.py:42
  122.5 15.4 %all-to-all-start.4 = ((bf16[32,4,12,128]{3,1,2,0:T(4,128)(2,1)}), bf16[32,4,12,128]{3,1,2,0:T(4,128)(2,1)S(1)}, u32[]{:S(2)}, u32[]{:S(2)}) async-start(bf16[32,4,12,128]{3,1,2,0:T(4,128)(2,1)} %copy.54), calls=%async_computation.4 | async-start | bytes 786432 | tf_op jit(solution)/shard_map/all_to_all | solution.py:41
  137.9 15.3 %all-to-all-start.6 = ((bf16[32,4,12,128]{3,1,2,0:T(4,128)(2,1)}), bf16[32,4,12,128]{3,1,2,0:T(4,128)(2,1)S(1)}, u32[]{:S(2)}, u32[]{:S(2)}) async-start(bf16[32,4,12,128]{3,1,2,0:T(4,128)(2,1)} %copy.58), calls=%async_computation.6 | async-start | bytes 786432 | tf_op jit(solution)/shard_map/all_to_all | solution.py:43
Sparse Core Ops, SparseCore 0:
  9.6 66.9 all-gather.1
where the time goes:
time: 162 us; the launch traced here: 161 us
  waiting for transfers between devices  88.8 us (55%)
  starting transfers between devices  31 us (19%)
  between operations  14.1 us (9%)
  local copies, waits for them, and re-layouts  13.8 us (9%)
  matrix products  13.2 us (8%)
    all_gather x1, waiting for transfers between devices, body(): lax.all_gather(out_proj, 'fsdp', axis=0, tiled=True)  22.9 us
    all_to_all x1, waiting for transfers between devices, body(): lax.all_to_all(key_states, 'tm', split_axis=1, concat_axis=0, tiled=True)  12.7 us
    all_to_all x1, waiting for transfers between devices, body(): lax.all_to_all(queries, 'tm', split_axis=1, concat_axis=0, tiled=True)  12.5 us
    all_to_all x1, waiting for transfers between devices, send_back(): lax.all_to_all(grads[1], 'tm', split_axis=0, concat_axis=1, tiled=True)  10.5 us
    all_to_all x1, waiting for transfers between devices, body(): lax.all_to_all(grad_attn, 'tm', split_axis=1, concat_axis=0, tiled=True)  10.3 us
    all_to_all x1, waiting for transfers between devices, send_back(): lax.all_to_all(grads[2], 'tm', split_axis=0, concat_axis=1, tiled=True)  9.9 us
    all_to_all x1, waiting for transfers between devices, send_back(): lax.all_to_all(grads[0], 'tm', split_axis=0, concat_axis=1, tiled=True)  9.33 us
    all_to_all x1, starting transfers between devices, body(): lax.all_to_all(queries, 'tm', split_axis=1, concat_axis=0, tiled=True)  7.28 us
  transfers between devices with their start and end apart: 8, of which 7 were waited for; matrix products, arithmetic and copies ran while one was open for 13% of the time, Pallas kernels for 0%

commit v1 on v0

--- a/solution.py
+++ b/solution.py
@@ -1,7 +1,15 @@
+import functools
+
 import jax
 import jax.numpy as jnp
 from jax import lax
+from jax.experimental import pallas as pl
+from jax.experimental.pallas import tpu as pltpu
 from jax.sharding import PartitionSpec as P
+
+ANY = pl.BlockSpec(memory_space=pl.ANY)
+VMEM_LIMIT = 48 * 1024 * 1024
+GROUPS = 4
 
 
 def attend_back(query_block, key_block, value_block, grad_block):
@@ -36,37 +44,309 @@
     return (query_grad, key_grad, value_grad)
 
 
-def send_back(grads):
-    return (
-        lax.all_to_all(grads[0], "tm", split_axis=0, concat_axis=1, tiled=True),
-        lax.all_to_all(grads[1], "tm", split_axis=0, concat_axis=1, tiled=True),
-        lax.all_to_all(grads[2], "tm", split_axis=0, concat_axis=1, tiled=True),
-    )
-
-
-def body(queries, key_states, value_states, out_grad, out_proj):
+def body_any(queries, key_states, value_states, out_grad, out_proj):
     frames_dev, pos_dev, heads, head_size = queries.shape
-    width = out_grad.shape[-1]
-    flat = out_grad.reshape(frames_dev * pos_dev, width)
-    grad_flat = lax.dot_general(
-        flat,
-        lax.all_gather(out_proj, "fsdp", axis=0, tiled=True),
-        (((1,), (1,)), ((), ())),
-        preferred_element_type=jnp.float32,
-    ).astype(jnp.bfloat16)
-    grad_attn = grad_flat.reshape(frames_dev, pos_dev, heads, head_size)
-    results = send_back(
-        attend_back(
-            lax.all_to_all(queries, "tm", split_axis=1, concat_axis=0, tiled=True),
-            lax.all_to_all(key_states, "tm", split_axis=1, concat_axis=0, tiled=True),
-            lax.all_to_all(value_states, "tm", split_axis=1, concat_axis=0, tiled=True),
-            lax.all_to_all(grad_attn, "tm", split_axis=1, concat_axis=0, tiled=True),
+    flat = out_grad.reshape(frames_dev * pos_dev, out_grad.shape[-1])
+    grad_attn = (
+        lax.dot_general(
+            flat,
+            lax.all_gather(out_proj, "fsdp", axis=0, tiled=True),
+            (((1,), (1,)), ((), ())),
+            preferred_element_type=jnp.float32,
         )
-    )
-    return (results[0], results[1], results[2])
+        .astype(jnp.bfloat16)
+        .reshape(frames_dev, pos_dev, heads, head_size)
+    )
+    there = functools.partial(
+        lax.all_to_all, axis_name="tm", split_axis=1, concat_axis=0, tiled=True
+    )
+    back = functools.partial(
+        lax.all_to_all, axis_name="tm", split_axis=0, concat_axis=1, tiled=True
+    )
+    grads = attend_back(there(queries), there(key_states), there(value_states), there(grad_attn))
+    return tuple(back(g) for g in grads)
+
+
+def group_of(tm):
+    return 2 * lax.rem(tm, 2) + lax.rem(tm // 2, 2)
+
+
+def part_of(tm):
+    return tm // GROUPS
+
+
+def copy_all(copies):
+    for copy in copies:
+        copy.start()
+    for copy in copies:
+        copy.wait()
+
+
+def pack_kernel(n_tm, q_ref, k_ref, v_ref, *refs):
+    outs, sems = refs[:n_tm], refs[n_tm]
+    me = lax.axis_index("tm")
+    _, _, g_heads, p_rows, _ = outs[0].shape
+    copies = []
+    for k in range(n_tm - 1, -1, -1):
+        there = me ^ k
+        heads = pl.ds(group_of(there) * g_heads, g_heads)
+        rows = pl.ds(pl.multiple_of(part_of(there) * p_rows, p_rows), p_rows)
+        for a, ref in enumerate((q_ref, k_ref, v_ref)):
+            copies.append(
+                pltpu.make_async_copy(ref.at[:, heads, rows], outs[k].at[a], sems.at[3 * k + a])
+            )
+    copy_all(copies)
+
+
+def pack(q, k, v, n_tm, p_rows):
+    frames_dev, heads, _, head_size = q.shape
+    shape = (3, frames_dev, heads // GROUPS, p_rows, head_size)
+    return pl.pallas_call(
+        functools.partial(pack_kernel, n_tm),
+        out_shape=[jax.ShapeDtypeStruct(shape, q.dtype)] * n_tm,
+        in_specs=[ANY] * 3,
+        out_specs=[ANY] * n_tm,
+        scratch_shapes=[pltpu.SemaphoreType.DMA((3 * n_tm,))],
+        compiler_params=pltpu.CompilerParams(vmem_limit_bytes=VMEM_LIMIT),
+        name="pack",
+    )(q, k, v)
+
+
+def unpack_kernel(n_tm, *refs):
+    slots, outs, sems = refs[:n_tm], refs[n_tm : n_tm + 3], refs[n_tm + 3]
+    me = lax.axis_index("tm")
+    _, _, g_heads, p_rows, _ = slots[0].shape
+    copies = []
+    for k in range(n_tm):
+        there = me ^ k
+        heads = pl.ds(group_of(there) * g_heads, g_heads)
+        rows = pl.ds(pl.multiple_of(part_of(there) * p_rows, p_rows), p_rows)
+        for a, ref in enumerate(outs):
+            copies.append(
+                pltpu.make_async_copy(slots[k].at[a], ref.at[:, heads, rows], sems.at[3 * k + a])
+            )
+    copy_all(copies)
+
+
+def unpack(slots, pos_dev):
+    n_tm = len(slots)
+    _, frames_dev, g_heads, _, head_size = slots[0].shape
+    shape = (frames_dev, g_heads * GROUPS, pos_dev, head_size)
+    return pl.pallas_call(
+        functools.partial(unpack_kernel, n_tm),
+        out_shape=[jax.ShapeDtypeStruct(shape, slots[0].dtype)] * 3,
+        in_specs=[ANY] * n_tm,
+        out_specs=[ANY] * 3,
+        scratch_shapes=[pltpu.SemaphoreType.DMA((3 * n_tm,))],
+        compiler_params=pltpu.CompilerParams(vmem_limit_bytes=VMEM_LIMIT),
+        name="unpack",
+    )(*slots)
+
+
+def project_kernel(n_tm, own_ref, other_ref, w_own_ref, w_other_ref, *refs):
+    outs, res, sems = refs[:n_tm], refs[n_tm], refs[n_tm + 1]
+    me = lax.axis_index("tm")
+    fs = lax.axis_index("fsdp")
+    half, core = fs // 2, lax.rem(fs, 2)
+    _, _, g_heads, frames_dev, pos_dev, head_size = res.shape
+    p_rows = outs[0].shape[2]
+    width = own_ref.shape[-1]
+    for s, src in enumerate((own_ref, other_ref)):
+        rows = src[...].reshape(frames_dev * pos_dev, width)
+        for w, w_ref in enumerate((w_own_ref, w_other_ref)):
+            out = lax.dot_general(
+                rows,
+                w_ref[...],
+                (((1,), (1,)), ((), ())),
+                preferred_element_type=jnp.float32,
+            ).astype(jnp.bfloat16)
+            for h in range(g_heads):
+                res[s, core ^ w, h] = out[:, h * head_size : (h + 1) * head_size].reshape(
+                    frames_dev, pos_dev, head_size
+                )
+    y, z = lax.rem(me, 2), me // 2
+    copies = []
+    for r in range(n_tm):
+        kz, kx = r // 2, r % 2
+        there_z, there_x = z ^ kz, y ^ kx
+        rows = pl.ds(pl.multiple_of((there_z // 2) * p_rows, p_rows), p_rows)
+        copies.append(
+            pltpu.make_async_copy(
+                res.at[half ^ there_x, lax.rem(there_z, 2), :, :, rows],
+                outs[r],
+                sems.at[r],
+            )
+        )
+    copy_all(copies)
+
+
+def project(own, other, w_own, w_other, n_tm, p_rows, head_size):
+    frames_dev, pos_dev, width = own.shape
+    g_heads = w_own.shape[0] // head_size
+    shape = (g_heads, frames_dev, p_rows, head_size)
+    rows = 2 * frames_dev * pos_dev
+    return pl.pallas_call(
+        functools.partial(project_kernel, n_tm),
+        out_shape=[jax.ShapeDtypeStruct(shape, own.dtype)] * n_tm,
+        in_specs=[pl.BlockSpec(memory_space=pltpu.VMEM)] * 4,
+        out_specs=[ANY] * n_tm,
+        scratch_shapes=[
+            pltpu.VMEM((2, 2, g_heads, frames_dev, pos_dev, head_size), jnp.bfloat16),
+            pltpu.SemaphoreType.DMA((n_tm,)),
+        ],
+        compiler_params=pltpu.CompilerParams(vmem_limit_bytes=VMEM_LIMIT),
+        cost_estimate=pl.CostEstimate(
+            flops=4 * rows * w_own.shape[0] * width,
+            bytes_accessed=2 * width * (rows + 2 * w_own.shape[0]),
+            transcendentals=0,
+        ),
+        name="project",
+    )(own, other, w_own, w_other)
+
+
+def attend_kernel(n_tm, *refs):
+    qkv, gin = refs[:n_tm], refs[n_tm : 2 * n_tm]
+    outs = refs[2 * n_tm : 3 * n_tm]
+    qkv_s, g_s, wide, back, qkv_sem, g_sem = refs[3 * n_tm :]
+    me = lax.axis_index("tm")
+    half = lax.axis_index("fsdp") // 2
+    _, _, frames_dev, g_heads, p_rows, head_size = qkv_s.shape
+    frames = n_tm * frames_dev
+    scale = head_size ** (-0.5)
+    twist = half ^ lax.rem(me, 2)
+    copies = []
+    for k in range(n_tm):
+        copies.append(pltpu.make_async_copy(qkv[k], qkv_s.at[k], qkv_sem.at[k]))
+    for r in range(n_tm):
+        slot = 2 * (r // 2) + (twist ^ (r % 2))
+        copies.append(pltpu.make_async_copy(gin[r], g_s.at[slot], g_sem.at[r]))
+    copy_all(copies)
+
+    per = max(1, 128 // frames)
+    block = per * frames
+    row = lax.broadcasted_iota(jnp.int32, (block, block), 0) // frames
+    col = lax.broadcasted_iota(jnp.int32, (block, block), 1) // frames
+    same = row == col
+    nt = (((1,), (1,)), ((), ()))
+    nn = (((1,), (0,)), ((), ()))
+    tn = (((0,), (0,)), ((), ()))
+    dot = functools.partial(lax.dot_general, preferred_element_type=jnp.float32)
+
+    for h in range(g_heads):
+        for a in range(3):
+            wide[a] = (
+                qkv_s[:, a, :, h].reshape(frames * p_rows, head_size).astype(jnp.float32)
+            )
+        wide[3] = g_s[:, h].reshape(frames * p_rows, head_size).astype(jnp.float32)
+        for b in range(p_rows // per):
+
+            def rows_of(a):
+                return jnp.concatenate(
+                    [wide[a, pl.ds(b * per + j, frames, stride=p_rows), :] for j in range(per)],
+                    axis=0,
+                ).astype(jnp.bfloat16)
+
+            q, k, v, g = rows_of(0), rows_of(1), rows_of(2), rows_of(3)
+            scores = jnp.where(same, dot(q, k, nt) * scale, -jnp.inf)
+            expo = jnp.exp(scores - jnp.max(scores, axis=-1, keepdims=True))
+            probs = expo / jnp.sum(expo, axis=-1, keepdims=True)
+            probs_b = probs.astype(jnp.bfloat16)
+            dprobs = dot(g, v, nt)
+            row_delta = jnp.sum(probs_b.astype(jnp.float32) * dprobs, axis=-1, keepdims=True)
+            dscores = (probs * (dprobs - row_delta)).astype(jnp.bfloat16)
+            grads = (
+                dot(dscores, k, nn) * scale,
+                dot(dscores, q, tn) * scale,
+                dot(probs_b, g, tn),
+            )
+            for a, grad in enumerate(grads):
+                for j in range(per):
+                    back[a, pl.ds(b * per + j, frames, stride=p_rows), :] = grad[
+                        j * frames : (j + 1) * frames
+                    ]
+        for a in range(3):
+            done = back[a].astype(jnp.bfloat16).reshape(n_tm, frames_dev, p_rows, head_size)
+            for k in range(n_tm):
+                outs[k][a, :, h] = done[k]
+
+
+def attend(qkv, gin):
+    n_tm = len(qkv)
+    shape = qkv[0].shape
+    _, frames_dev, g_heads, p_rows, head_size = shape
+    frames = n_tm * frames_dev
+    return pl.pallas_call(
+        functools.partial(attend_kernel, n_tm),
+        out_shape=[jax.ShapeDtypeStruct(shape, qkv[0].dtype)] * n_tm,
+        in_specs=[ANY] * (2 * n_tm),
+        out_specs=[pl.BlockSpec(memory_space=pltpu.VMEM)] * n_tm,
+        scratch_shapes=[
+            pltpu.VMEM((n_tm,) + shape, jnp.bfloat16),
+            pltpu.VMEM((n_tm, g_heads, frames_dev, p_rows, head_size), jnp.bfloat16),
+            pltpu.VMEM((4, frames * p_rows, head_size), jnp.float32),
+            pltpu.VMEM((3, frames * p_rows, head_size), jnp.float32),
+            pltpu.SemaphoreType.DMA((n_tm,)),
+            pltpu.SemaphoreType.DMA((n_tm,)),
+        ],
+        compiler_params=pltpu.CompilerParams(vmem_limit_bytes=VMEM_LIMIT),
+        name="attend",
+    )(*qkv, *gin)
+
+
+def body_permutes(n_tm, n_fsdp, queries, key_states, value_states, out_grad, out_proj):
+    frames_dev, pos_dev, heads, head_size = queries.shape
+    p_rows = pos_dev * GROUPS // n_tm
+
+    def swap(x, bit):
+        return lax.ppermute(x, "fsdp", [(i, i ^ bit) for i in range(n_fsdp)])
+
+    def over_tm(messages):
+        return [messages[0]] + [
+            lax.ppermute(messages[k], "tm", [(i, i ^ k) for i in range(n_tm)])
+            for k in range(1, n_tm)
+        ]
+
+    def round_of(message, r):
+        kz, kx = r // 2, r % 2
+        pairs = []
+        for tm in range(n_tm):
+            for fs in range(n_fsdp):
+                z, y, x, core = tm // 2, tm % 2, fs // 2, fs % 2
+                there = (2 * (z ^ kz) + x) * n_fsdp + 2 * (y ^ kx) + core
+                pairs.append((tm * n_fsdp + fs, there))
+        return lax.ppermute(message, ("tm", "fsdp"), pairs)
+
+    other = swap(out_grad, 2)
+    w_other = swap(out_proj, 1)
+    heads_out = lambda x: jnp.transpose(x, (0, 2, 1, 3))
+    qkv = over_tm(
+        pack(heads_out(queries), heads_out(key_states), heads_out(value_states), n_tm, p_rows)
+    )
+    messages = project(out_grad, other, out_proj, w_other, n_tm, p_rows, head_size)
+    gin = [round_of(m, r) for r, m in enumerate(messages)]
+    grads = over_tm(attend(qkv, gin))
+    return tuple(heads_out(g) for g in unpack(grads, pos_dev))
 
 
 def solution(mesh):
+    n_tm, n_fsdp = mesh.shape["tm"], mesh.shape["fsdp"]
+
+    def body(queries, key_states, value_states, out_grad, out_proj):
+        _, pos_dev, heads, head_size = queries.shape
+        fits = (
+            n_tm == 2 * GROUPS
+            and n_fsdp == GROUPS
+            and heads % GROUPS == 0
+            and out_proj.shape[0] * GROUPS == heads * head_size
+            and pos_dev % 32 == 0
+            and head_size == 128
+        )
+        if fits:
+            return body_permutes(
+                n_tm, n_fsdp, queries, key_states, value_states, out_grad, out_proj
+            )
+        return body_any(queries, key_states, value_states, out_grad, out_proj)
+
     return jax.shard_map(
         body,
         mesh=mesh,

time: 162 us -> 94.1 us (0.58)
  waiting for transfers between devices: 88.8 us -> 24 us
  starting transfers between devices: 31 us -> 46.6 us
  Pallas kernels: 0 us -> 14.8 us
  between operations: 14.1 us -> 0.72 us
  matrix products: 13.2 us -> 0 us
  local copies, waits for them, and re-layouts: 13.8 us -> 6.01 us
    all_to_all x7 -> x0, waiting for transfers between devices: 65.2 us -> none  [the longest x1 12.7 us: body(): lax.all_to_all(key_states, 'tm', split_axis=1, concat_axis=0, tiled=True)]
    ppermute x0 -> x24, starting transfers between devices: none -> 46.6 us  [the longest x14 26.5 us: over_tm(): lax.ppermute(messages[k], 'tm', [(i, i ^ k) for i in range(n_tm)])]
    all_to_all x7 -> x0, starting transfers between devices: 31 us -> none  [the longest x1 7.28 us: body(): lax.all_to_all(queries, 'tm', split_axis=1, concat_axis=0, tiled=True)]
    ppermute x0 -> x24, waiting for transfers between devices: none -> 24 us  [the longest x14 18.7 us: over_tm(): lax.ppermute(messages[k], 'tm', [(i, i ^ k) for i in range(n_tm)])]
    all_gather x1 -> x0, waiting for transfers between devices: 22.9 us -> none  [body(): lax.all_gather(out_proj, 'fsdp', axis=0, tiled=True)]
    pallas_call x0 -> x4, Pallas kernels: none -> 14.8 us  [the longest x1 8.52 us: attend(): pl.pallas_call(functools.partial(attend_kernel, n_tm), out_shape=[jax.Sha...]
    dot_general x6 -> x0, matrix products: 11.9 us -> none  [the longest x1 6.9 us: body(): lax.dot_general(flat, lax.all_gather(out_proj, 'fsdp', axis=0, tiled=True...]
    all_to_all x7 -> x0, local copies, waits for them, and re-layouts: 3.3 us -> none  [the longest x1 0.9 us: send_back(): lax.all_to_all(grads[2], 'tm', split_axis=0, concat_axis=1, tiled=True)]
  transfers between devices with their start and end apart: 8 -> 24, of which waited for: 7 -> 7; matrix products, arithmetic and copies ran while one was open for 13% -> 0% of each run, Pallas kernels for 0% -> 6%
where the time goes in v1:
time: 94.1 us; the launch traced here: 92.2 us
  starting transfers between devices  46.6 us (50%)
  waiting for transfers between devices  24 us (26%)
  Pallas kernels  14.8 us (16%)
  local copies, waits for them, and re-layouts  6.01 us (6%)
    ppermute x14, starting transfers between devices, over_tm(): lax.ppermute(messages[k], 'tm', [(i, i ^ k) for i in range(n_tm)])  26.5 us
    ppermute x14, waiting for transfers between devices, over_tm(): lax.ppermute(messages[k], 'tm', [(i, i ^ k) for i in range(n_tm)])  18.7 us
    ppermute x8, starting transfers between devices, round_of(): return lax.ppermute(message, ('tm', 'fsdp'), pairs)  17 us
    pallas_call x1, Pallas kernels, attend(): pl.pallas_call(functools.partial(attend_kernel, n_tm), out_shape=[jax.Sha...  8.52 us
    unnamed x12, local copies, waits for them, and re-layouts  6.01 us
    pallas_call x1, Pallas kernels, project(): pl.pallas_call(functools.partial(project_kernel, n_tm), out_shape=[jax.Sh...  4.67 us
    ppermute x2, waiting for transfers between devices, swap(): return lax.ppermute(x, 'fsdp', [(i, i ^ bit) for i in range(n_fsdp)])  4.26 us
    ppermute x2, starting transfers between devices, swap(): return lax.ppermute(x, 'fsdp', [(i, i ^ bit) for i in range(n_fsdp)])  3.08 us
  transfers between devices with their start and end apart: 24, of which 7 were waited for; matrix products, arithmetic and copies ran while one was open for 0% of the time, Pallas kernels for 6%

profile of v1, /device:TPU:0, one launch (start us, length us, event | category | flops | bytes accessed | tf_op | source)
XLA Modules:
  0.0 92.2 jit_solution(5856494003879325956)
XLA Ops:
  0.6 0.5 collective-permute-start.8
  1.1 2.6 %collective-permute-start.7 = (bf16[4,32,3072]{2,1,0:T(8,128)(2,1)}, bf16[4,32,3072]{2,1,0:T(8,128)(2,1)S(1)}, u32[]{:S(2)}, u32[]{:S(2)}) collective-permute-start(bf16[4,32,3072]{2,1,0:T(8,128)(2,1)} %own_ref.1), channel_id=1, source_target_pairs={{0,2},{1,3},{2,0},{3,1},{4,6},{5,7},{6,4},{7,5},{8,10},{9,11},{10,... | collective-permute-start | bytes 2359304 | tf_op jit(solution)/shard_map/ppermute | solution.py:301
  3.7 1.0 %copy-done.2 = bf16[4,32,12,128]{3,1,2,0:T(8,128)(2,1)S(1)} copy-done((bf16[4,32,12,128]{3,1,2,0:T(8,128)(2,1)S(1)}, bf16[4,32,12,128]{3,1,2,0:T(8,128)(2,1)}, u32[]{:S(2)}) %copy-start.2) | copy-done | bytes 393240
  4.7 1.0 %copy-done.3 = bf16[4,32,12,128]{3,1,2,0:T(8,128)(2,1)S(1)} copy-done((bf16[4,32,12,128]{3,1,2,0:T(8,128)(2,1)S(1)}, bf16[4,32,12,128]{3,1,2,0:T(8,128)(2,1)}, u32[]{:S(2)}) %copy-start.3) | copy-done | bytes 393240
  5.7 1.0 %copy-done.4 = bf16[4,32,12,128]{3,1,2,0:T(8,128)(2,1)S(1)} copy-done((bf16[4,32,12,128]{3,1,2,0:T(8,128)(2,1)S(1)}, bf16[4,32,12,128]{3,1,2,0:T(8,128)(2,1)}, u32[]{:S(2)}) %copy-start.4) | copy-done | bytes 393240
  6.7 0.5 pack.1
  7.2 1.6 %collective-permute-start = (bf16[3,4,3,16,128]{4,3,2,1,0:T(8,128)(2,1)S(1)}, bf16[3,4,3,16,128]{4,3,2,1,0:T(8,128)(2,1)S(1)}, u32[]{:S(2)}, u32[]{:S(2)}) collective-permute-start(bf16[3,4,3,16,128]{4,3,2,1,0:T(8,128)(2,1)S(1)} %get-tuple-element.31), channel_id=1, source_target_pairs={{0,4},{4,0},{8,12},{12,8},{16,20},{20,16},{24,28},{28,24},{1,5},{5... | collective-permute-start | bytes 442376 | tf_op jit(solution)/shard_map/ppermute | solution.py:305
  8.8 1.6 %collective-permute-start.1 = (bf16[3,4,3,16,128]{4,3,2,1,0:T(8,128)(2,1)S(1)}, bf16[3,4,3,16,128]{4,3,2,1,0:T(8,128)(2,1)S(1)}, u32[]{:S(2)}, u32[]{:S(2)}) collective-permute-start(bf16[3,4,3,16,128]{4,3,2,1,0:T(8,128)(2,1)S(1)} %get-tuple-element.32), channel_id=1, source_target_pairs={{0,8},{4,12},{8,0},{12,4},{16,24},{20,28},{24,16},{28,20},{1,9},{5... | collective-permute-start | bytes 442376 | tf_op jit(solution)/shard_map/ppermute | solution.py:305
  10.3 0.4 collective-permute-start.2
  10.7 2.4 %collective-permute-done.refs_1_ = bf16[3,4,3,16,128]{4,3,2,1,0:T(8,128)(2,1)S(1)} collective-permute-done((bf16[3,4,3,16,128]{4,3,2,1,0:T(8,128)(2,1)S(1)}, bf16[3,4,3,16,128]{4,3,2,1,0:T(8,128)(2,1)S(1)}, u32[]{:S(2)}, u32[]{:S(2)}) %collective-permute-start) | collective-permute-done | bytes 147488 | tf_op jit(solution)/shard_map/ppermute | solution.py:305
  13.1 2.6 %collective-permute-start.3 = (bf16[3,4,3,16,128]{4,3,2,1,0:T(8,128)(2,1)S(1)}, bf16[3,4,3,16,128]{4,3,2,1,0:T(8,128)(2,1)S(1)}, u32[]{:S(2)}, u32[]{:S(2)}) collective-permute-start(bf16[3,4,3,16,128]{4,3,2,1,0:T(8,128)(2,1)S(1)} %get-tuple-element.34), channel_id=1, source_target_pairs={{0,16},{4,20},{8,24},{12,28},{16,0},{20,4},{24,8},{28,12},{1,17},{... | collective-permute-start | bytes 442376 | tf_op jit(solution)/shard_map/ppermute | solution.py:305
  15.7 0.0 collective-permute-done.1.refs_2_
  15.7 2.1 %collective-permute-start.4 = (bf16[3,4,3,16,128]{4,3,2,1,0:T(8,128)(2,1)S(1)}, bf16[3,4,3,16,128]{4,3,2,1,0:T(8,128)(2,1)S(1)}, u32[]{:S(2)}, u32[]{:S(2)}) collective-permute-start(bf16[3,4,3,16,128]{4,3,2,1,0:T(8,128)(2,1)S(1)} %get-tuple-element.35), channel_id=1, source_target_pairs={{0,20},{4,16},{8,28},{12,24},{16,4},{20,0},{24,12},{28,8},{1,21},{... | collective-permute-start | bytes 442376 | tf_op jit(solution)/shard_map/ppermute | solution.py:305
  17.8 4.3 %collective-permute-done.7.other_ref = bf16[4,32,3072]{2,1,0:T(8,128)(2,1)S(1)} collective-permute-done((bf16[4,32,3072]{2,1,0:T(8,128)(2,1)}, bf16[4,32,3072]{2,1,0:T(8,128)(2,1)S(1)}, u32[]{:S(2)}, u32[]{:S(2)}) %collective-permute-start.7) | collective-permute-done | bytes 786464 | tf_op jit(solution)/shard_map/ppermute | solution.py:301
  22.1 3.9 %collective-permute-start.5 = (bf16[3,4,3,16,128]{4,3,2,1,0:T(8,128)(2,1)S(1)}, bf16[3,4,3,16,128]{4,3,2,1,0:T(8,128)(2,1)S(1)}, u32[]{:S(2)}, u32[]{:S(2)}) collective-permute-start(bf16[3,4,3,16,128]{4,3,2,1,0:T(8,128)(2,1)S(1)} %get-tuple-element.36), channel_id=1, source_target_pairs={{0,24},{4,28},{8,16},{12,20},{16,8},{20,12},{24,0},{28,4},{1,25},{... | collective-permute-start | bytes 442376 | tf_op jit(solution)/shard_map/ppermute | solution.py:305
  25.9 0.0 collective-permute-done.8.w_other_ref
  25.9 1.2 %collective-permute-start.6 = (bf16[3,4,3,16,128]{4,3,2,1,0:T(8,128)(2,1)S(1)}, bf16[3,4,3,16,128]{4,3,2,1,0:T(8,128)(2,1)S(1)}, u32[]{:S(2)}, u32[]{:S(2)}) collective-permute-start(bf16[3,4,3,16,128]{4,3,2,1,0:T(8,128)(2,1)S(1)} %get-tuple-element.37), channel_id=1, source_target_pairs={{0,28},{4,24},{8,20},{12,16},{16,12},{20,8},{24,4},{28,0},{1,29},{... | collective-permute-start | bytes 442376 | tf_op jit(solution)/shard_map/ppermute | solution.py:305
  27.1 0.2 copy-done.5
  27.3 1.7 %copy-done = bf16[384,3072]{1,0:T(8,128)(2,1)S(1)} copy-done((bf16[384,3072]{1,0:T(8,128)(2,1)S(1)}, bf16[384,3072]{1,0:T(8,128)(2,1)}, u32[]{:S(2)}) %copy-start) | copy-done | bytes 2359320
  29.0 1.1 %copy-done.1 = bf16[4,32,3072]{2,1,0:T(8,128)(2,1)S(1)} copy-done((bf16[4,32,3072]{2,1,0:T(8,128)(2,1)S(1)}, bf16[4,32,3072]{2,1,0:T(8,128)(2,1)}, u32[]{:S(2)}) %copy-start.1) | copy-done | bytes 786456
  30.1 4.7 %project.1 = (bf16[3,4,16,128]{3,2,1,0:T(8,128)(2,1)S(1)}, bf16[3,4,16,128]{3,2,1,0:T(8,128)(2,1)S(1)}, bf16[3,4,16,128]{3,2,1,0:T(8,128)(2,1)S(1)}, bf16[3,4,16...) custom-call(bf16[4,32,3072]{2,1,0:T(8,128)(2,1)S(1)} %copy-done.1, ...), custom_call_target="tpu_custom_call" | custom-call | flops 1207959552 | bytes 6291456 | tf_op jit(solution)/shard_map/project/pallas_call | solution.py:188
  34.8 0.0 collective-permute-done.2.refs_3_
  34.8 1.5 %collective-permute-start.10 = (bf16[3,4,16,128]{3,2,1,0:T(8,128)(2,1)S(1)}, bf16[3,4,16,128]{3,2,1,0:T(8,128)(2,1)S(1)}, u32[]{:S(2)}, u32[]{:S(2)}) collective-permute-start(bf16[3,4,16,128]{3,2,1,0:T(8,128)(2,1)S(1)} %get-tuple-element.39), channel_id=1, source_target_pairs={{0,2},{1,3},{2,6},{3,7},{4,0},{5,1},{6,4},{7,5},{8,10},{9,11},{10,... | collective-permute-start | bytes 147464 | tf_op jit(solution)/shard_map/ppermute | solution.py:317
  36.4 0.8 collective-permute-done.4.refs_5_
  37.2 2.1 %collective-permute-start.12 = (bf16[3,4,16,128]{3,2,1,0:T(8,128)(2,1)S(1)}, bf16[3,4,16,128]{3,2,1,0:T(8,128)(2,1)S(1)}, u32[]{:S(2)}, u32[]{:S(2)}) collective-permute-start(bf16[3,4,16,128]{3,2,1,0:T(8,128)(2,1)S(1)} %get-tuple-element.41), channel_id=1, source_target_pairs={{0,10},{1,11},{2,14},{3,15},{4,8},{5,9},{6,12},{7,13},{8,2},{9,3},... | collective-permute-start | bytes 147464 | tf_op jit(solution)/shard_map/ppermute | solution.py:317
  39.3 0.0 collective-permute-done.5.refs_6_
  39.3 2.5 %collective-permute-start.13 = (bf16[3,4,16,128]{3,2,1,0:T(8,128)(2,1)S(1)}, bf16[3,4,16,128]{3,2,1,0:T(8,128)(2,1)S(1)}, u32[]{:S(2)}, u32[]{:S(2)}) collective-permute-start(bf16[3,4,16,128]{3,2,1,0:T(8,128)(2,1)S(1)} %get-tuple-element.42), channel_id=1, source_target_pairs={{0,16},{1,17},{2,20},{3,21},{4,18},{5,19},{6,22},{7,23},{8,24},{9,... | collective-permute-start | bytes 147464 | tf_op jit(solution)/shard_map/ppermute | solution.py:317
  41.8 0.0 collective-permute-done.6.refs_7_
  41.8 4.6 %collective-permute-start.14 = (bf16[3,4,16,128]{3,2,1,0:T(8,128)(2,1)S(1)}, bf16[3,4,16,128]{3,2,1,0:T(8,128)(2,1)S(1)}, u32[]{:S(2)}, u32[]{:S(2)}) collective-permute-start(bf16[3,4,16,128]{3,2,1,0:T(8,128)(2,1)S(1)} %get-tuple-element.43), channel_id=1, source_target_pairs={{0,18},{1,19},{2,22},{3,23},{4,16},{5,17},{6,20},{7,21},{8,26},{9,... | collective-permute-start | bytes 147464 | tf_op jit(solution)/shard_map/ppermute | solution.py:317
  46.4 0.0 collective-permute-done.10.refs_9_
  46.4 0.1 collective-permute-start.15
  46.5 0.0 collective-permute-done.11.refs_10_
  46.5 5.5 %collective-permute-start.16 = (bf16[3,4,16,128]{3,2,1,0:T(8,128)(2,1)S(1)}, bf16[3,4,16,128]{3,2,1,0:T(8,128)(2,1)S(1)}, u32[]{:S(2)}, u32[]{:S(2)}) collective-permute-start(bf16[3,4,16,128]{3,2,1,0:T(8,128)(2,1)S(1)} %get-tuple-element.45), channel_id=1, source_target_pairs={{0,26},{1,27},{2,30},{3,31},{4,24},{5,25},{6,28},{7,29},{8,18},{9,... | collective-permute-start | bytes 147464 | tf_op jit(solution)/shard_map/ppermute | solution.py:317
  52.0 0.7 collective-permute-start.9
  52.7 0.0 collective-permute-done.13.refs_12_
  52.7 0.0 collective-permute-done.14.refs_13_
  52.7 1.1 %collective-permute-done.16.refs_15_ = bf16[3,4,16,128]{3,2,1,0:T(8,128)(2,1)S(1)} collective-permute-done((bf16[3,4,16,128]{3,2,1,0:T(8,128)(2,1)S(1)}, bf16[3,4,16,128]{3,2,1,0:T(8,128)(2,1)S(1)}, u32[]{:S(2)}, u32[]{:S(2)}) %collective-permute-start.16) | collective-permute-done | bytes 49184 | tf_op jit(solution)/shard_map/ppermute | solution.py:317
  53.8 0.0 collective-permute-done.9.refs_8_
  53.8 8.5 %attend.1 = (bf16[3,4,3,16,128]{4,3,2,1,0:T(8,128)(2,1)S(1)}, bf16[3,4,3,16,128]{4,3,2,1,0:T(8,128)(2,1)S(1)}, bf16[3,4,3,16,128]{4,3,2,1,0:T(8,128)(2,1)S(1)}, ...) custom-call(bf16[3,4,3,16,128]{4,3,2,1,0:T(8,128)(2,1)S(1)} %get-tup, ...), custom_call_target="tpu_custom_call" | custom-call | tf_op jit(solution)/shard_map/attend/pallas_call | solution.py:278
  62.3 4.8 %collective-permute-start.17 = (bf16[3,4,3,16,128]{4,3,2,1,0:T(8,128)(2,1)S(1)}, bf16[3,4,3,16,128]{4,3,2,1,0:T(8,128)(2,1)S(1)}, u32[]{:S(2)}, u32[]{:S(2)}) collective-permute-start(bf16[3,4,3,16,128]{4,3,2,1,0:T(8,128)(2,1)S(1)} %get-tuple-element.47), channel_id=1, source_target_pairs={{0,4},{4,0},{8,12},{12,8},{16,20},{20,16},{24,28},{28,24},{1,5},{5... | collective-permute-start | bytes 442376 | tf_op jit(solution)/shard_map/ppermute | solution.py:305
  67.1 1.5 %collective-permute-start.19 = (bf16[3,4,3,16,128]{4,3,2,1,0:T(8,128)(2,1)S(1)}, bf16[3,4,3,16,128]{4,3,2,1,0:T(8,128)(2,1)S(1)}, u32[]{:S(2)}, u32[]{:S(2)}) collective-permute-start(bf16[3,4,3,16,128]{4,3,2,1,0:T(8,128)(2,1)S(1)} %get-tuple-element.49), channel_id=1, source_target_pairs={{0,12},{4,8},{8,4},{12,0},{16,28},{20,24},{24,20},{28,16},{1,13},{... | collective-permute-start | bytes 442376 | tf_op jit(solution)/shard_map/ppermute | solution.py:305
  68.7 4.3 %collective-permute-start.21 = (bf16[3,4,3,16,128]{4,3,2,1,0:T(8,128)(2,1)S(1)}, bf16[3,4,3,16,128]{4,3,2,1,0:T(8,128)(2,1)S(1)}, u32[]{:S(2)}, u32[]{:S(2)}) collective-permute-start(bf16[3,4,3,16,128]{4,3,2,1,0:T(8,128)(2,1)S(1)} %get-tuple-element.51), channel_id=1, source_target_pairs={{0,20},{4,16},{8,28},{12,24},{16,4},{20,0},{24,12},{28,8},{1,21},{... | collective-permute-start | bytes 442376 | tf_op jit(solution)/shard_map/ppermute | solution.py:305
  73.0 0.1 collective-permute-start.22
  73.1 0.7 collective-permute-done.18.refs_2_
  73.9 2.5 %collective-permute-start.23 = (bf16[3,4,3,16,128]{4,3,2,1,0:T(8,128)(2,1)S(1)}, bf16[3,4,3,16,128]{4,3,2,1,0:T(8,128)(2,1)S(1)}, u32[]{:S(2)}, u32[]{:S(2)}) collective-permute-start(bf16[3,4,3,16,128]{4,3,2,1,0:T(8,128)(2,1)S(1)} %get-tuple-element.53), channel_id=1, source_target_pairs={{0,28},{4,24},{8,20},{12,16},{16,12},{20,8},{24,4},{28,0},{1,29},{... | collective-permute-start | bytes 442376 | tf_op jit(solution)/shard_map/ppermute | solution.py:305
  76.3 10.3 %collective-permute-done.20.refs_4_ = bf16[3,4,3,16,128]{4,3,2,1,0:T(8,128)(2,1)S(1)} collective-permute-done((bf16[3,4,3,16,128]{4,3,2,1,0:T(8,128)(2,1)S(1)}, bf16[3,4,3,16,128]{4,3,2,1,0:T(8,128)(2,1)S(1)}, u32[]{:S(2)}, u32[]{:S(2)}) %collective-permute-start.20) | collective-permute-done | bytes 147488 | tf_op jit(solution)/shard_map/ppermute | solution.py:305
  86.7 4.3 %collective-permute-done.21.refs_5_ = bf16[3,4,3,16,128]{4,3,2,1,0:T(8,128)(2,1)S(1)} collective-permute-done((bf16[3,4,3,16,128]{4,3,2,1,0:T(8,128)(2,1)S(1)}, bf16[3,4,3,16,128]{4,3,2,1,0:T(8,128)(2,1)S(1)}, u32[]{:S(2)}, u32[]{:S(2)}) %collective-permute-start.21) | collective-permute-done | bytes 147488 | tf_op jit(solution)/shard_map/ppermute | solution.py:305
  91.0 1.2 %unpack.1 = (bf16[4,12,32,128]{3,2,1,0:T(8,128)(2,1)}, bf16[4,12,32,128]{3,2,1,0:T(8,128)(2,1)}, bf16[4,12,32,128]{3,2,1,0:T(8,128)(2,1)}) custom-call(bf16[3,4,3,16,128]{4,3,2,1,0:T(8,128)(2,1)S(1)} %get-tuple-element.46.refs_0_, bf16[3,4,3,16,128]{4,3,2,1,0:T(8,128)(2,1)S(1)} %collective-permute-done.17.refs_1_, ...), custom_call_target="tpu_custom_call" | custom-call | tf_op jit(solution)/shard_map/unpack/pallas_call | solution.py:135
  (16 shorter events, 0.0 us)
Async XLA Ops:
  0.6 25.3 %collective-permute-start.8 = (bf16[384,3072]{1,0:T(8,128)(2,1)}, bf16[384,3072]{1,0:T(8,128)(2,1)S(1)}, u32[]{:S(2)}, u32[]{:S(2)}) collective-permute-start(bf16[384,3072]{1,0:T(8,128)(2,1)} %w_own_ref.1), channel_id=1, source_target_pairs={{0,1},{1,0},{2,3},{3,2},{4,5},{5,4},{6,7},{7,6},{8,9},{9,8},{10,11... | collective-permute-start | bytes 7077896 | tf_op jit(solution)/shard_map/ppermute | solution.py:301
  1.1 20.9 %collective-permute-start.7 = (bf16[4,32,3072]{2,1,0:T(8,128)(2,1)}, bf16[4,32,3072]{2,1,0:T(8,128)(2,1)S(1)}, u32[]{:S(2)}, u32[]{:S(2)}) collective-permute-start(bf16[4,32,3072]{2,1,0:T(8,128)(2,1)} %own_ref.1), channel_id=1, source_target_pairs={{0,2},{1,3},{2,0},{3,1},{4,6},{5,7},{6,4},{7,5},{8,10},{9,11},{10,... | collective-permute-start | bytes 2359304 | tf_op jit(solution)/shard_map/ppermute | solution.py:301
  3.7 1.0 %copy-start.2 = (bf16[4,32,12,128]{3,1,2,0:T(8,128)(2,1)S(1)}, bf16[4,32,12,128]{3,1,2,0:T(8,128)(2,1)}, u32[]{:S(2)}) copy-start(bf16[4,32,12,128]{3,1,2,0:T(8,128)(2,1)} %param.5) | copy-start | bytes 1179652
  4.7 1.0 %copy-start.3 = (bf16[4,32,12,128]{3,1,2,0:T(8,128)(2,1)S(1)}, bf16[4,32,12,128]{3,1,2,0:T(8,128)(2,1)}, u32[]{:S(2)}) copy-start(bf16[4,32,12,128]{3,1,2,0:T(8,128)(2,1)} %param.6) | copy-start | bytes 1179652
  5.7 1.0 %copy-start.4 = (bf16[4,32,12,128]{3,1,2,0:T(8,128)(2,1)S(1)}, bf16[4,32,12,128]{3,1,2,0:T(8,128)(2,1)}, u32[]{:S(2)}) copy-start(bf16[4,32,12,128]{3,1,2,0:T(8,128)(2,1)} %param.7) | copy-start | bytes 1179652
  7.2 6.0 %collective-permute-start = (bf16[3,4,3,16,128]{4,3,2,1,0:T(8,128)(2,1)S(1)}, bf16[3,4,3,16,128]{4,3,2,1,0:T(8,128)(2,1)S(1)}, u32[]{:S(2)}, u32[]{:S(2)}) collective-permute-start(bf16[3,4,3,16,128]{4,3,2,1,0:T(8,128)(2,1)S(1)} %get-tuple-element.31), channel_id=1, source_target_pairs={{0,4},{4,0},{8,12},{12,8},{16,20},{20,16},{24,28},{28,24},{1,5},{5... | collective-permute-start | bytes 442376 | tf_op jit(solution)/shard_map/ppermute | solution.py:305
  8.8 7.0 %collective-permute-start.1 = (bf16[3,4,3,16,128]{4,3,2,1,0:T(8,128)(2,1)S(1)}, bf16[3,4,3,16,128]{4,3,2,1,0:T(8,128)(2,1)S(1)}, u32[]{:S(2)}, u32[]{:S(2)}) collective-permute-start(bf16[3,4,3,16,128]{4,3,2,1,0:T(8,128)(2,1)S(1)} %get-tuple-element.32), channel_id=1, source_target_pairs={{0,8},{4,12},{8,0},{12,4},{16,24},{20,28},{24,16},{28,20},{1,9},{5... | collective-permute-start | bytes 442376 | tf_op jit(solution)/shard_map/ppermute | solution.py:305
  10.3 24.5 %collective-permute-start.2 = (bf16[3,4,3,16,128]{4,3,2,1,0:T(8,128)(2,1)S(1)}, bf16[3,4,3,16,128]{4,3,2,1,0:T(8,128)(2,1)S(1)}, u32[]{:S(2)}, u32[]{:S(2)}) collective-permute-start(bf16[3,4,3,16,128]{4,3,2,1,0:T(8,128)(2,1)S(1)} %get-tuple-element.33), channel_id=1, source_target_pairs={{0,12},{4,8},{8,4},{12,0},{16,28},{20,24},{24,20},{28,16},{1,13},{... | collective-permute-start | bytes 442376 | tf_op jit(solution)/shard_map/ppermute | solution.py:305
  13.1 23.2 %collective-permute-start.3 = (bf16[3,4,3,16,128]{4,3,2,1,0:T(8,128)(2,1)S(1)}, bf16[3,4,3,16,128]{4,3,2,1,0:T(8,128)(2,1)S(1)}, u32[]{:S(2)}, u32[]{:S(2)}) collective-permute-start(bf16[3,4,3,16,128]{4,3,2,1,0:T(8,128)(2,1)S(1)} %get-tuple-element.34), channel_id=1, source_target_pairs={{0,16},{4,20},{8,24},{12,28},{16,0},{20,4},{24,8},{28,12},{1,17},{... | collective-permute-start | bytes 442376 | tf_op jit(solution)/shard_map/ppermute | solution.py:305
  15.7 21.4 %collective-permute-start.4 = (bf16[3,4,3,16,128]{4,3,2,1,0:T(8,128)(2,1)S(1)}, bf16[3,4,3,16,128]{4,3,2,1,0:T(8,128)(2,1)S(1)}, u32[]{:S(2)}, u32[]{:S(2)}) collective-permute-start(bf16[3,4,3,16,128]{4,3,2,1,0:T(8,128)(2,1)S(1)} %get-tuple-element.35), channel_id=1, source_target_pairs={{0,20},{4,16},{8,28},{12,24},{16,4},{20,0},{24,12},{28,8},{1,21},{... | collective-permute-start | bytes 442376 | tf_op jit(solution)/shard_map/ppermute | solution.py:305
  22.1 17.2 %collective-permute-start.5 = (bf16[3,4,3,16,128]{4,3,2,1,0:T(8,128)(2,1)S(1)}, bf16[3,4,3,16,128]{4,3,2,1,0:T(8,128)(2,1)S(1)}, u32[]{:S(2)}, u32[]{:S(2)}) collective-permute-start(bf16[3,4,3,16,128]{4,3,2,1,0:T(8,128)(2,1)S(1)} %get-tuple-element.36), channel_id=1, source_target_pairs={{0,24},{4,28},{8,16},{12,20},{16,8},{20,12},{24,0},{28,4},{1,25},{... | collective-permute-start | bytes 442376 | tf_op jit(solution)/shard_map/ppermute | solution.py:305
  25.9 1.4 %copy-start.5 = (bf16[384,3072]{1,0:T(8,128)(2,1)}, bf16[384,3072]{1,0:T(8,128)(2,1)S(1)}, u32[]{:S(2)}) copy-start(bf16[384,3072]{1,0:T(8,128)(2,1)S(1)} %collective-permute-done.8.w_other_ref) | copy-start | bytes 7077892
  25.9 15.9 %collective-permute-start.6 = (bf16[3,4,3,16,128]{4,3,2,1,0:T(8,128)(2,1)S(1)}, bf16[3,4,3,16,128]{4,3,2,1,0:T(8,128)(2,1)S(1)}, u32[]{:S(2)}, u32[]{:S(2)}) collective-permute-start(bf16[3,4,3,16,128]{4,3,2,1,0:T(8,128)(2,1)S(1)} %get-tuple-element.37), channel_id=1, source_target_pairs={{0,28},{4,24},{8,20},{12,16},{16,12},{20,8},{24,4},{28,0},{1,29},{... | collective-permute-start | bytes 442376 | tf_op jit(solution)/shard_map/ppermute | solution.py:305
  27.3 1.7 %copy-start = (bf16[384,3072]{1,0:T(8,128)(2,1)S(1)}, bf16[384,3072]{1,0:T(8,128)(2,1)}, u32[]{:S(2)}) copy-start(bf16[384,3072]{1,0:T(8,128)(2,1)} %w_own_ref.1) | copy-start | bytes 7077892
  29.0 1.1 %copy-start.1 = (bf16[4,32,3072]{2,1,0:T(8,128)(2,1)S(1)}, bf16[4,32,3072]{2,1,0:T(8,128)(2,1)}, u32[]{:S(2)}) copy-start(bf16[4,32,3072]{2,1,0:T(8,128)(2,1)} %own_ref.1) | copy-start | bytes 2359300
  34.8 11.6 %collective-permute-start.10 = (bf16[3,4,16,128]{3,2,1,0:T(8,128)(2,1)S(1)}, bf16[3,4,16,128]{3,2,1,0:T(8,128)(2,1)S(1)}, u32[]{:S(2)}, u32[]{:S(2)}) collective-permute-start(bf16[3,4,16,128]{3,2,1,0:T(8,128)(2,1)S(1)} %get-tuple-element.39), channel_id=1, source_target_pairs={{0,2},{1,3},{2,6},{3,7},{4,0},{5,1},{6,4},{7,5},{8,10},{9,11},{10,... | collective-permute-start | bytes 147464 | tf_op jit(solution)/shard_map/ppermute | solution.py:317
  36.4 10.2 %collective-permute-start.11 = (bf16[3,4,16,128]{3,2,1,0:T(8,128)(2,1)S(1)}, bf16[3,4,16,128]{3,2,1,0:T(8,128)(2,1)S(1)}, u32[]{:S(2)}, u32[]{:S(2)}) collective-permute-start(bf16[3,4,16,128]{3,2,1,0:T(8,128)(2,1)S(1)} %get-tuple-element.40), channel_id=1, source_target_pairs={{0,8},{1,9},{2,12},{3,13},{4,10},{5,11},{6,14},{7,15},{8,0},{9,1},... | collective-permute-start | bytes 147464 | tf_op jit(solution)/shard_map/ppermute | solution.py:317
  37.2 14.8 %collective-permute-start.12 = (bf16[3,4,16,128]{3,2,1,0:T(8,128)(2,1)S(1)}, bf16[3,4,16,128]{3,2,1,0:T(8,128)(2,1)S(1)}, u32[]{:S(2)}, u32[]{:S(2)}) collective-permute-start(bf16[3,4,16,128]{3,2,1,0:T(8,128)(2,1)S(1)} %get-tuple-element.41), channel_id=1, source_target_pairs={{0,10},{1,11},{2,14},{3,15},{4,8},{5,9},{6,12},{7,13},{8,2},{9,3},... | collective-permute-start | bytes 147464 | tf_op jit(solution)/shard_map/ppermute | solution.py:317
  39.3 13.4 %collective-permute-start.13 = (bf16[3,4,16,128]{3,2,1,0:T(8,128)(2,1)S(1)}, bf16[3,4,16,128]{3,2,1,0:T(8,128)(2,1)S(1)}, u32[]{:S(2)}, u32[]{:S(2)}) collective-permute-start(bf16[3,4,16,128]{3,2,1,0:T(8,128)(2,1)S(1)} %get-tuple-element.42), channel_id=1, source_target_pairs={{0,16},{1,17},{2,20},{3,21},{4,18},{5,19},{6,22},{7,23},{8,24},{9,... | collective-permute-start | bytes 147464 | tf_op jit(solution)/shard_map/ppermute | solution.py:317
  41.8 10.9 %collective-permute-start.14 = (bf16[3,4,16,128]{3,2,1,0:T(8,128)(2,1)S(1)}, bf16[3,4,16,128]{3,2,1,0:T(8,128)(2,1)S(1)}, u32[]{:S(2)}, u32[]{:S(2)}) collective-permute-start(bf16[3,4,16,128]{3,2,1,0:T(8,128)(2,1)S(1)} %get-tuple-element.43), channel_id=1, source_target_pairs={{0,18},{1,19},{2,22},{3,23},{4,16},{5,17},{6,20},{7,21},{8,26},{9,... | collective-permute-start | bytes 147464 | tf_op jit(solution)/shard_map/ppermute | solution.py:317
  46.4 6.3 %collective-permute-start.15 = (bf16[3,4,16,128]{3,2,1,0:T(8,128)(2,1)S(1)}, bf16[3,4,16,128]{3,2,1,0:T(8,128)(2,1)S(1)}, u32[]{:S(2)}, u32[]{:S(2)}) collective-permute-start(bf16[3,4,16,128]{3,2,1,0:T(8,128)(2,1)S(1)} %get-tuple-element.44), channel_id=1, source_target_pairs={{0,24},{1,25},{2,28},{3,29},{4,26},{5,27},{6,30},{7,31},{8,16},{9,... | collective-permute-start | bytes 147464 | tf_op jit(solution)/shard_map/ppermute | solution.py:317
  46.5 7.3 %collective-permute-start.16 = (bf16[3,4,16,128]{3,2,1,0:T(8,128)(2,1)S(1)}, bf16[3,4,16,128]{3,2,1,0:T(8,128)(2,1)S(1)}, u32[]{:S(2)}, u32[]{:S(2)}) collective-permute-start(bf16[3,4,16,128]{3,2,1,0:T(8,128)(2,1)S(1)} %get-tuple-element.45), channel_id=1, source_target_pairs={{0,26},{1,27},{2,30},{3,31},{4,24},{5,25},{6,28},{7,29},{8,18},{9,... | collective-permute-start | bytes 147464 | tf_op jit(solution)/shard_map/ppermute | solution.py:317
  52.0 1.8 %collective-permute-start.9 = (bf16[3,4,16,128]{3,2,1,0:T(8,128)(2,1)S(1)}, bf16[3,4,16,128]{3,2,1,0:T(8,128)(2,1)S(1)}, u32[]{:S(2)}, u32[]{:S(2)}) collective-permute-start(bf16[3,4,16,128]{3,2,1,0:T(8,128)(2,1)S(1)} %get-tuple-element.38), channel_id=1, source_target_pairs={{0,0},{1,1},{2,4},{3,5},{4,2},{5,3},{6,6},{7,7},{8,8},{9,9},{10,12... | collective-permute-start | bytes 147464 | tf_op jit(solution)/shard_map/ppermute | solution.py:317
  62.3 10.7 %collective-permute-start.17 = (bf16[3,4,3,16,128]{4,3,2,1,0:T(8,128)(2,1)S(1)}, bf16[3,4,3,16,128]{4,3,2,1,0:T(8,128)(2,1)S(1)}, u32[]{:S(2)}, u32[]{:S(2)}) collective-permute-start(bf16[3,4,3,16,128]{4,3,2,1,0:T(8,128)(2,1)S(1)} %get-tuple-element.47), channel_id=1, source_target_pairs={{0,4},{4,0},{8,12},{12,8},{16,20},{20,16},{24,28},{28,24},{1,5},{5... | collective-permute-start | bytes 442376 | tf_op jit(solution)/shard_map/ppermute | solution.py:305
  67.1 6.7 %collective-permute-start.18 = (bf16[3,4,3,16,128]{4,3,2,1,0:T(8,128)(2,1)S(1)}, bf16[3,4,3,16,128]{4,3,2,1,0:T(8,128)(2,1)S(1)}, u32[]{:S(2)}, u32[]{:S(2)}) collective-permute-start(bf16[3,4,3,16,128]{4,3,2,1,0:T(8,128)(2,1)S(1)} %get-tuple-element.48), channel_id=1, source_target_pairs={{0,8},{4,12},{8,0},{12,4},{16,24},{20,28},{24,16},{28,20},{1,9},{5... | collective-permute-start | bytes 442376 | tf_op jit(solution)/shard_map/ppermute | solution.py:305
  67.1 9.2 %collective-permute-start.19 = (bf16[3,4,3,16,128]{4,3,2,1,0:T(8,128)(2,1)S(1)}, bf16[3,4,3,16,128]{4,3,2,1,0:T(8,128)(2,1)S(1)}, u32[]{:S(2)}, u32[]{:S(2)}) collective-permute-start(bf16[3,4,3,16,128]{4,3,2,1,0:T(8,128)(2,1)S(1)} %get-tuple-element.49), channel_id=1, source_target_pairs={{0,12},{4,8},{8,4},{12,0},{16,28},{20,24},{24,20},{28,16},{1,13},{... | collective-permute-start | bytes 442376 | tf_op jit(solution)/shard_map/ppermute | solution.py:305
  68.7 18.0 %collective-permute-start.20 = (bf16[3,4,3,16,128]{4,3,2,1,0:T(8,128)(2,1)S(1)}, bf16[3,4,3,16,128]{4,3,2,1,0:T(8,128)(2,1)S(1)}, u32[]{:S(2)}, u32[]{:S(2)}) collective-permute-start(bf16[3,4,3,16,128]{4,3,2,1,0:T(8,128)(2,1)S(1)} %get-tuple-element.50), channel_id=1, source_target_pairs={{0,16},{4,20},{8,24},{12,28},{16,0},{20,4},{24,8},{28,12},{1,17},{... | collective-permute-start | bytes 442376 | tf_op jit(solution)/shard_map/ppermute | solution.py:305
  68.7 22.3 %collective-permute-start.21 = (bf16[3,4,3,16,128]{4,3,2,1,0:T(8,128)(2,1)S(1)}, bf16[3,4,3,16,128]{4,3,2,1,0:T(8,128)(2,1)S(1)}, u32[]{:S(2)}, u32[]{:S(2)}) collective-permute-start(bf16[3,4,3,16,128]{4,3,2,1,0:T(8,128)(2,1)S(1)} %get-tuple-element.51), channel_id=1, source_target_pairs={{0,20},{4,16},{8,28},{12,24},{16,4},{20,0},{24,12},{28,8},{1,21},{... | collective-permute-start | bytes 442376 | tf_op jit(solution)/shard_map/ppermute | solution.py:305
  73.0 18.0 %collective-permute-start.22 = (bf16[3,4,3,16,128]{4,3,2,1,0:T(8,128)(2,1)S(1)}, bf16[3,4,3,16,128]{4,3,2,1,0:T(8,128)(2,1)S(1)}, u32[]{:S(2)}, u32[]{:S(2)}) collective-permute-start(bf16[3,4,3,16,128]{4,3,2,1,0:T(8,128)(2,1)S(1)} %get-tuple-element.52), channel_id=1, source_target_pairs={{0,24},{4,28},{8,16},{12,20},{16,8},{20,12},{24,0},{28,4},{1,25},{... | collective-permute-start | bytes 442376 | tf_op jit(solution)/shard_map/ppermute | solution.py:305
  73.9 17.2 %collective-permute-start.23 = (bf16[3,4,3,16,128]{4,3,2,1,0:T(8,128)(2,1)S(1)}, bf16[3,4,3,16,128]{4,3,2,1,0:T(8,128)(2,1)S(1)}, u32[]{:S(2)}, u32[]{:S(2)}) collective-permute-start(bf16[3,4,3,16,128]{4,3,2,1,0:T(8,128)(2,1)S(1)} %get-tuple-element.53), channel_id=1, source_target_pairs={{0,28},{4,24},{8,20},{12,16},{16,12},{20,8},{24,4},{28,0},{1,29},{... | collective-permute-start | bytes 442376 | tf_op jit(solution)/shard_map/ppermute | solution.py:305

commit v2 on v1

v2 whole, which is shorter than its diff:
```python
import functools

import jax
import jax.numpy as jnp
from jax import lax
from jax.experimental import pallas as pl
from jax.experimental.pallas import tpu as pltpu
from jax.sharding import PartitionSpec as P

ANY = pl.BlockSpec(memory_space=pl.ANY)
HBM = pl.BlockSpec(memory_space=pltpu.HBM)
VMEM = pl.BlockSpec(memory_space=pltpu.VMEM)
MIB = 1024 * 1024
SLOTS = (7, 4, 6, 5, 3, 2, 1, 0)
ROUNDS = (0, 1, 2, 3, 4, 5, 6, 7)
GROUPS = 4


NT = (((1,), (1,)), ((), ()))
dot = functools.partial(lax.dot_general, preferred_element_type=jnp.float32)


def blocks_dot(a, b, over_a, over_b):
    return dot(a, b, (((over_a,), (over_b,)), ((0,), (0,))))


def attend_back(query_block, key_block, value_block, grad_block):
    score_scale = query_block.shape[-1] ** (-0.5)
    scores = (
        jnp.einsum("fphd,gphd->phfg", query_block, key_block, preferred_element_type=jnp.float32)
        * score_scale
    )
    peak = jnp.max(scores, axis=-1, keepdims=True)
    expo = jnp.exp(scores - peak)
    probs = expo / jnp.sum(expo, axis=-1, keepdims=True)
    probs_b = probs.astype(jnp.bfloat16)
    attn_out = jnp.einsum(
        "phfg,gphd->fphd", probs_b, value_block, preferred_element_type=jnp.float32
    )
    row_delta = jnp.einsum("fphd,fphd->phf", grad_block.astype(jnp.float32), attn_out)
    dprobs = jnp.einsum(
        "fphd,gphd->phfg", grad_block, value_block, preferred_element_type=jnp.float32
    )
    dscores = (probs * (dprobs - row_delta[..., None])).astype(jnp.bfloat16)
    query_grad = (
        jnp.einsum("phfg,gphd->fphd", dscores, key_block, preferred_element_type=jnp.float32)
        * score_scale
    ).astype(jnp.bfloat16)
    key_grad = (
        jnp.einsum("phfg,fphd->gphd", dscores, query_block, preferred_element_type=jnp.float32)
        * score_scale
    ).astype(jnp.bfloat16)
    value_grad = jnp.einsum(
        "phfg,fphd->gphd", probs_b, grad_block, preferred_element_type=jnp.float32
    ).astype(jnp.bfloat16)
    return (query_grad, key_grad, value_grad)


def body_any(queries, key_states, value_states, out_grad, out_proj):
    frames_dev, pos_dev, heads, head_size = queries.shape
    flat = out_grad.reshape(frames_dev * pos_dev, out_grad.shape[-1])
    grad_attn = (
        lax.dot_general(
            flat,
            lax.all_gather(out_proj, "fsdp", axis=0, tiled=True),
            (((1,), (1,)), ((), ())),
            preferred_element_type=jnp.float32,
        )
        .astype(jnp.bfloat16)
        .reshape(frames_dev, pos_dev, heads, head_size)
    )
    there = functools.partial(
        lax.all_to_all, axis_name="tm", split_axis=1, concat_axis=0, tiled=True
    )
    back = functools.partial(
        lax.all_to_all, axis_name="tm", split_axis=0, concat_axis=1, tiled=True
    )
    grads = attend_back(there(queries), there(key_states), there(value_states), there(grad_attn))
    return tuple(back(g) for g in grads)


def group_of(tm):
    return 2 * (tm % 2) + tm // 2 % 2


def part_of(tm):
    return tm // GROUPS


def copy_all(copies):
    for copy in copies:
        copy.start()
    for copy in copies:
        copy.wait()


def pack_kernel(n_tm, q_ref, k_ref, v_ref, out, sems):
    _, _, _, g_heads, p_rows, _ = out.shape
    copies = []
    for i in range(n_tm):
        heads = slice(group_of(i) * g_heads, (group_of(i) + 1) * g_heads)
        rows = slice(part_of(i) * p_rows, (part_of(i) + 1) * p_rows)
        for a, ref in enumerate((q_ref, k_ref, v_ref)):
            copies.append(
                pltpu.make_async_copy(ref.at[:, heads, rows], out.at[i, a], sems.at[3 * i + a])
            )
    copy_all(copies)


def pack(q, k, v, n_tm, p_rows):
    frames_dev, heads, _, head_size = q.shape
    shape = (n_tm, 3, frames_dev, heads // GROUPS, p_rows, head_size)
    return pl.pallas_call(
        functools.partial(pack_kernel, n_tm),
        out_shape=jax.ShapeDtypeStruct(shape, q.dtype),
        in_specs=[HBM] * 3,
        out_specs=VMEM,
        scratch_shapes=[pltpu.SemaphoreType.DMA((3 * n_tm,))],
        compiler_params=pltpu.CompilerParams(vmem_limit_bytes=4 * MIB),
        name="pack",
    )(*(pltpu.with_memory_space_constraint(x, pltpu.HBM) for x in (q, k, v)))


def unpack_kernel(slots, *refs):
    n_tm = len(slots)
    grads, outs, sems = refs[:n_tm], refs[n_tm : n_tm + 3], refs[n_tm + 3]
    me = lax.axis_index("tm")
    _, _, g_heads, p_rows, _ = grads[0].shape
    copies = []
    for j, k in enumerate(slots):
        there = me ^ k
        heads = pl.ds(group_of(there) * g_heads, g_heads)
        rows = pl.ds(pl.multiple_of(part_of(there) * p_rows, p_rows), p_rows)
        for a, ref in enumerate(outs):
            copies.append(
                pltpu.make_async_copy(grads[j].at[a], ref.at[:, heads, rows], sems.at[3 * j + a])
            )
    copy_all(copies)


def unpack(grads, slots, pos_dev):
    n_tm = len(grads)
    _, frames_dev, g_heads, _, head_size = grads[0].shape
    shape = (frames_dev, g_heads * GROUPS, pos_dev, head_size)
    return pl.pallas_call(
        functools.partial(unpack_kernel, slots),
        out_shape=[jax.ShapeDtypeStruct(shape, grads[0].dtype)] * 3,
        in_specs=[ANY] * n_tm,
        out_specs=[HBM] * 3,
        scratch_shapes=[pltpu.SemaphoreType.DMA((3 * n_tm,))],
        compiler_params=pltpu.CompilerParams(vmem_limit_bytes=1 * MIB),
        name="unpack",
    )(*grads)


def project_kernel(n_tm, own_ref, other_ref, w_own_ref, w_other_ref, *refs):
    outs = refs[:n_tm]
    rows_ref, w_ref, res, row_sems, w_sems, out_sems = refs[n_tm:]
    me, fs = lax.axis_index("tm"), lax.axis_index("fsdp")
    half, core = fs // 2, lax.rem(fs, 2)
    _, _, g_heads, frames_dev, pos_dev, head_size = res.shape
    row_copies = [
        pltpu.make_async_copy(ref, rows_ref.at[i], row_sems.at[i])
        for i, ref in enumerate((own_ref, other_ref))
    ]
    w_copies = [
        pltpu.make_async_copy(ref, w_ref.at[i], w_sems.at[i])
        for i, ref in enumerate((w_own_ref, w_other_ref))
    ]
    for copy in (w_copies[0], *row_copies, w_copies[1]):
        copy.start()
    for copy in row_copies:
        copy.wait()
    rows = rows_ref[...].reshape(2 * frames_dev * pos_dev, rows_ref.shape[-1])
    for w in range(2):
        w_copies[w].wait()
        out = dot(rows, w_ref[w], NT).astype(jnp.bfloat16)
        for h in range(g_heads):
            res[core ^ w, :, h] = out[:, h * head_size : (h + 1) * head_size].reshape(
                2, frames_dev, pos_dev, head_size
            )
    p_rows = outs[0].shape[2]
    y, z = lax.rem(me, 2), me // 2
    copies = []
    for j, r in enumerate(ROUNDS):
        there_z, there_x = z ^ (r // 2), y ^ (r % 2)
        part = pl.ds(pl.multiple_of((there_z // 2) * p_rows, p_rows), p_rows)
        copies.append(
            pltpu.make_async_copy(
                res.at[lax.rem(there_z, 2), half ^ there_x, :, :, part],
                outs[j],
                out_sems.at[j],
            )
        )
    copy_all(copies)


def project(own, other, w_own, w_other, n_tm, p_rows, head_size):
    frames_dev, pos_dev, width = own.shape
    w_rows = w_own.shape[0]
    g_heads = w_rows // head_size
    shape = (g_heads, frames_dev, p_rows, head_size)
    rows = 2 * frames_dev * pos_dev
    return pl.pallas_call(
        functools.partial(project_kernel, n_tm),
        out_shape=[jax.ShapeDtypeStruct(shape, own.dtype)] * n_tm,
        in_specs=[ANY] * 4,
        out_specs=[ANY] * n_tm,
        scratch_shapes=[
            pltpu.VMEM((2, frames_dev, pos_dev, width), jnp.bfloat16),
            pltpu.VMEM((2, w_rows, width), jnp.bfloat16),
            pltpu.VMEM((2, 2, g_heads, frames_dev, pos_dev, head_size), jnp.bfloat16),
            pltpu.SemaphoreType.DMA((2,)),
            pltpu.SemaphoreType.DMA((2,)),
            pltpu.SemaphoreType.DMA((n_tm,)),
        ],
        compiler_params=pltpu.CompilerParams(vmem_limit_bytes=20 * MIB),
        cost_estimate=pl.CostEstimate(
            flops=256 * rows * w_rows * width,
            bytes_accessed=2 * width * (rows + 2 * w_rows),
            transcendentals=0,
        ),
        name="project",
    )(
        pltpu.with_memory_space_constraint(own, pltpu.HBM),
        other,
        pltpu.with_memory_space_constraint(w_own, pltpu.HBM),
        w_other,
    )


def by_position(wide, out, frames, p_rows):
    per = out.shape[1] // frames
    groups = p_rows // per
    for h in range(wide.shape[0]):
        for p in range(p_rows):
            rows = slice(p % per * frames, (p % per + 1) * frames)
            out[h * groups + p // per, rows] = wide[h, pl.ds(p, frames, stride=p_rows), :].astype(
                jnp.bfloat16
            )


def probs_kernel(qkv, *refs):
    by_pos, probs_ref, wide = refs[:3], refs[3], refs[4]
    n_tm, _, frames_dev, g_heads, p_rows, head_size = qkv.shape
    frames = n_tm * frames_dev
    slot_rows = frames_dev * p_rows
    block = probs_ref.shape[-1]
    for a in range(3):
        for h in range(g_heads):
            for k in range(n_tm):
                wide[a, h, k * slot_rows : (k + 1) * slot_rows] = (
                    qkv[k, a, :, h].reshape(slot_rows, head_size).astype(jnp.float32)
                )
        by_position(wide.at[a], by_pos[a], frames, p_rows)
    row = lax.broadcasted_iota(jnp.int32, (1, block, block), 1) // frames
    col = lax.broadcasted_iota(jnp.int32, (1, block, block), 2) // frames
    scores = blocks_dot(by_pos[0][...], by_pos[1][...], 2, 2) * head_size ** (-0.5)
    scores = jnp.where(row == col, scores, -jnp.inf)
    expo = jnp.exp(scores - jnp.max(scores, axis=-1, keepdims=True))
    probs_ref[...] = expo / jnp.sum(expo, axis=-1, keepdims=True)


def grads_kernel(n_tm, slots, *refs):
    gin = refs[:n_tm]
    q_ref, k_ref, v_ref, probs_ref = refs[n_tm : n_tm + 4]
    outs = refs[n_tm + 4 : 2 * n_tm + 4]
    wide, g_ref, back = refs[2 * n_tm + 4 :]
    g_heads, frames_dev, p_rows, head_size = gin[0].shape
    frames = n_tm * frames_dev
    slot_rows = frames_dev * p_rows
    scale = head_size ** (-0.5)
    me, half = lax.axis_index("tm"), lax.axis_index("fsdp") // 2
    for j, r in enumerate(ROUNDS):
        slot = 2 * ((me // 2) ^ (r // 2)) + (half ^ (r % 2))
        rows = pl.ds(pl.multiple_of(slot * slot_rows, slot_rows), slot_rows)
        for h in range(g_heads):
            wide[h, rows] = gin[j][h].reshape(slot_rows, head_size).astype(jnp.float32)
    by_position(wide, g_ref, frames, p_rows)
    g, probs = g_ref[...], probs_ref[...]
    probs_b = probs.astype(jnp.bfloat16)
    dprobs = blocks_dot(g, v_ref[...], 2, 2)
    row_delta = jnp.sum(probs_b.astype(jnp.float32) * dprobs, axis=-1, keepdims=True)
    dscores = (probs * (dprobs - row_delta)).astype(jnp.bfloat16)
    grads = (
        blocks_dot(dscores, k_ref[...], 2, 1) * scale,
        blocks_dot(dscores, q_ref[...], 1, 1) * scale,
        blocks_dot(probs_b, g, 1, 1),
    )
    per = g.shape[1] // frames
    groups = p_rows // per
    for a, grad in enumerate(grads):
        for h in range(g_heads):
            for p in range(p_rows):
                back[a, h, pl.ds(p, frames, stride=p_rows), :] = grad[
                    h * groups + p // per, p % per * frames : (p % per + 1) * frames
                ]
    for a in range(3):
        for h in range(g_heads):
            for k, out in zip(slots, outs):
                rows = pl.ds(pl.multiple_of((me ^ k) * slot_rows, slot_rows), slot_rows)
                out[a, :, h] = (
                    back[a, h, rows]
                    .astype(jnp.bfloat16)
                    .reshape(frames_dev, p_rows, head_size)
                )


def probs_of(qkv):
    n_tm, _, frames_dev, g_heads, p_rows, head_size = qkv.shape
    frames = n_tm * frames_dev
    per = max(1, 128 // frames)
    block = per * frames
    count = g_heads * p_rows // per
    return pl.pallas_call(
        probs_kernel,
        out_shape=[jax.ShapeDtypeStruct((count, block, head_size), jnp.bfloat16)] * 3
        + [jax.ShapeDtypeStruct((count, block, block), jnp.float32)],
        in_specs=[VMEM],
        out_specs=[VMEM] * 4,
        scratch_shapes=[pltpu.VMEM((3, g_heads, frames * p_rows, head_size), jnp.float32)],
        compiler_params=pltpu.CompilerParams(vmem_limit_bytes=16 * MIB),
        name="probs",
    )(qkv)


def grads_of(gin, by_pos, slots, shape):
    n_tm = len(gin)
    _, frames_dev, g_heads, p_rows, head_size = shape
    frames = n_tm * frames_dev
    return pl.pallas_call(
        functools.partial(grads_kernel, n_tm, slots),
        out_shape=[jax.ShapeDtypeStruct(shape, jnp.bfloat16)] * n_tm,
        in_specs=[VMEM] * (n_tm + 4),
        out_specs=[VMEM] * n_tm,
        scratch_shapes=[
            pltpu.VMEM((g_heads, frames * p_rows, head_size), jnp.float32),
            pltpu.VMEM(by_pos[0].shape, jnp.bfloat16),
            pltpu.VMEM((3, g_heads, frames * p_rows, head_size), jnp.float32),
        ],
        compiler_params=pltpu.CompilerParams(vmem_limit_bytes=16 * MIB),
        name="grads",
    )(*gin, *by_pos)


def after(later, earlier):
    return lax.optimization_barrier((later, earlier))


def body_permutes(n_tm, n_fsdp, queries, key_states, value_states, out_grad, out_proj):
    _, pos_dev, _, head_size = queries.shape
    p_rows = pos_dev * GROUPS // n_tm
    slots = SLOTS

    def swap(x, bit):
        return lax.ppermute(x, "fsdp", [(i, i ^ bit) for i in range(n_fsdp)])

    def send(message, k):
        return lax.ppermute(message, "tm", [(i, i ^ k) for i in range(n_tm)]) if k else message

    def round_of(message, r):
        kz, kx = r // 2, r % 2
        pairs = []
        for tm in range(n_tm):
            for fs in range(n_fsdp):
                z, y, x, core = tm // 2, tm % 2, fs // 2, fs % 2
                there = (2 * (z ^ kz) + x) * n_fsdp + 2 * (y ^ kx) + core
                pairs.append((tm * n_fsdp + fs, there))
        return lax.ppermute(message, ("tm", "fsdp"), pairs)

    other = swap(out_grad, 2)
    w_other = swap(out_proj, 1)
    heads_out = lambda x: jnp.transpose(x, (0, 2, 1, 3))
    qkv = lax.all_to_all(
        pack(heads_out(queries), heads_out(key_states), heads_out(value_states), n_tm, p_rows),
        "tm",
        split_axis=0,
        concat_axis=0,
        tiled=True,
    )
    messages = project(out_grad, other, out_proj, w_other, n_tm, p_rows, head_size)
    gin = [round_of(m, r) for r, m in zip(ROUNDS, messages)]
    grads = grads_of(gin, probs_of(qkv), slots, qkv.shape[1:])
    grads = [send(g, k) for g, k in zip(grads, slots)]
    return tuple(heads_out(g) for g in unpack(grads, slots, pos_dev))


def solution(mesh):
    n_tm, n_fsdp = mesh.shape["tm"], mesh.shape["fsdp"]

    def body(queries, key_states, value_states, out_grad, out_proj):
        _, pos_dev, heads, head_size = queries.shape
        fits = (
            n_tm == 2 * GROUPS
            and n_fsdp == GROUPS
            and heads % GROUPS == 0
            and out_proj.shape[0] * GROUPS == heads * head_size
            and pos_dev % 32 == 0
            and head_size == 128
        )
        if fits:
            return body_permutes(
                n_tm, n_fsdp, queries, key_states, value_states, out_grad, out_proj
            )
        return body_any(queries, key_states, value_states, out_grad, out_proj)

    return jax.shard_map(
        body,
        mesh=mesh,
        in_specs=(
            P("tm", "fsdp", None, None),
            P("tm", "fsdp", None, None),
            P("tm", "fsdp", None, None),
            P("tm", "fsdp", None),
            P("fsdp", None),
        ),
        out_specs=(
            P("tm", "fsdp", None, None),
            P("tm", "fsdp", None, None),
            P("tm", "fsdp", None, None),
        ),
        check_vma=False,
    )
```

time: 94.1 us -> 83.2 us (0.88); the launches traced: 92.2 us -> 82.9 us
  local copies, waits for them, and re-layouts: 6.01 us -> 0 us
  Pallas kernels: 14.8 us -> 12 us
    ppermute x14 -> x7, waiting for transfers between devices: 18.7 us -> 9.27 us  [send(): lax.ppermute(message, 'tm', [(i, i ^ k) for i in range(n_tm)])]
    unnamed x12 -> x0, local copies, waits for them, and re-layouts: 6.01 us -> none
    ppermute x14 -> x7, starting transfers between devices: 26.5 us -> 20.7 us  [send(): lax.ppermute(message, 'tm', [(i, i ^ k) for i in range(n_tm)])]
    all_to_all x0 -> x1, starting transfers between devices: none -> 5.85 us  [body_permutes(): lax.all_to_all(pack(heads_out(queries), heads_out(key_states), heads_out(...]
    ppermute x2, waiting for transfers between devices: 4.26 us -> 10.1 us  [swap(): return lax.ppermute(x, 'fsdp', [(i, i ^ bit) for i in range(n_fsdp)])]
    pallas_call x3 -> x4, Pallas kernels: 10.2 us -> 7 us  [the longest x1 2.52 us: pack(): pl.pallas_call(functools.partial(pack_kernel, n_tm), out_shape=jax.ShapeD...]
    ppermute x8, waiting for transfers between devices: 1.07 us -> 4.2 us  [round_of(): return lax.ppermute(message, ('tm', 'fsdp'), pairs)]
  transfers between devices with their start and end apart: 24 -> 18, of which waited for: 7 -> 9; matrix products, arithmetic and copies ran while one was open for 0% -> 0% of each run, Pallas kernels for 6% -> 11%
where the time goes in v2:
time: 83.2 us; the launch traced here: 82.9 us
  starting transfers between devices  46 us (55%)
  waiting for transfers between devices  24.2 us (29%)
  Pallas kernels  12 us (14%)
    ppermute x7, starting transfers between devices, send(): lax.ppermute(message, 'tm', [(i, i ^ k) for i in range(n_tm)])  20.7 us
    ppermute x8, starting transfers between devices, round_of(): return lax.ppermute(message, ('tm', 'fsdp'), pairs)  16.4 us
    ppermute x2, waiting for transfers between devices, swap(): return lax.ppermute(x, 'fsdp', [(i, i ^ bit) for i in range(n_fsdp)])  10.1 us
    ppermute x7, waiting for transfers between devices, send(): lax.ppermute(message, 'tm', [(i, i ^ k) for i in range(n_tm)])  9.27 us
    all_to_all x1, starting transfers between devices, body_permutes(): lax.all_to_all(pack(heads_out(queries), heads_out(key_states), heads_out(...  5.85 us
    pallas_call x1, Pallas kernels, project(): pl.pallas_call(functools.partial(project_kernel, n_tm), out_shape=[jax.Sh...  4.99 us
    ppermute x8, waiting for transfers between devices, round_of(): return lax.ppermute(message, ('tm', 'fsdp'), pairs)  4.2 us
    ppermute x2, starting transfers between devices, swap(): return lax.ppermute(x, 'fsdp', [(i, i ^ bit) for i in range(n_fsdp)])  3.08 us
  transfers between devices with their start and end apart: 18, of which 9 were waited for; matrix products, arithmetic and copies ran while one was open for 0% of the time, Pallas kernels for 11%

profile of v2, /device:TPU:0, one launch (start us, length us, event | category | flops | bytes accessed | tf_op | source)
XLA Modules:
  0.0 82.9 jit_solution(15233209339347769512)
XLA Ops:
  0.6 0.5 collective-permute-start.1
  1.1 2.6 %collective-permute-start = (bf16[4,32,3072]{2,1,0:T(8,128)(2,1)}, bf16[4,32,3072]{2,1,0:T(8,128)(2,1)}, u32[]{:S(2)}, u32[]{:S(2)}) collective-permute-start(bf16[4,32,3072]{2,1,0:T(8,128)(2,1)} %own_ref.1), channel_id=1, source_target_pairs={{0,2},{1,3},{2,0},{3,1},{4,6},{5,7},{6,4},{7,5},{8,10},{9,11},{10,... | collective-permute-start | bytes 2359304 | tf_op jit(solution)/shard_map/ppermute | solution.py:356
  3.7 2.5 %pack.1 = bf16[8,3,4,3,16,128]{5,4,3,2,1,0:T(8,128)(2,1)} custom-call(bf16[4,12,32,128]{3,2,1,0:T(8,128)(2,1)} %bitcast.6, bf16[4,12,32,128]{3,2,1,0:T(8,128)(2,1)} %bitcast.7, bf16[4,12,32,128]{3,2,1,0:T(8,128)(2,1)} %bitcast.8), custom_call_target="tpu_custom_call" | custom-call | tf_op jit(solution)/shard_map/pack/pallas_call | solution.py:113
  6.2 5.8 %all-to-all-start = ((bf16[8,3,4,3,16,128]{5,4,3,2,1,0:T(8,128)(2,1)}), bf16[8,3,4,3,16,128]{5,4,3,2,1,0:T(8,128)(2,1)S(1)}, u32[]{:S(2)}, u32[]{:S(2)}) async-start(bf16[8,3,4,3,16,128]{5,4,3,2,1,0:T(8,128)(2,1)} %pack.1), calls=%async_computation | async-start | bytes 2359296 | tf_op jit(solution)/shard_map/all_to_all | solution.py:374
  12.1 10.1 %collective-permute-done.other_ref = bf16[4,32,3072]{2,1,0:T(8,128)(2,1)} collective-permute-done((bf16[4,32,3072]{2,1,0:T(8,128)(2,1)}, bf16[4,32,3072]{2,1,0:T(8,128)(2,1)}, u32[]{:S(2)}, u32[]{:S(2)}) %collective-permute-start) | collective-permute-done | bytes 786464 | tf_op jit(solution)/shard_map/ppermute | solution.py:356
  22.2 0.0 collective-permute-done.1.w_other_ref
  22.2 5.0 %project.1 = (bf16[3,4,16,128]{3,2,1,0:T(8,128)(2,1)S(1)}, bf16[3,4,16,128]{3,2,1,0:T(8,128)(2,1)S(1)}, bf16[3,4,16,128]{3,2,1,0:T(8,128)(2,1)S(1)}, bf16[3,4,16...) custom-call(bf16[4,32,3072]{2,1,0:T(8,128)(2,1)} %own_ref.1, ...), custom_call_target="tpu_custom_call" | custom-call | flops 77309411328 | bytes 6291456 | tf_op jit(solution)/shard_map/project/pallas_call | solution.py:204
  27.2 0.7 collective-permute-start.2
  27.8 4.5 %collective-permute-start.3 = (bf16[3,4,16,128]{3,2,1,0:T(8,128)(2,1)S(1)}, bf16[3,4,16,128]{3,2,1,0:T(8,128)(2,1)S(1)}, u32[]{:S(2)}, u32[]{:S(2)}) collective-permute-start(bf16[3,4,16,128]{3,2,1,0:T(8,128)(2,1)S(1)} %get-tuple-element.27), channel_id=1, source_target_pairs={{0,2},{1,3},{2,6},{3,7},{4,0},{5,1},{6,4},{7,5},{8,10},{9,11},{10,... | collective-permute-start | bytes 147464 | tf_op jit(solution)/shard_map/ppermute | solution.py:369
  32.4 1.6 %collective-permute-start.4 = (bf16[3,4,16,128]{3,2,1,0:T(8,128)(2,1)S(1)}, bf16[3,4,16,128]{3,2,1,0:T(8,128)(2,1)S(1)}, u32[]{:S(2)}, u32[]{:S(2)}) collective-permute-start(bf16[3,4,16,128]{3,2,1,0:T(8,128)(2,1)S(1)} %get-tuple-element.28), channel_id=1, source_target_pairs={{0,8},{1,9},{2,12},{3,13},{4,10},{5,11},{6,14},{7,15},{8,0},{9,1},... | collective-permute-start | bytes 147464 | tf_op jit(solution)/shard_map/ppermute | solution.py:369
  34.0 0.8 %collective-permute-start.5 = (bf16[3,4,16,128]{3,2,1,0:T(8,128)(2,1)}, bf16[3,4,16,128]{3,2,1,0:T(8,128)(2,1)S(1)}, u32[]{:S(2)}, u32[]{:S(2)}) collective-permute-start(bf16[3,4,16,128]{3,2,1,0:T(8,128)(2,1)} %get-tuple-element.29), channel_id=1, source_target_pairs={{0,10},{1,11},{2,14},{3,15},{4,8},{5,9},{6,12},{7,13},{8,2},{9,3},... | collective-permute-start | bytes 147464 | tf_op jit(solution)/shard_map/ppermute | solution.py:369
  34.8 2.6 %collective-permute-start.6 = (bf16[3,4,16,128]{3,2,1,0:T(8,128)(2,1)}, bf16[3,4,16,128]{3,2,1,0:T(8,128)(2,1)S(1)}, u32[]{:S(2)}, u32[]{:S(2)}) collective-permute-start(bf16[3,4,16,128]{3,2,1,0:T(8,128)(2,1)} %get-tuple-element.30), channel_id=1, source_target_pairs={{0,16},{1,17},{2,20},{3,21},{4,18},{5,19},{6,22},{7,23},{8,24},{9,... | collective-permute-start | bytes 147464 | tf_op jit(solution)/shard_map/ppermute | solution.py:369
  37.4 0.0 collective-permute-done.2.refs_0_
  37.4 1.7 %collective-permute-start.7 = (bf16[3,4,16,128]{3,2,1,0:T(8,128)(2,1)}, bf16[3,4,16,128]{3,2,1,0:T(8,128)(2,1)S(1)}, u32[]{:S(2)}, u32[]{:S(2)}) collective-permute-start(bf16[3,4,16,128]{3,2,1,0:T(8,128)(2,1)} %get-tuple-element.31), channel_id=1, source_target_pairs={{0,18},{1,19},{2,22},{3,23},{4,16},{5,17},{6,20},{7,21},{8,26},{9,... | collective-permute-start | bytes 147464 | tf_op jit(solution)/shard_map/ppermute | solution.py:369
  39.1 0.0 collective-permute-done.3.refs_1_
  39.1 3.6 %collective-permute-start.8 = (bf16[3,4,16,128]{3,2,1,0:T(8,128)(2,1)}, bf16[3,4,16,128]{3,2,1,0:T(8,128)(2,1)S(1)}, u32[]{:S(2)}, u32[]{:S(2)}) collective-permute-start(bf16[3,4,16,128]{3,2,1,0:T(8,128)(2,1)} %get-tuple-element.32), channel_id=1, source_target_pairs={{0,24},{1,25},{2,28},{3,29},{4,26},{5,27},{6,30},{7,31},{8,16},{9,... | collective-permute-start | bytes 147464 | tf_op jit(solution)/shard_map/ppermute | solution.py:369
  42.7 0.0 collective-permute-done.4.refs_2_
  42.7 0.8 collective-permute-start.9
  43.6 0.7 all-to-all-done.qkv
  44.2 1.4 %probs.1 = (bf16[12,128,128]{2,1,0:T(8,128)(2,1)S(1)}, bf16[12,128,128]{2,1,0:T(8,128)(2,1)S(1)}, bf16[12,128,128]{2,1,0:T(8,128)(2,1)S(1)}, f32[12,128,128]{2,1,0:T(8,128)S(1)}) custom-call(bf16[8,3,4,3,16,128]{5,4,3,2,1,0:T(8,128)(2,1)S(1)} %all-to-all-done.qkv), custom_call_target="tpu_custom_call" | custom-call | tf_op jit(solution)/shard_map/probs/pallas_call | solution.py:315
  45.6 0.0 collective-permute-done.5.refs_3_
  45.7 1.2 %collective-permute-done.6.refs_4_ = bf16[3,4,16,128]{3,2,1,0:T(8,128)(2,1)S(1)} collective-permute-done((bf16[3,4,16,128]{3,2,1,0:T(8,128)(2,1)}, bf16[3,4,16,128]{3,2,1,0:T(8,128)(2,1)S(1)}, u32[]{:S(2)}, u32[]{:S(2)}) %collective-permute-start.6) | collective-permute-done | bytes 49184 | tf_op jit(solution)/shard_map/ppermute | solution.py:369
  46.9 1.8 %collective-permute-done.7.refs_5_ = bf16[3,4,16,128]{3,2,1,0:T(8,128)(2,1)S(1)} collective-permute-done((bf16[3,4,16,128]{3,2,1,0:T(8,128)(2,1)}, bf16[3,4,16,128]{3,2,1,0:T(8,128)(2,1)S(1)}, u32[]{:S(2)}, u32[]{:S(2)}) %collective-permute-start.7) | collective-permute-done | bytes 49184 | tf_op jit(solution)/shard_map/ppermute | solution.py:369
  48.7 0.0 collective-permute-done.8.refs_6_
  48.7 1.1 %collective-permute-done.9.refs_7_ = bf16[3,4,16,128]{3,2,1,0:T(8,128)(2,1)S(1)} collective-permute-done((bf16[3,4,16,128]{3,2,1,0:T(8,128)(2,1)}, bf16[3,4,16,128]{3,2,1,0:T(8,128)(2,1)S(1)}, u32[]{:S(2)}, u32[]{:S(2)}) %collective-permute-start.9) | collective-permute-done | bytes 49184 | tf_op jit(solution)/shard_map/ppermute | solution.py:369
  49.8 1.9 %grads.1 = (bf16[3,4,3,16,128]{4,3,2,1,0:T(8,128)(2,1)S(1)}, bf16[3,4,3,16,128]{4,3,2,1,0:T(8,128)(2,1)S(1)}, bf16[3,4,3,16,128]{4,3,2,1,0:T(8,128)(2,1)S(1)}, b...) custom-call(bf16[3,4,16,128]{3,2,1,0:T(8,128)(2,1)S(1)} %collective-, ...), custom_call_target="tpu_custom_call" | custom-call | tf_op jit(solution)/shard_map/grads/pallas_call | solution.py:331
  51.7 1.3 %collective-permute-start.10 = (bf16[3,4,3,16,128]{4,3,2,1,0:T(8,128)(2,1)S(1)}, bf16[3,4,3,16,128]{4,3,2,1,0:T(8,128)(2,1)S(1)}, u32[]{:S(2)}, u32[]{:S(2)}) collective-permute-start(bf16[3,4,3,16,128]{4,3,2,1,0:T(8,128)(2,1)S(1)} %get-tuple-element.38), channel_id=1, source_target_pairs={{0,28},{4,24},{8,20},{12,16},{16,12},{20,8},{24,4},{28,0},{1,29},{... | collective-permute-start | bytes 442376 | tf_op jit(solution)/shard_map/ppermute | solution.py:359
  53.1 0.6 collective-permute-start.11
  53.7 3.1 %collective-permute-start.12 = (bf16[3,4,3,16,128]{4,3,2,1,0:T(8,128)(2,1)S(1)}, bf16[3,4,3,16,128]{4,3,2,1,0:T(8,128)(2,1)S(1)}, u32[]{:S(2)}, u32[]{:S(2)}) collective-permute-start(bf16[3,4,3,16,128]{4,3,2,1,0:T(8,128)(2,1)S(1)} %get-tuple-element.40), channel_id=1, source_target_pairs={{0,24},{4,28},{8,16},{12,20},{16,8},{20,12},{24,0},{28,4},{1,25},{... | collective-permute-start | bytes 442376 | tf_op jit(solution)/shard_map/ppermute | solution.py:359
  56.8 1.7 %collective-permute-start.13 = (bf16[3,4,3,16,128]{4,3,2,1,0:T(8,128)(2,1)S(1)}, bf16[3,4,3,16,128]{4,3,2,1,0:T(8,128)(2,1)S(1)}, u32[]{:S(2)}, u32[]{:S(2)}) collective-permute-start(bf16[3,4,3,16,128]{4,3,2,1,0:T(8,128)(2,1)S(1)} %get-tuple-element.41), channel_id=1, source_target_pairs={{0,20},{4,16},{8,28},{12,24},{16,4},{20,0},{24,12},{28,8},{1,21},{... | collective-permute-start | bytes 442376 | tf_op jit(solution)/shard_map/ppermute | solution.py:359
  58.5 0.5 collective-permute-start.14
  59.0 2.4 %collective-permute-done.10.refs_0_ = bf16[3,4,3,16,128]{4,3,2,1,0:T(8,128)(2,1)S(1)} collective-permute-done((bf16[3,4,3,16,128]{4,3,2,1,0:T(8,128)(2,1)S(1)}, bf16[3,4,3,16,128]{4,3,2,1,0:T(8,128)(2,1)S(1)}, u32[]{:S(2)}, u32[]{:S(2)}) %collective-permute-start.10) | collective-permute-done | bytes 147488 | tf_op jit(solution)/shard_map/ppermute | solution.py:359
  61.4 11.4 %collective-permute-start.15 = (bf16[3,4,3,16,128]{4,3,2,1,0:T(8,128)(2,1)S(1)}, bf16[3,4,3,16,128]{4,3,2,1,0:T(8,128)(2,1)S(1)}, u32[]{:S(2)}, u32[]{:S(2)}) collective-permute-start(bf16[3,4,3,16,128]{4,3,2,1,0:T(8,128)(2,1)S(1)} %get-tuple-element.43), channel_id=1, source_target_pairs={{0,8},{4,12},{8,0},{12,4},{16,24},{20,28},{24,16},{28,20},{1,9},{5... | collective-permute-start | bytes 442376 | tf_op jit(solution)/shard_map/ppermute | solution.py:359
  72.8 0.5 collective-permute-done.11.refs_1_
  73.3 2.0 %collective-permute-start.16 = (bf16[3,4,3,16,128]{4,3,2,1,0:T(8,128)(2,1)S(1)}, bf16[3,4,3,16,128]{4,3,2,1,0:T(8,128)(2,1)S(1)}, u32[]{:S(2)}, u32[]{:S(2)}) collective-permute-start(bf16[3,4,3,16,128]{4,3,2,1,0:T(8,128)(2,1)S(1)} %get-tuple-element.44), channel_id=1, source_target_pairs={{0,4},{4,0},{8,12},{12,8},{16,20},{20,16},{24,28},{28,24},{1,5},{5... | collective-permute-start | bytes 442376 | tf_op jit(solution)/shard_map/ppermute | solution.py:359
  75.3 0.0 collective-permute-done.12.refs_2_
  75.3 4.4 %collective-permute-done.13.refs_3_ = bf16[3,4,3,16,128]{4,3,2,1,0:T(8,128)(2,1)S(1)} collective-permute-done((bf16[3,4,3,16,128]{4,3,2,1,0:T(8,128)(2,1)S(1)}, bf16[3,4,3,16,128]{4,3,2,1,0:T(8,128)(2,1)S(1)}, u32[]{:S(2)}, u32[]{:S(2)}) %collective-permute-start.13) | collective-permute-done | bytes 147488 | tf_op jit(solution)/shard_map/ppermute | solution.py:359
  79.7 0.0 collective-permute-done.14.refs_4_
  79.7 0.0 collective-permute-done.15.refs_5_
  79.7 2.0 %collective-permute-done.16.refs_6_ = bf16[3,4,3,16,128]{4,3,2,1,0:T(8,128)(2,1)S(1)} collective-permute-done((bf16[3,4,3,16,128]{4,3,2,1,0:T(8,128)(2,1)S(1)}, bf16[3,4,3,16,128]{4,3,2,1,0:T(8,128)(2,1)S(1)}, u32[]{:S(2)}, u32[]{:S(2)}) %collective-permute-start.16) | collective-permute-done | bytes 147488 | tf_op jit(solution)/shard_map/ppermute | solution.py:359
  81.7 1.2 %unpack.1 = (bf16[4,12,32,128]{3,2,1,0:T(8,128)(2,1)}, bf16[4,12,32,128]{3,2,1,0:T(8,128)(2,1)}, bf16[4,12,32,128]{3,2,1,0:T(8,128)(2,1)}) custom-call(bf16[3,4,3,16,128]{4,3,2,1,0:T(8,128)(2,1)S(1)} %collective-permute-done.10.refs_0_, bf16[3,4,3,16,128]{4,3,2,1,0:T(8,128)(2,1)S(1)} %collective-permute-done.11.refs_1_, ...), custom_call_target="tpu_custom_call" | custom-call | tf_op jit(solution)/shard_map/unpack/pallas_call | solution.py:145
Async XLA Ops:
  0.6 21.5 %collective-permute-start.1 = (bf16[384,3072]{1,0:T(8,128)(2,1)}, bf16[384,3072]{1,0:T(8,128)(2,1)S(1)}, u32[]{:S(2)}, u32[]{:S(2)}) collective-permute-start(bf16[384,3072]{1,0:T(8,128)(2,1)} %w_own_ref.1), channel_id=1, source_target_pairs={{0,1},{1,0},{2,3},{3,2},{4,5},{5,4},{6,7},{7,6},{8,9},{9,8},{10,11... | collective-permute-start | bytes 7077896 | tf_op jit(solution)/shard_map/ppermute | solution.py:356
  1.1 21.0 %collective-permute-start = (bf16[4,32,3072]{2,1,0:T(8,128)(2,1)}, bf16[4,32,3072]{2,1,0:T(8,128)(2,1)}, u32[]{:S(2)}, u32[]{:S(2)}) collective-permute-start(bf16[4,32,3072]{2,1,0:T(8,128)(2,1)} %own_ref.1), channel_id=1, source_target_pairs={{0,2},{1,3},{2,0},{3,1},{4,6},{5,7},{6,4},{7,5},{8,10},{9,11},{10,... | collective-permute-start | bytes 2359304 | tf_op jit(solution)/shard_map/ppermute | solution.py:356
  6.2 38.0 %all-to-all-start = ((bf16[8,3,4,3,16,128]{5,4,3,2,1,0:T(8,128)(2,1)}), bf16[8,3,4,3,16,128]{5,4,3,2,1,0:T(8,128)(2,1)S(1)}, u32[]{:S(2)}, u32[]{:S(2)}) async-start(bf16[8,3,4,3,16,128]{5,4,3,2,1,0:T(8,128)(2,1)} %pack.1), calls=%async_computation | async-start | bytes 2359296 | tf_op jit(solution)/shard_map/all_to_all | solution.py:374
  27.2 10.2 %collective-permute-start.2 = (bf16[3,4,16,128]{3,2,1,0:T(8,128)(2,1)S(1)}, bf16[3,4,16,128]{3,2,1,0:T(8,128)(2,1)S(1)}, u32[]{:S(2)}, u32[]{:S(2)}) collective-permute-start(bf16[3,4,16,128]{3,2,1,0:T(8,128)(2,1)S(1)} %get-tuple-element.26), channel_id=1, source_target_pairs={{0,0},{1,1},{2,4},{3,5},{4,2},{5,3},{6,6},{7,7},{8,8},{9,9},{10,12... | collective-permute-start | bytes 147464 | tf_op jit(solution)/shard_map/ppermute | solution.py:369
  27.8 11.3 %collective-permute-start.3 = (bf16[3,4,16,128]{3,2,1,0:T(8,128)(2,1)S(1)}, bf16[3,4,16,128]{3,2,1,0:T(8,128)(2,1)S(1)}, u32[]{:S(2)}, u32[]{:S(2)}) collective-permute-start(bf16[3,4,16,128]{3,2,1,0:T(8,128)(2,1)S(1)} %get-tuple-element.27), channel_id=1, source_target_pairs={{0,2},{1,3},{2,6},{3,7},{4,0},{5,1},{6,4},{7,5},{8,10},{9,11},{10,... | collective-permute-start | bytes 147464 | tf_op jit(solution)/shard_map/ppermute | solution.py:369
  32.4 10.4 %collective-permute-start.4 = (bf16[3,4,16,128]{3,2,1,0:T(8,128)(2,1)S(1)}, bf16[3,4,16,128]{3,2,1,0:T(8,128)(2,1)S(1)}, u32[]{:S(2)}, u32[]{:S(2)}) collective-permute-start(bf16[3,4,16,128]{3,2,1,0:T(8,128)(2,1)S(1)} %get-tuple-element.28), channel_id=1, source_target_pairs={{0,8},{1,9},{2,12},{3,13},{4,10},{5,11},{6,14},{7,15},{8,0},{9,1},... | collective-permute-start | bytes 147464 | tf_op jit(solution)/shard_map/ppermute | solution.py:369
  34.0 11.7 %collective-permute-start.5 = (bf16[3,4,16,128]{3,2,1,0:T(8,128)(2,1)}, bf16[3,4,16,128]{3,2,1,0:T(8,128)(2,1)S(1)}, u32[]{:S(2)}, u32[]{:S(2)}) collective-permute-start(bf16[3,4,16,128]{3,2,1,0:T(8,128)(2,1)} %get-tuple-element.29), channel_id=1, source_target_pairs={{0,10},{1,11},{2,14},{3,15},{4,8},{5,9},{6,12},{7,13},{8,2},{9,3},... | collective-permute-start | bytes 147464 | tf_op jit(solution)/shard_map/ppermute | solution.py:369
  34.8 12.1 %collective-permute-start.6 = (bf16[3,4,16,128]{3,2,1,0:T(8,128)(2,1)}, bf16[3,4,16,128]{3,2,1,0:T(8,128)(2,1)S(1)}, u32[]{:S(2)}, u32[]{:S(2)}) collective-permute-start(bf16[3,4,16,128]{3,2,1,0:T(8,128)(2,1)} %get-tuple-element.30), channel_id=1, source_target_pairs={{0,16},{1,17},{2,20},{3,21},{4,18},{5,19},{6,22},{7,23},{8,24},{9,... | collective-permute-start | bytes 147464 | tf_op jit(solution)/shard_map/ppermute | solution.py:369
  37.4 11.3 %collective-permute-start.7 = (bf16[3,4,16,128]{3,2,1,0:T(8,128)(2,1)}, bf16[3,4,16,128]{3,2,1,0:T(8,128)(2,1)S(1)}, u32[]{:S(2)}, u32[]{:S(2)}) collective-permute-start(bf16[3,4,16,128]{3,2,1,0:T(8,128)(2,1)} %get-tuple-element.31), channel_id=1, source_target_pairs={{0,18},{1,19},{2,22},{3,23},{4,16},{5,17},{6,20},{7,21},{8,26},{9,... | collective-permute-start | bytes 147464 | tf_op jit(solution)/shard_map/ppermute | solution.py:369
  39.1 9.6 %collective-permute-start.8 = (bf16[3,4,16,128]{3,2,1,0:T(8,128)(2,1)}, bf16[3,4,16,128]{3,2,1,0:T(8,128)(2,1)S(1)}, u32[]{:S(2)}, u32[]{:S(2)}) collective-permute-start(bf16[3,4,16,128]{3,2,1,0:T(8,128)(2,1)} %get-tuple-element.32), channel_id=1, source_target_pairs={{0,24},{1,25},{2,28},{3,29},{4,26},{5,27},{6,30},{7,31},{8,16},{9,... | collective-permute-start | bytes 147464 | tf_op jit(solution)/shard_map/ppermute | solution.py:369
  42.7 7.1 %collective-permute-start.9 = (bf16[3,4,16,128]{3,2,1,0:T(8,128)(2,1)}, bf16[3,4,16,128]{3,2,1,0:T(8,128)(2,1)S(1)}, u32[]{:S(2)}, u32[]{:S(2)}) collective-permute-start(bf16[3,4,16,128]{3,2,1,0:T(8,128)(2,1)} %get-tuple-element.33), channel_id=1, source_target_pairs={{0,26},{1,27},{2,30},{3,31},{4,24},{5,25},{6,28},{7,29},{8,18},{9,... | collective-permute-start | bytes 147464 | tf_op jit(solution)/shard_map/ppermute | solution.py:369
  51.7 9.6 %collective-permute-start.10 = (bf16[3,4,3,16,128]{4,3,2,1,0:T(8,128)(2,1)S(1)}, bf16[3,4,3,16,128]{4,3,2,1,0:T(8,128)(2,1)S(1)}, u32[]{:S(2)}, u32[]{:S(2)}) collective-permute-start(bf16[3,4,3,16,128]{4,3,2,1,0:T(8,128)(2,1)S(1)} %get-tuple-element.38), channel_id=1, source_target_pairs={{0,28},{4,24},{8,20},{12,16},{16,12},{20,8},{24,4},{28,0},{1,29},{... | collective-permute-start | bytes 442376 | tf_op jit(solution)/shard_map/ppermute | solution.py:359
  53.1 20.2 %collective-permute-start.11 = (bf16[3,4,3,16,128]{4,3,2,1,0:T(8,128)(2,1)S(1)}, bf16[3,4,3,16,128]{4,3,2,1,0:T(8,128)(2,1)S(1)}, u32[]{:S(2)}, u32[]{:S(2)}) collective-permute-start(bf16[3,4,3,16,128]{4,3,2,1,0:T(8,128)(2,1)S(1)} %get-tuple-element.39), channel_id=1, source_target_pairs={{0,16},{4,20},{8,24},{12,28},{16,0},{20,4},{24,8},{28,12},{1,17},{... | collective-permute-start | bytes 442376 | tf_op jit(solution)/shard_map/ppermute | solution.py:359
  53.7 21.6 %collective-permute-start.12 = (bf16[3,4,3,16,128]{4,3,2,1,0:T(8,128)(2,1)S(1)}, bf16[3,4,3,16,128]{4,3,2,1,0:T(8,128)(2,1)S(1)}, u32[]{:S(2)}, u32[]{:S(2)}) collective-permute-start(bf16[3,4,3,16,128]{4,3,2,1,0:T(8,128)(2,1)S(1)} %get-tuple-element.40), channel_id=1, source_target_pairs={{0,24},{4,28},{8,16},{12,20},{16,8},{20,12},{24,0},{28,4},{1,25},{... | collective-permute-start | bytes 442376 | tf_op jit(solution)/shard_map/ppermute | solution.py:359
  56.8 22.9 %collective-permute-start.13 = (bf16[3,4,3,16,128]{4,3,2,1,0:T(8,128)(2,1)S(1)}, bf16[3,4,3,16,128]{4,3,2,1,0:T(8,128)(2,1)S(1)}, u32[]{:S(2)}, u32[]{:S(2)}) collective-permute-start(bf16[3,4,3,16,128]{4,3,2,1,0:T(8,128)(2,1)S(1)} %get-tuple-element.41), channel_id=1, source_target_pairs={{0,20},{4,16},{8,28},{12,24},{16,4},{20,0},{24,12},{28,8},{1,21},{... | collective-permute-start | bytes 442376 | tf_op jit(solution)/shard_map/ppermute | solution.py:359
  58.5 21.2 %collective-permute-start.14 = (bf16[3,4,3,16,128]{4,3,2,1,0:T(8,128)(2,1)S(1)}, bf16[3,4,3,16,128]{4,3,2,1,0:T(8,128)(2,1)S(1)}, u32[]{:S(2)}, u32[]{:S(2)}) collective-permute-start(bf16[3,4,3,16,128]{4,3,2,1,0:T(8,128)(2,1)S(1)} %get-tuple-element.42), channel_id=1, source_target_pairs={{0,12},{4,8},{8,4},{12,0},{16,28},{20,24},{24,20},{28,16},{1,13},{... | collective-permute-start | bytes 442376 | tf_op jit(solution)/shard_map/ppermute | solution.py:359
  61.4 18.3 %collective-permute-start.15 = (bf16[3,4,3,16,128]{4,3,2,1,0:T(8,128)(2,1)S(1)}, bf16[3,4,3,16,128]{4,3,2,1,0:T(8,128)(2,1)S(1)}, u32[]{:S(2)}, u32[]{:S(2)}) collective-permute-start(bf16[3,4,3,16,128]{4,3,2,1,0:T(8,128)(2,1)S(1)} %get-tuple-element.43), channel_id=1, source_target_pairs={{0,8},{4,12},{8,0},{12,4},{16,24},{20,28},{24,16},{28,20},{1,9},{5... | collective-permute-start | bytes 442376 | tf_op jit(solution)/shard_map/ppermute | solution.py:359
  73.3 8.4 %collective-permute-start.16 = (bf16[3,4,3,16,128]{4,3,2,1,0:T(8,128)(2,1)S(1)}, bf16[3,4,3,16,128]{4,3,2,1,0:T(8,128)(2,1)S(1)}, u32[]{:S(2)}, u32[]{:S(2)}) collective-permute-start(bf16[3,4,3,16,128]{4,3,2,1,0:T(8,128)(2,1)S(1)} %get-tuple-element.44), channel_id=1, source_target_pairs={{0,4},{4,0},{8,12},{12,8},{16,20},{20,16},{24,28},{28,24},{1,5},{5... | collective-permute-start | bytes 442376 | tf_op jit(solution)/shard_map/ppermute | solution.py:359

commit v3 on v2

--- a/solution.py
+++ b/solution.py
@@ -12,7 +12,8 @@
 VMEM = pl.BlockSpec(memory_space=pltpu.VMEM)
 MIB = 1024 * 1024
 SLOTS = (7, 4, 6, 5, 3, 2, 1, 0)
-ROUNDS = (0, 1, 2, 3, 4, 5, 6, 7)
+FAR = (7, 4, 6, 5)
+ROUNDS = (0, 1, 4, 5, 6, 7, 2, 3)
 GROUPS = 4
 
 
@@ -94,31 +95,85 @@
         copy.wait()
 
 
-def pack_kernel(n_tm, q_ref, k_ref, v_ref, out, sems):
-    _, _, _, g_heads, p_rows, _ = out.shape
-    copies = []
-    for i in range(n_tm):
-        heads = slice(group_of(i) * g_heads, (group_of(i) + 1) * g_heads)
-        rows = slice(part_of(i) * p_rows, (part_of(i) + 1) * p_rows)
-        for a, ref in enumerate((q_ref, k_ref, v_ref)):
-            copies.append(
-                pltpu.make_async_copy(ref.at[:, heads, rows], out.at[i, a], sems.at[3 * i + a])
-            )
-    copy_all(copies)
-
-
-def pack(q, k, v, n_tm, p_rows):
+def pack_copies(there, q_k_v, message, sems):
+    _, _, g_heads, p_rows, _ = message.shape
+    heads = pl.ds(group_of(there) * g_heads, g_heads)
+    rows = pl.ds(pl.multiple_of(part_of(there) * p_rows, p_rows), p_rows)
+    return [
+        pltpu.make_async_copy(ref.at[:, heads, rows], message.at[a], sems.at[a])
+        for a, ref in enumerate(q_k_v)
+    ]
+
+
+def pack_far_kernel(ks, *refs):
+    q_k_v, outs, (stage, in_sems, out_sems) = refs[:3], refs[3:-3], refs[-3:]
+    me = lax.axis_index("tm")
+    arrivals = [
+        pack_copies(me ^ k, q_k_v, stage.at[j], in_sems.at[j]) for j, k in enumerate(ks)
+    ]
+    departures = [
+        pltpu.make_async_copy(stage.at[j], out, out_sems.at[j]) for j, out in enumerate(outs)
+    ]
+    for copies in arrivals:
+        for copy in copies:
+            copy.start()
+    for copies, departure in zip(arrivals, departures):
+        for copy in copies:
+            copy.wait()
+        departure.start()
+    for departure in departures:
+        departure.wait()
+
+
+def pack_near_kernel(*refs):
+    q_k_v, out, stage, sems = refs[:3], refs[3], refs[4], refs[5]
+    first = lax.axis_index("tm") // GROUPS * GROUPS
+    copy_all(
+        [
+            copy
+            for j in range(GROUPS)
+            for copy in pack_copies(first + j, q_k_v, stage.at[j], sems.at[j])
+        ]
+    )
+    out[...] = stage[...]
+
+
+def message_shape(q, p_rows):
     frames_dev, heads, _, head_size = q.shape
-    shape = (n_tm, 3, frames_dev, heads // GROUPS, p_rows, head_size)
-    return pl.pallas_call(
-        functools.partial(pack_kernel, n_tm),
-        out_shape=jax.ShapeDtypeStruct(shape, q.dtype),
+    return (3, frames_dev, heads // GROUPS, p_rows, head_size)
+
+
+def pack_far(q_k_v, ks, p_rows):
+    shape = message_shape(q_k_v[0], p_rows)
+    return pl.pallas_call(
+        functools.partial(pack_far_kernel, ks),
+        out_shape=[jax.ShapeDtypeStruct(shape, q_k_v[0].dtype)] * len(ks),
+        in_specs=[HBM] * 3,
+        out_specs=[ANY] * len(ks),
+        scratch_shapes=[
+            pltpu.VMEM((len(ks),) + shape, q_k_v[0].dtype),
+            pltpu.SemaphoreType.DMA((len(ks), 3)),
+            pltpu.SemaphoreType.DMA((len(ks),)),
+        ],
+        compiler_params=pltpu.CompilerParams(vmem_limit_bytes=4 * MIB),
+        name="pack_far",
+    )(*(pltpu.with_memory_space_constraint(x, pltpu.HBM) for x in q_k_v))
+
+
+def pack_near(q_k_v, p_rows):
+    shape = (GROUPS,) + message_shape(q_k_v[0], p_rows)
+    return pl.pallas_call(
+        pack_near_kernel,
+        out_shape=jax.ShapeDtypeStruct(shape, q_k_v[0].dtype),
         in_specs=[HBM] * 3,
         out_specs=VMEM,
-        scratch_shapes=[pltpu.SemaphoreType.DMA((3 * n_tm,))],
+        scratch_shapes=[
+            pltpu.VMEM(shape, q_k_v[0].dtype),
+            pltpu.SemaphoreType.DMA((GROUPS, 3)),
+        ],
         compiler_params=pltpu.CompilerParams(vmem_limit_bytes=4 * MIB),
-        name="pack",
-    )(*(pltpu.with_memory_space_constraint(x, pltpu.HBM) for x in (q, k, v)))
+        name="pack_near",
+    )(*(pltpu.with_memory_space_constraint(x, pltpu.HBM) for x in q_k_v))
 
 
 def unpack_kernel(slots, *refs):
@@ -153,32 +208,44 @@
     )(*grads)
 
 
-def project_kernel(n_tm, own_ref, other_ref, w_own_ref, w_other_ref, *refs):
-    outs = refs[:n_tm]
-    rows_ref, w_ref, res, row_sems, w_sems, out_sems = refs[n_tm:]
+def project_into(res, at, w, out):
+    g_heads, frames_dev, pos_dev, head_size = res.shape[2:]
+    for h in range(g_heads):
+        res[w, at, h] = out[:, h * head_size : (h + 1) * head_size].reshape(
+            frames_dev, pos_dev, head_size
+        )
+
+
+def flat(rows_ref):
+    frames_dev, pos_dev, width = rows_ref.shape
+    return rows_ref[...].reshape(frames_dev * pos_dev, width)
+
+
+def project_own_kernel(own_ref, w_own_ref, w_other_ref, res, w_ref, rows_ref, sems):
+    core = lax.rem(lax.axis_index("fsdp"), 2)
+    w_copies = [
+        pltpu.make_async_copy(ref, w_ref.at[i], sems.at[i])
+        for i, ref in enumerate((w_own_ref, w_other_ref))
+    ]
+    rows_copy = pltpu.make_async_copy(own_ref, rows_ref, sems.at[2])
+    for copy in (w_copies[0], rows_copy, w_copies[1]):
+        copy.start()
+    rows_copy.wait()
+    rows = flat(rows_ref)
+    for i, copy in enumerate(w_copies):
+        copy.wait()
+        project_into(res, 0, core ^ i, dot(rows, w_ref[i], NT).astype(jnp.bfloat16))
+
+
+def project_other_kernel(n_tm, other_ref, w_ref, own_ref, *refs):
+    outs, res, sems = refs[:n_tm], refs[n_tm], refs[n_tm + 1]
     me, fs = lax.axis_index("tm"), lax.axis_index("fsdp")
     half, core = fs // 2, lax.rem(fs, 2)
-    _, _, g_heads, frames_dev, pos_dev, head_size = res.shape
-    row_copies = [
-        pltpu.make_async_copy(ref, rows_ref.at[i], row_sems.at[i])
-        for i, ref in enumerate((own_ref, other_ref))
-    ]
-    w_copies = [
-        pltpu.make_async_copy(ref, w_ref.at[i], w_sems.at[i])
-        for i, ref in enumerate((w_own_ref, w_other_ref))
-    ]
-    for copy in (w_copies[0], *row_copies, w_copies[1]):
-        copy.start()
-    for copy in row_copies:
-        copy.wait()
-    rows = rows_ref[...].reshape(2 * frames_dev * pos_dev, rows_ref.shape[-1])
-    for w in range(2):
-        w_copies[w].wait()
-        out = dot(rows, w_ref[w], NT).astype(jnp.bfloat16)
-        for h in range(g_heads):
-            res[core ^ w, :, h] = out[:, h * head_size : (h + 1) * head_size].reshape(
-                2, frames_dev, pos_dev, head_size
-            )
+    rows = flat(other_ref)
+    for i in range(2):
+        project_into(res, 1, core ^ i, dot(rows, w_ref[i], NT).astype(jnp.bfloat16))
+    for i in range(2):
+        res[i, 0] = own_ref[i, 0]
     p_rows = outs[0].shape[2]
     y, z = lax.rem(me, 2), me // 2
     copies = []
@@ -189,44 +256,60 @@
             pltpu.make_async_copy(
                 res.at[lax.rem(there_z, 2), half ^ there_x, :, :, part],
                 outs[j],
-                out_sems.at[j],
+                sems.at[j],
             )
         )
     copy_all(copies)
 
 
-def project(own, other, w_own, w_other, n_tm, p_rows, head_size):
+def project_cost(own, w_own, weight):
+    rows = own.shape[0] * own.shape[1]
+    return pl.CostEstimate(
+        flops=weight * 4 * rows * w_own.shape[0] * own.shape[2],
+        bytes_accessed=2 * own.shape[2] * (rows + 2 * w_own.shape[0]),
+        transcendentals=0,
+    )
+
+
+def project_own(own, w_own, w_other, head_size):
     frames_dev, pos_dev, width = own.shape
     w_rows = w_own.shape[0]
-    g_heads = w_rows // head_size
+    return pl.pallas_call(
+        project_own_kernel,
+        out_shape=[
+            jax.ShapeDtypeStruct(
+                (2, 1, w_rows // head_size, frames_dev, pos_dev, head_size), own.dtype
+            ),
+            jax.ShapeDtypeStruct((2, w_rows, width), own.dtype),
+        ],
+        in_specs=[HBM] * 3,
+        out_specs=[VMEM] * 2,
+        scratch_shapes=[
+            pltpu.VMEM(own.shape, own.dtype),
+            pltpu.SemaphoreType.DMA((3,)),
+        ],
+        compiler_params=pltpu.CompilerParams(vmem_limit_bytes=14 * MIB),
+        cost_estimate=project_cost(own, w_own, 1),
+        name="project_own",
+    )(*(pltpu.with_memory_space_constraint(x, pltpu.HBM) for x in (own, w_own, w_other)))
+
+
+def project_other(other, w, res_own, n_tm, p_rows):
+    _, _, g_heads, frames_dev, pos_dev, head_size = res_own.shape
     shape = (g_heads, frames_dev, p_rows, head_size)
-    rows = 2 * frames_dev * pos_dev
-    return pl.pallas_call(
-        functools.partial(project_kernel, n_tm),
-        out_shape=[jax.ShapeDtypeStruct(shape, own.dtype)] * n_tm,
-        in_specs=[ANY] * 4,
+    return pl.pallas_call(
+        functools.partial(project_other_kernel, n_tm),
+        out_shape=[jax.ShapeDtypeStruct(shape, other.dtype)] * n_tm,
+        in_specs=[VMEM] * 3,
         out_specs=[ANY] * n_tm,
         scratch_shapes=[
-            pltpu.VMEM((2, frames_dev, pos_dev, width), jnp.bfloat16),
-            pltpu.VMEM((2, w_rows, width), jnp.bfloat16),
-            pltpu.VMEM((2, 2, g_heads, frames_dev, pos_dev, head_size), jnp.bfloat16),
-            pltpu.SemaphoreType.DMA((2,)),
-            pltpu.SemaphoreType.DMA((2,)),
+            pltpu.VMEM((2, 2) + res_own.shape[2:], jnp.bfloat16),
             pltpu.SemaphoreType.DMA((n_tm,)),
         ],
-        compiler_params=pltpu.CompilerParams(vmem_limit_bytes=20 * MIB),
-        cost_estimate=pl.CostEstimate(
-            flops=256 * rows * w_rows * width,
-            bytes_accessed=2 * width * (rows + 2 * w_rows),
-            transcendentals=0,
-        ),
-        name="project",
-    )(
-        pltpu.with_memory_space_constraint(own, pltpu.HBM),
-        other,
-        pltpu.with_memory_space_constraint(w_own, pltpu.HBM),
-        w_other,
-    )
+        compiler_params=pltpu.CompilerParams(vmem_limit_bytes=14 * MIB),
+        cost_estimate=project_cost(other, w[0], 16),
+        name="project_other",
+    )(other, w, res_own)
 
 
 def by_position(wide, out, frames, p_rows):
@@ -240,17 +323,23 @@
             )
 
 
-def probs_kernel(qkv, *refs):
-    by_pos, probs_ref, wide = refs[:3], refs[3], refs[4]
-    n_tm, _, frames_dev, g_heads, p_rows, head_size = qkv.shape
+def probs_kernel(ks, *refs):
+    far, near = refs[: len(ks)], refs[len(ks)]
+    by_pos, probs_ref, wide = refs[len(ks) + 1 : len(ks) + 4], refs[len(ks) + 4], refs[-1]
+    _, frames_dev, g_heads, p_rows, head_size = far[0].shape
+    n_tm = len(ks) + GROUPS
+    me = lax.axis_index("tm")
+    slots = [(me ^ k, ref) for k, ref in zip(ks, far)]
+    slots += [(me // GROUPS * GROUPS + j, near.at[j]) for j in range(GROUPS)]
     frames = n_tm * frames_dev
     slot_rows = frames_dev * p_rows
     block = probs_ref.shape[-1]
     for a in range(3):
         for h in range(g_heads):
-            for k in range(n_tm):
-                wide[a, h, k * slot_rows : (k + 1) * slot_rows] = (
-                    qkv[k, a, :, h].reshape(slot_rows, head_size).astype(jnp.float32)
+            for slot, ref in slots:
+                rows = pl.ds(pl.multiple_of(slot * slot_rows, slot_rows), slot_rows)
+                wide[a, h, rows] = (
+                    ref[a, :, h].reshape(slot_rows, head_size).astype(jnp.float32)
                 )
         by_position(wide.at[a], by_pos[a], frames, p_rows)
     row = lax.broadcasted_iota(jnp.int32, (1, block, block), 1) // frames
@@ -306,22 +395,22 @@
                 )
 
 
-def probs_of(qkv):
-    n_tm, _, frames_dev, g_heads, p_rows, head_size = qkv.shape
-    frames = n_tm * frames_dev
+def probs_of(far, near, ks):
+    _, frames_dev, g_heads, p_rows, head_size = far[0].shape
+    frames = (len(ks) + GROUPS) * frames_dev
     per = max(1, 128 // frames)
     block = per * frames
     count = g_heads * p_rows // per
     return pl.pallas_call(
-        probs_kernel,
+        functools.partial(probs_kernel, ks),
         out_shape=[jax.ShapeDtypeStruct((count, block, head_size), jnp.bfloat16)] * 3
         + [jax.ShapeDtypeStruct((count, block, block), jnp.float32)],
-        in_specs=[VMEM],
+        in_specs=[VMEM] * (len(ks) + 1),
         out_specs=[VMEM] * 4,
         scratch_shapes=[pltpu.VMEM((3, g_heads, frames * p_rows, head_size), jnp.float32)],
         compiler_params=pltpu.CompilerParams(vmem_limit_bytes=16 * MIB),
         name="probs",
-    )(qkv)
+    )(*far, near)
 
 
 def grads_of(gin, by_pos, slots, shape):
@@ -371,16 +460,24 @@
     other = swap(out_grad, 2)
     w_other = swap(out_proj, 1)
     heads_out = lambda x: jnp.transpose(x, (0, 2, 1, 3))
-    qkv = lax.all_to_all(
-        pack(heads_out(queries), heads_out(key_states), heads_out(value_states), n_tm, p_rows),
+    q_k_v = (heads_out(queries), heads_out(key_states), heads_out(value_states))
+    far = FAR
+    far_messages = list(pack_far(q_k_v, far, p_rows))
+    near_message = pack_near(q_k_v, p_rows)
+    far_messages[3], w_other = after(far_messages[3], w_other)
+    far_qkv = [send(m, k) for m, k in zip(far_messages, far)]
+    near_qkv = lax.all_to_all(
+        near_message,
         "tm",
         split_axis=0,
         concat_axis=0,
+        axis_index_groups=[[b + j for j in range(GROUPS)] for b in range(0, n_tm, GROUPS)],
         tiled=True,
     )
-    messages = project(out_grad, other, out_proj, w_other, n_tm, p_rows, head_size)
+    res_own, w_both = project_own(out_grad, out_proj, w_other, head_size)
+    messages = project_other(other, w_both, res_own, n_tm, p_rows)
     gin = [round_of(m, r) for r, m in zip(ROUNDS, messages)]
-    grads = grads_of(gin, probs_of(qkv), slots, qkv.shape[1:])
+    grads = grads_of(gin, probs_of(far_qkv, near_qkv, far), slots, far_qkv[0].shape)
     grads = [send(g, k) for g, k in zip(grads, slots)]
     return tuple(heads_out(g) for g in unpack(grads, slots, pos_dev))
 

time: 83.2 us -> 77.9 us (0.936)
  waiting for transfers between devices: 24.2 us -> 9.85 us
  starting transfers between devices: 46 us -> 52.6 us
  Pallas kernels: 12 us -> 14.4 us
    ppermute x2, waiting for transfers between devices: 10.1 us -> 0.01 us  [swap(): return lax.ppermute(x, 'fsdp', [(i, i ^ bit) for i in range(n_fsdp)])]
    ppermute x7 -> x11, starting transfers between devices: 20.7 us -> 27.2 us  [send(): lax.ppermute(message, 'tm', [(i, i ^ k) for i in range(n_tm)])]
    ppermute x8, waiting for transfers between devices: 4.2 us -> 0.61 us  [round_of(): return lax.ppermute(message, ('tm', 'fsdp'), pairs)]
    ppermute x8, starting transfers between devices: 16.4 us -> 18.8 us  [round_of(): return lax.ppermute(message, ('tm', 'fsdp'), pairs)]
    pallas_call x3 -> x5, Pallas kernels: 8.91 us -> 11.3 us  [the longest x1 3.92 us: project_own(): pl.pallas_call(project_own_kernel, out_shape=[jax.ShapeDtypeStruct((2, 1,...]
    all_to_all x1, starting transfers between devices: 5.85 us -> 3.49 us  [body_permutes(): lax.all_to_all(near_message, 'tm', split_axis=0, concat_axis=0, axis_inde...]
    ppermute x7 -> x11, waiting for transfers between devices: 9.27 us -> 9.23 us  [send(): lax.ppermute(message, 'tm', [(i, i ^ k) for i in range(n_tm)])]
  transfers between devices with their start and end apart: 18 -> 22, of which waited for: 9 -> 5; matrix products, arithmetic and copies ran while one was open for 0% -> 0% of each run, Pallas kernels for 11% -> 15%
where the time goes in v3:
time: 77.9 us; the launch traced here: 77.6 us
  starting transfers between devices  52.6 us (68%)
  Pallas kernels  14.4 us (18%)
  waiting for transfers between devices  9.85 us (13%)
    ppermute x11, starting transfers between devices, send(): lax.ppermute(message, 'tm', [(i, i ^ k) for i in range(n_tm)])  27.2 us
    ppermute x8, starting transfers between devices, round_of(): return lax.ppermute(message, ('tm', 'fsdp'), pairs)  18.8 us
    ppermute x11, waiting for transfers between devices, send(): lax.ppermute(message, 'tm', [(i, i ^ k) for i in range(n_tm)])  9.23 us
    pallas_call x1, Pallas kernels, project_own(): pl.pallas_call(project_own_kernel, out_shape=[jax.ShapeDtypeStruct((2, 1,...  3.92 us
    all_to_all x1, starting transfers between devices, body_permutes(): lax.all_to_all(near_message, 'tm', split_axis=0, concat_axis=0, axis_inde...  3.49 us
    ppermute x2, starting transfers between devices, swap(): return lax.ppermute(x, 'fsdp', [(i, i ^ bit) for i in range(n_fsdp)])  3.09 us
    pallas_call x1, Pallas kernels, pack_near(): pl.pallas_call(pack_near_kernel, out_shape=jax.ShapeDtypeStruct(shape, q_...  2.04 us
    pallas_call x1, Pallas kernels, probs_of(): pl.pallas_call(functools.partial(probs_kernel, ks), out_shape=[jax.ShapeD...  1.92 us
  transfers between devices with their start and end apart: 22, of which 5 were waited for; matrix products, arithmetic and copies ran while one was open for 0% of the time, Pallas kernels for 15%

profile of v3, /device:TPU:0, one launch (start us, length us, event | category | flops | bytes accessed | tf_op | source)
XLA Modules:
  0.0 77.6 jit_solution(18271571607313684594)
XLA Ops:
  0.6 0.5 collective-permute-start.1
  1.1 2.6 %collective-permute-start = (bf16[4,32,3072]{2,1,0:T(8,128)(2,1)}, bf16[4,32,3072]{2,1,0:T(8,128)(2,1)S(1)}, u32[]{:S(2)}, u32[]{:S(2)}) collective-permute-start(bf16[4,32,3072]{2,1,0:T(8,128)(2,1)} %own_ref.1), channel_id=1, source_target_pairs={{0,2},{1,3},{2,0},{3,1},{4,6},{5,7},{6,4},{7,5},{8,10},{9,11},{10,... | collective-permute-start | bytes 2359304 | tf_op jit(solution)/shard_map/ppermute | solution.py:445
  3.7 1.8 %pack_far.1 = (bf16[3,4,3,16,128]{4,3,2,1,0:T(8,128)(2,1)S(1)}, bf16[3,4,3,16,128]{4,3,2,1,0:T(8,128)(2,1)S(1)}, bf16[3,4,3,16,128]{4,3,2,1,0:T(8,128)(2,1)S(1)}, bf16[3,4,3,16,128]{4,3,2,1,0:T(8,128)(2,1)S(1)}) custom-call(bf16[4,12,32,128]{3,2,1,0:T(8,128)(2,1)} %bitcast.6, bf16[4,12,32,128]{3,2,1,0:T(8,128)(2,1)} %bitcast.8, bf16[4,12,32,128]{3,2,1,0:T(8,128)(2,1)} %bitcast.10), custom_call_target="tpu_custom_call" | custom-call | tf_op jit(solution)/shard_map/pack_far/pallas_call | solution.py:148
  5.5 4.6 %collective-permute-start.10 = (bf16[3,4,3,16,128]{4,3,2,1,0:T(8,128)(2,1)S(1)}, bf16[3,4,3,16,128]{4,3,2,1,0:T(8,128)(2,1)S(1)}, u32[]{:S(2)}, u32[]{:S(2)}) collective-permute-start(bf16[3,4,3,16,128]{4,3,2,1,0:T(8,128)(2,1)S(1)} %get-tuple-element.46), channel_id=1, source_target_pairs={{0,28},{4,24},{8,20},{12,16},{16,12},{20,8},{24,4},{28,0},{1,29},{... | collective-permute-start | bytes 442376 | tf_op jit(solution)/shard_map/ppermute | solution.py:448
  10.1 0.0 collective-permute-start.11
  10.1 1.9 %collective-permute-start.12 = (bf16[3,4,3,16,128]{4,3,2,1,0:T(8,128)(2,1)S(1)}, bf16[3,4,3,16,128]{4,3,2,1,0:T(8,128)(2,1)S(1)}, u32[]{:S(2)}, u32[]{:S(2)}) collective-permute-start(bf16[3,4,3,16,128]{4,3,2,1,0:T(8,128)(2,1)S(1)} %get-tuple-element.48), channel_id=1, source_target_pairs={{0,24},{4,28},{8,16},{12,20},{16,8},{20,12},{24,0},{28,4},{1,25},{... | collective-permute-start | bytes 442376 | tf_op jit(solution)/shard_map/ppermute | solution.py:448
  12.0 2.0 %pack_near.1 = bf16[4,3,4,3,16,128]{5,4,3,2,1,0:T(8,128)(2,1)} custom-call(bf16[4,12,32,128]{3,2,1,0:T(8,128)(2,1)} %bitcast.7, bf16[4,12,32,128]{3,2,1,0:T(8,128)(2,1)} %bitcast.9, bf16[4,12,32,128]{3,2,1,0:T(8,128)(2,1)} %bitcast.11), custom_call_target="tpu_custom_call" | custom-call | tf_op jit(solution)/shard_map/pack_near/pallas_call | solution.py:165
  14.1 3.5 %all-to-all-start = ((bf16[4,3,4,3,16,128]{5,4,3,2,1,0:T(8,128)(2,1)}), bf16[4,3,4,3,16,128]{5,4,3,2,1,0:T(8,128)(2,1)S(1)}, u32[]{:S(2)}, u32[]{:S(2)}) async-start(bf16[4,3,4,3,16,128]{5,4,3,2,1,0:T(8,128)(2,1)} %pack_near.1), calls=%async_computation | async-start | bytes 1179648 | tf_op jit(solution)/shard_map/all_to_all | solution.py:469
  17.6 0.0 collective-permute-done.1.w_other_ref
  17.6 2.4 %collective-permute-start.13 = (bf16[3,4,3,16,128]{4,3,2,1,0:T(8,128)(2,1)S(1)}, bf16[3,4,3,16,128]{4,3,2,1,0:T(8,128)(2,1)S(1)}, u32[]{:S(2)}, u32[]{:S(2)}) collective-permute-start(bf16[3,4,3,16,128]{4,3,2,1,0:T(8,128)(2,1)S(1)} %get-tuple-element.49), channel_id=1, source_target_pairs={{0,20},{4,16},{8,28},{12,24},{16,4},{20,0},{24,12},{28,8},{1,21},{... | collective-permute-start | bytes 442376 | tf_op jit(solution)/shard_map/ppermute | solution.py:448
  20.0 3.9 %project_own.1 = (bf16[2,1,3,4,32,128]{5,4,3,2,1,0:T(8,128)(2,1)S(1)}, bf16[2,384,3072]{2,1,0:T(8,128)(2,1)S(1)}) custom-call(bf16[4,32,3072]{2,1,0:T(8,128)(2,1)} %own_ref.1, bf16[384,3072]{1,0:T(8,128)(2,1)} %w_own_ref.1, bf16[384,3072]{1,0:T(8,128)(2,1)} %collective-permute-done.1.w_other_ref), custom_call_target="tpu_custom_call" | custom-call | flops 603979776 | bytes 5505024 | tf_op jit(solution)/shard_map/project_own/pallas_call | solution.py:277
  23.9 0.0 collective-permute-done.other_ref
  23.9 1.7 %project_other.1 = (bf16[3,4,16,128]{3,2,1,0:T(8,128)(2,1)S(1)}, bf16[3,4,16,128]{3,2,1,0:T(8,128)(2,1)S(1)}, bf16[3,4,16,128]{3,2,1,0:T(8,128)(2,1)S(1)}, bf16[...) custom-call(bf16[4,32,3072]{2,1,0:T(8,128)(2,1)S(1)} %collective-per, ...), custom_call_target="tpu_custom_call" | custom-call | flops 9663676416 | bytes 5505024 | tf_op jit(solution)/shard_map/project_other/pallas_call | solution.py:300
  25.6 0.7 collective-permute-start.2
  26.3 0.0 collective-permute-done.10.refs_0_
  26.3 2.9 %collective-permute-start.3 = (bf16[3,4,16,128]{3,2,1,0:T(8,128)(2,1)S(1)}, bf16[3,4,16,128]{3,2,1,0:T(8,128)(2,1)S(1)}, u32[]{:S(2)}, u32[]{:S(2)}) collective-permute-start(bf16[3,4,16,128]{3,2,1,0:T(8,128)(2,1)S(1)} %get-tuple-element.39), channel_id=1, source_target_pairs={{0,2},{1,3},{2,6},{3,7},{4,0},{5,1},{6,4},{7,5},{8,10},{9,11},{10,... | collective-permute-start | bytes 147464 | tf_op jit(solution)/shard_map/ppermute | solution.py:458
  29.2 0.0 collective-permute-done.11.refs_1_
  29.2 2.4 %collective-permute-start.4 = (bf16[3,4,16,128]{3,2,1,0:T(8,128)(2,1)S(1)}, bf16[3,4,16,128]{3,2,1,0:T(8,128)(2,1)S(1)}, u32[]{:S(2)}, u32[]{:S(2)}) collective-permute-start(bf16[3,4,16,128]{3,2,1,0:T(8,128)(2,1)S(1)} %get-tuple-element.40), channel_id=1, source_target_pairs={{0,16},{1,17},{2,20},{3,21},{4,18},{5,19},{6,22},{7,23},{8,24},{9,... | collective-permute-start | bytes 147464 | tf_op jit(solution)/shard_map/ppermute | solution.py:458
  31.5 0.0 collective-permute-done.12.refs_2_
  31.6 3.2 %collective-permute-start.5 = (bf16[3,4,16,128]{3,2,1,0:T(8,128)(2,1)S(1)}, bf16[3,4,16,128]{3,2,1,0:T(8,128)(2,1)S(1)}, u32[]{:S(2)}, u32[]{:S(2)}) collective-permute-start(bf16[3,4,16,128]{3,2,1,0:T(8,128)(2,1)S(1)} %get-tuple-element.41), channel_id=1, source_target_pairs={{0,18},{1,19},{2,22},{3,23},{4,16},{5,17},{6,20},{7,21},{8,26},{9,... | collective-permute-start | bytes 147464 | tf_op jit(solution)/shard_map/ppermute | solution.py:458
  34.7 0.0 collective-permute-done.2.refs_0_
  34.7 1.5 %collective-permute-start.6 = (bf16[3,4,16,128]{3,2,1,0:T(8,128)(2,1)S(1)}, bf16[3,4,16,128]{3,2,1,0:T(8,128)(2,1)S(1)}, u32[]{:S(2)}, u32[]{:S(2)}) collective-permute-start(bf16[3,4,16,128]{3,2,1,0:T(8,128)(2,1)S(1)} %get-tuple-element.42), channel_id=1, source_target_pairs={{0,24},{1,25},{2,28},{3,29},{4,26},{5,27},{6,30},{7,31},{8,16},{9,... | collective-permute-start | bytes 147464 | tf_op jit(solution)/shard_map/ppermute | solution.py:458
  36.2 0.0 collective-permute-done.3.refs_1_
  36.2 5.2 %collective-permute-start.7 = (bf16[3,4,16,128]{3,2,1,0:T(8,128)(2,1)S(1)}, bf16[3,4,16,128]{3,2,1,0:T(8,128)(2,1)S(1)}, u32[]{:S(2)}, u32[]{:S(2)}) collective-permute-start(bf16[3,4,16,128]{3,2,1,0:T(8,128)(2,1)S(1)} %get-tuple-element.43), channel_id=1, source_target_pairs={{0,26},{1,27},{2,30},{3,31},{4,24},{5,25},{6,28},{7,29},{8,18},{9,... | collective-permute-start | bytes 147464 | tf_op jit(solution)/shard_map/ppermute | solution.py:458
  41.4 0.0 collective-permute-done.4.refs_2_
  41.4 0.0 collective-permute-start.8
  41.4 0.0 collective-permute-done.13.refs_3_
  41.4 3.1 %collective-permute-start.9 = (bf16[3,4,16,128]{3,2,1,0:T(8,128)(2,1)S(1)}, bf16[3,4,16,128]{3,2,1,0:T(8,128)(2,1)S(1)}, u32[]{:S(2)}, u32[]{:S(2)}) collective-permute-start(bf16[3,4,16,128]{3,2,1,0:T(8,128)(2,1)S(1)} %get-tuple-element.45), channel_id=1, source_target_pairs={{0,10},{1,11},{2,14},{3,15},{4,8},{5,9},{6,12},{7,13},{8,2},{9,3},... | collective-permute-start | bytes 147464 | tf_op jit(solution)/shard_map/ppermute | solution.py:458
  44.5 0.0 all-to-all-done.refs_4_
  44.5 1.9 %probs.1 = (bf16[12,128,128]{2,1,0:T(8,128)(2,1)S(1)}, bf16[12,128,128]{2,1,0:T(8,128)(2,1)S(1)}, bf16[12,128,128]{2,1,0:T(8,128)(2,1)S(1)}, f32[12,128,128]{2,1,0:T(8,128)S(1)}) custom-call(bf16[3,4,3,16,128]{4,3,2,1,0:T(8,128)(2,1)S(1)} %collective-permute-done.10.refs_0_, bf16[3,4,3,16,128]{4,3,2,1,0:T(8,128)(2,1)S(1)} %collective-permute-done.11.refs_1_, ...), custom_call_target="tpu_custom_call" | custom-call | tf_op jit(solution)/shard_map/probs/pallas_call | solution.py:404
  46.4 0.0 collective-permute-done.5.refs_3_
  46.4 0.0 collective-permute-done.6.refs_4_
  46.4 0.0 collective-permute-done.7.refs_5_
  46.5 0.0 collective-permute-done.8.refs_6_
  46.5 0.6 collective-permute-done.9.refs_7_
  47.1 1.9 %grads.1 = (bf16[3,4,3,16,128]{4,3,2,1,0:T(8,128)(2,1)S(1)}, bf16[3,4,3,16,128]{4,3,2,1,0:T(8,128)(2,1)S(1)}, bf16[3,4,3,16,128]{4,3,2,1,0:T(8,128)(2,1)S(1)}, b...) custom-call(bf16[3,4,16,128]{3,2,1,0:T(8,128)(2,1)S(1)} %collective-, ...), custom_call_target="tpu_custom_call" | custom-call | tf_op jit(solution)/shard_map/grads/pallas_call | solution.py:420
  49.0 2.8 %collective-permute-start.14 = (bf16[3,4,3,16,128]{4,3,2,1,0:T(8,128)(2,1)S(1)}, bf16[3,4,3,16,128]{4,3,2,1,0:T(8,128)(2,1)S(1)}, u32[]{:S(2)}, u32[]{:S(2)}) collective-permute-start(bf16[3,4,3,16,128]{4,3,2,1,0:T(8,128)(2,1)S(1)} %get-tuple-element.54), channel_id=1, source_target_pairs={{0,28},{4,24},{8,20},{12,16},{16,12},{20,8},{24,4},{28,0},{1,29},{... | collective-permute-start | bytes 442376 | tf_op jit(solution)/shard_map/ppermute | solution.py:448
  51.7 1.1 %collective-permute-start.15 = (bf16[3,4,3,16,128]{4,3,2,1,0:T(8,128)(2,1)S(1)}, bf16[3,4,3,16,128]{4,3,2,1,0:T(8,128)(2,1)S(1)}, u32[]{:S(2)}, u32[]{:S(2)}) collective-permute-start(bf16[3,4,3,16,128]{4,3,2,1,0:T(8,128)(2,1)S(1)} %get-tuple-element.55), channel_id=1, source_target_pairs={{0,16},{4,20},{8,24},{12,28},{16,0},{20,4},{24,8},{28,12},{1,17},{... | collective-permute-start | bytes 442376 | tf_op jit(solution)/shard_map/ppermute | solution.py:448
  52.9 2.8 %collective-permute-start.16 = (bf16[3,4,3,16,128]{4,3,2,1,0:T(8,128)(2,1)S(1)}, bf16[3,4,3,16,128]{4,3,2,1,0:T(8,128)(2,1)S(1)}, u32[]{:S(2)}, u32[]{:S(2)}) collective-permute-start(bf16[3,4,3,16,128]{4,3,2,1,0:T(8,128)(2,1)S(1)} %get-tuple-element.56), channel_id=1, source_target_pairs={{0,24},{4,28},{8,16},{12,20},{16,8},{20,12},{24,0},{28,4},{1,25},{... | collective-permute-start | bytes 442376 | tf_op jit(solution)/shard_map/ppermute | solution.py:448
  55.7 0.0 collective-permute-start.17
  55.8 2.4 %collective-permute-start.18 = (bf16[3,4,3,16,128]{4,3,2,1,0:T(8,128)(2,1)S(1)}, bf16[3,4,3,16,128]{4,3,2,1,0:T(8,128)(2,1)S(1)}, u32[]{:S(2)}, u32[]{:S(2)}) collective-permute-start(bf16[3,4,3,16,128]{4,3,2,1,0:T(8,128)(2,1)S(1)} %get-tuple-element.58), channel_id=1, source_target_pairs={{0,12},{4,8},{8,4},{12,0},{16,28},{20,24},{24,20},{28,16},{1,13},{... | collective-permute-start | bytes 442376 | tf_op jit(solution)/shard_map/ppermute | solution.py:448
  58.2 0.4 collective-permute-done.14.refs_0_
  58.6 9.0 %collective-permute-start.19 = (bf16[3,4,3,16,128]{4,3,2,1,0:T(8,128)(2,1)S(1)}, bf16[3,4,3,16,128]{4,3,2,1,0:T(8,128)(2,1)S(1)}, u32[]{:S(2)}, u32[]{:S(2)}) collective-permute-start(bf16[3,4,3,16,128]{4,3,2,1,0:T(8,128)(2,1)S(1)} %get-tuple-element.59), channel_id=1, source_target_pairs={{0,8},{4,12},{8,0},{12,4},{16,24},{20,28},{24,16},{28,20},{1,9},{5... | collective-permute-start | bytes 442376 | tf_op jit(solution)/shard_map/ppermute | solution.py:448
  67.6 3.0 %collective-permute-done.15.refs_1_ = bf16[3,4,3,16,128]{4,3,2,1,0:T(8,128)(2,1)S(1)} collective-permute-done((bf16[3,4,3,16,128]{4,3,2,1,0:T(8,128)(2,1)S(1)}, bf16[3,4,3,16,128]{4,3,2,1,0:T(8,128)(2,1)S(1)}, u32[]{:S(2)}, u32[]{:S(2)}) %collective-permute-start.15) | collective-permute-done | bytes 147488 | tf_op jit(solution)/shard_map/ppermute | solution.py:448
  70.6 4.3 %collective-permute-done.17.refs_3_ = bf16[3,4,3,16,128]{4,3,2,1,0:T(8,128)(2,1)S(1)} collective-permute-done((bf16[3,4,3,16,128]{4,3,2,1,0:T(8,128)(2,1)S(1)}, bf16[3,4,3,16,128]{4,3,2,1,0:T(8,128)(2,1)S(1)}, u32[]{:S(2)}, u32[]{:S(2)}) %collective-permute-start.17) | collective-permute-done | bytes 147488 | tf_op jit(solution)/shard_map/ppermute | solution.py:448
  74.9 0.0 collective-permute-done.18.refs_4_
  74.9 1.5 %collective-permute-done.20.refs_6_ = bf16[3,4,3,16,128]{4,3,2,1,0:T(8,128)(2,1)S(1)} collective-permute-done((bf16[3,4,3,16,128]{4,3,2,1,0:T(8,128)(2,1)S(1)}, bf16[3,4,3,16,128]{4,3,2,1,0:T(8,128)(2,1)S(1)}, u32[]{:S(2)}, u32[]{:S(2)}) %collective-permute-start.20) | collective-permute-done | bytes 147488 | tf_op jit(solution)/shard_map/ppermute | solution.py:448
  76.4 1.2 %unpack.1 = (bf16[4,12,32,128]{3,2,1,0:T(8,128)(2,1)}, bf16[4,12,32,128]{3,2,1,0:T(8,128)(2,1)}, bf16[4,12,32,128]{3,2,1,0:T(8,128)(2,1)}) custom-call(bf16[3,4,3,16,128]{4,3,2,1,0:T(8,128)(2,1)S(1)} %collective-permute-done.14.refs_0_, bf16[3,4,3,16,128]{4,3,2,1,0:T(8,128)(2,1)S(1)} %collective-permute-done.15.refs_1_, ...), custom_call_target="tpu_custom_call" | custom-call | tf_op jit(solution)/shard_map/unpack/pallas_call | solution.py:200
  (3 shorter events, 0.0 us)
Async XLA Ops:
  0.6 16.9 %collective-permute-start.1 = (bf16[384,3072]{1,0:T(8,128)(2,1)}, bf16[384,3072]{1,0:T(8,128)(2,1)}, u32[]{:S(2)}, u32[]{:S(2)}) collective-permute-start(bf16[384,3072]{1,0:T(8,128)(2,1)} %w_own_ref.1), channel_id=1, source_target_pairs={{0,1},{1,0},{2,3},{3,2},{4,5},{5,4},{6,7},{7,6},{8,9},{9,8},{10,11... | collective-permute-start | bytes 7077896 | tf_op jit(solution)/shard_map/ppermute | solution.py:445
  1.1 22.8 %collective-permute-start = (bf16[4,32,3072]{2,1,0:T(8,128)(2,1)}, bf16[4,32,3072]{2,1,0:T(8,128)(2,1)S(1)}, u32[]{:S(2)}, u32[]{:S(2)}) collective-permute-start(bf16[4,32,3072]{2,1,0:T(8,128)(2,1)} %own_ref.1), channel_id=1, source_target_pairs={{0,2},{1,3},{2,0},{3,1},{4,6},{5,7},{6,4},{7,5},{8,10},{9,11},{10,... | collective-permute-start | bytes 2359304 | tf_op jit(solution)/shard_map/ppermute | solution.py:445
  5.5 20.8 %collective-permute-start.10 = (bf16[3,4,3,16,128]{4,3,2,1,0:T(8,128)(2,1)S(1)}, bf16[3,4,3,16,128]{4,3,2,1,0:T(8,128)(2,1)S(1)}, u32[]{:S(2)}, u32[]{:S(2)}) collective-permute-start(bf16[3,4,3,16,128]{4,3,2,1,0:T(8,128)(2,1)S(1)} %get-tuple-element.46), channel_id=1, source_target_pairs={{0,28},{4,24},{8,20},{12,16},{16,12},{20,8},{24,4},{28,0},{1,29},{... | collective-permute-start | bytes 442376 | tf_op jit(solution)/shard_map/ppermute | solution.py:448
  10.1 19.1 %collective-permute-start.11 = (bf16[3,4,3,16,128]{4,3,2,1,0:T(8,128)(2,1)S(1)}, bf16[3,4,3,16,128]{4,3,2,1,0:T(8,128)(2,1)S(1)}, u32[]{:S(2)}, u32[]{:S(2)}) collective-permute-start(bf16[3,4,3,16,128]{4,3,2,1,0:T(8,128)(2,1)S(1)} %get-tuple-element.47), channel_id=1, source_target_pairs={{0,16},{4,20},{8,24},{12,28},{16,0},{20,4},{24,8},{28,12},{1,17},{... | collective-permute-start | bytes 442376 | tf_op jit(solution)/shard_map/ppermute | solution.py:448
  10.1 21.4 %collective-permute-start.12 = (bf16[3,4,3,16,128]{4,3,2,1,0:T(8,128)(2,1)S(1)}, bf16[3,4,3,16,128]{4,3,2,1,0:T(8,128)(2,1)S(1)}, u32[]{:S(2)}, u32[]{:S(2)}) collective-permute-start(bf16[3,4,3,16,128]{4,3,2,1,0:T(8,128)(2,1)S(1)} %get-tuple-element.48), channel_id=1, source_target_pairs={{0,24},{4,28},{8,16},{12,20},{16,8},{20,12},{24,0},{28,4},{1,25},{... | collective-permute-start | bytes 442376 | tf_op jit(solution)/shard_map/ppermute | solution.py:448
  14.1 30.4 %all-to-all-start = ((bf16[4,3,4,3,16,128]{5,4,3,2,1,0:T(8,128)(2,1)}), bf16[4,3,4,3,16,128]{5,4,3,2,1,0:T(8,128)(2,1)S(1)}, u32[]{:S(2)}, u32[]{:S(2)}) async-start(bf16[4,3,4,3,16,128]{5,4,3,2,1,0:T(8,128)(2,1)} %pack_near.1), calls=%async_computation | async-start | bytes 1179648 | tf_op jit(solution)/shard_map/all_to_all | solution.py:469
  17.6 23.9 %collective-permute-start.13 = (bf16[3,4,3,16,128]{4,3,2,1,0:T(8,128)(2,1)S(1)}, bf16[3,4,3,16,128]{4,3,2,1,0:T(8,128)(2,1)S(1)}, u32[]{:S(2)}, u32[]{:S(2)}) collective-permute-start(bf16[3,4,3,16,128]{4,3,2,1,0:T(8,128)(2,1)S(1)} %get-tuple-element.49), channel_id=1, source_target_pairs={{0,20},{4,16},{8,28},{12,24},{16,4},{20,0},{24,12},{28,8},{1,21},{... | collective-permute-start | bytes 442376 | tf_op jit(solution)/shard_map/ppermute | solution.py:448
  25.6 9.1 %collective-permute-start.2 = (bf16[3,4,16,128]{3,2,1,0:T(8,128)(2,1)S(1)}, bf16[3,4,16,128]{3,2,1,0:T(8,128)(2,1)S(1)}, u32[]{:S(2)}, u32[]{:S(2)}) collective-permute-start(bf16[3,4,16,128]{3,2,1,0:T(8,128)(2,1)S(1)} %get-tuple-element.38), channel_id=1, source_target_pairs={{0,0},{1,1},{2,4},{3,5},{4,2},{5,3},{6,6},{7,7},{8,8},{9,9},{10,12... | collective-permute-start | bytes 147464 | tf_op jit(solution)/shard_map/ppermute | solution.py:458
  26.3 9.9 %collective-permute-start.3 = (bf16[3,4,16,128]{3,2,1,0:T(8,128)(2,1)S(1)}, bf16[3,4,16,128]{3,2,1,0:T(8,128)(2,1)S(1)}, u32[]{:S(2)}, u32[]{:S(2)}) collective-permute-start(bf16[3,4,16,128]{3,2,1,0:T(8,128)(2,1)S(1)} %get-tuple-element.39), channel_id=1, source_target_pairs={{0,2},{1,3},{2,6},{3,7},{4,0},{5,1},{6,4},{7,5},{8,10},{9,11},{10,... | collective-permute-start | bytes 147464 | tf_op jit(solution)/shard_map/ppermute | solution.py:458
  29.2 12.3 %collective-permute-start.4 = (bf16[3,4,16,128]{3,2,1,0:T(8,128)(2,1)S(1)}, bf16[3,4,16,128]{3,2,1,0:T(8,128)(2,1)S(1)}, u32[]{:S(2)}, u32[]{:S(2)}) collective-permute-start(bf16[3,4,16,128]{3,2,1,0:T(8,128)(2,1)S(1)} %get-tuple-element.40), channel_id=1, source_target_pairs={{0,16},{1,17},{2,20},{3,21},{4,18},{5,19},{6,22},{7,23},{8,24},{9,... | collective-permute-start | bytes 147464 | tf_op jit(solution)/shard_map/ppermute | solution.py:458
  31.6 14.9 %collective-permute-start.5 = (bf16[3,4,16,128]{3,2,1,0:T(8,128)(2,1)S(1)}, bf16[3,4,16,128]{3,2,1,0:T(8,128)(2,1)S(1)}, u32[]{:S(2)}, u32[]{:S(2)}) collective-permute-start(bf16[3,4,16,128]{3,2,1,0:T(8,128)(2,1)S(1)} %get-tuple-element.41), channel_id=1, source_target_pairs={{0,18},{1,19},{2,22},{3,23},{4,16},{5,17},{6,20},{7,21},{8,26},{9,... | collective-permute-start | bytes 147464 | tf_op jit(solution)/shard_map/ppermute | solution.py:458
  34.7 11.7 %collective-permute-start.6 = (bf16[3,4,16,128]{3,2,1,0:T(8,128)(2,1)S(1)}, bf16[3,4,16,128]{3,2,1,0:T(8,128)(2,1)S(1)}, u32[]{:S(2)}, u32[]{:S(2)}) collective-permute-start(bf16[3,4,16,128]{3,2,1,0:T(8,128)(2,1)S(1)} %get-tuple-element.42), channel_id=1, source_target_pairs={{0,24},{1,25},{2,28},{3,29},{4,26},{5,27},{6,30},{7,31},{8,16},{9,... | collective-permute-start | bytes 147464 | tf_op jit(solution)/shard_map/ppermute | solution.py:458
  36.2 10.2 %collective-permute-start.7 = (bf16[3,4,16,128]{3,2,1,0:T(8,128)(2,1)S(1)}, bf16[3,4,16,128]{3,2,1,0:T(8,128)(2,1)S(1)}, u32[]{:S(2)}, u32[]{:S(2)}) collective-permute-start(bf16[3,4,16,128]{3,2,1,0:T(8,128)(2,1)S(1)} %get-tuple-element.43), channel_id=1, source_target_pairs={{0,26},{1,27},{2,30},{3,31},{4,24},{5,25},{6,28},{7,29},{8,18},{9,... | collective-permute-start | bytes 147464 | tf_op jit(solution)/shard_map/ppermute | solution.py:458
  41.4 5.0 %collective-permute-start.8 = (bf16[3,4,16,128]{3,2,1,0:T(8,128)(2,1)S(1)}, bf16[3,4,16,128]{3,2,1,0:T(8,128)(2,1)S(1)}, u32[]{:S(2)}, u32[]{:S(2)}) collective-permute-start(bf16[3,4,16,128]{3,2,1,0:T(8,128)(2,1)S(1)} %get-tuple-element.44), channel_id=1, source_target_pairs={{0,8},{1,9},{2,12},{3,13},{4,10},{5,11},{6,14},{7,15},{8,0},{9,1},... | collective-permute-start | bytes 147464 | tf_op jit(solution)/shard_map/ppermute | solution.py:458
  41.4 5.6 %collective-permute-start.9 = (bf16[3,4,16,128]{3,2,1,0:T(8,128)(2,1)S(1)}, bf16[3,4,16,128]{3,2,1,0:T(8,128)(2,1)S(1)}, u32[]{:S(2)}, u32[]{:S(2)}) collective-permute-start(bf16[3,4,16,128]{3,2,1,0:T(8,128)(2,1)S(1)} %get-tuple-element.45), channel_id=1, source_target_pairs={{0,10},{1,11},{2,14},{3,15},{4,8},{5,9},{6,12},{7,13},{8,2},{9,3},... | collective-permute-start | bytes 147464 | tf_op jit(solution)/shard_map/ppermute | solution.py:458
  49.0 9.6 %collective-permute-start.14 = (bf16[3,4,3,16,128]{4,3,2,1,0:T(8,128)(2,1)S(1)}, bf16[3,4,3,16,128]{4,3,2,1,0:T(8,128)(2,1)S(1)}, u32[]{:S(2)}, u32[]{:S(2)}) collective-permute-start(bf16[3,4,3,16,128]{4,3,2,1,0:T(8,128)(2,1)S(1)} %get-tuple-element.54), channel_id=1, source_target_pairs={{0,28},{4,24},{8,20},{12,16},{16,12},{20,8},{24,4},{28,0},{1,29},{... | collective-permute-start | bytes 442376 | tf_op jit(solution)/shard_map/ppermute | solution.py:448
  51.7 18.8 %collective-permute-start.15 = (bf16[3,4,3,16,128]{4,3,2,1,0:T(8,128)(2,1)S(1)}, bf16[3,4,3,16,128]{4,3,2,1,0:T(8,128)(2,1)S(1)}, u32[]{:S(2)}, u32[]{:S(2)}) collective-permute-start(bf16[3,4,3,16,128]{4,3,2,1,0:T(8,128)(2,1)S(1)} %get-tuple-element.55), channel_id=1, source_target_pairs={{0,16},{4,20},{8,24},{12,28},{16,0},{20,4},{24,8},{28,12},{1,17},{... | collective-permute-start | bytes 442376 | tf_op jit(solution)/shard_map/ppermute | solution.py:448
  52.9 17.7 %collective-permute-start.16 = (bf16[3,4,3,16,128]{4,3,2,1,0:T(8,128)(2,1)S(1)}, bf16[3,4,3,16,128]{4,3,2,1,0:T(8,128)(2,1)S(1)}, u32[]{:S(2)}, u32[]{:S(2)}) collective-permute-start(bf16[3,4,3,16,128]{4,3,2,1,0:T(8,128)(2,1)S(1)} %get-tuple-element.56), channel_id=1, source_target_pairs={{0,24},{4,28},{8,16},{12,20},{16,8},{20,12},{24,0},{28,4},{1,25},{... | collective-permute-start | bytes 442376 | tf_op jit(solution)/shard_map/ppermute | solution.py:448
  55.7 19.2 %collective-permute-start.17 = (bf16[3,4,3,16,128]{4,3,2,1,0:T(8,128)(2,1)S(1)}, bf16[3,4,3,16,128]{4,3,2,1,0:T(8,128)(2,1)S(1)}, u32[]{:S(2)}, u32[]{:S(2)}) collective-permute-start(bf16[3,4,3,16,128]{4,3,2,1,0:T(8,128)(2,1)S(1)} %get-tuple-element.57), channel_id=1, source_target_pairs={{0,20},{4,16},{8,28},{12,24},{16,4},{20,0},{24,12},{28,8},{1,21},{... | collective-permute-start | bytes 442376 | tf_op jit(solution)/shard_map/ppermute | solution.py:448
  55.8 19.1 %collective-permute-start.18 = (bf16[3,4,3,16,128]{4,3,2,1,0:T(8,128)(2,1)S(1)}, bf16[3,4,3,16,128]{4,3,2,1,0:T(8,128)(2,1)S(1)}, u32[]{:S(2)}, u32[]{:S(2)}) collective-permute-start(bf16[3,4,3,16,128]{4,3,2,1,0:T(8,128)(2,1)S(1)} %get-tuple-element.58), channel_id=1, source_target_pairs={{0,12},{4,8},{8,4},{12,0},{16,28},{20,24},{24,20},{28,16},{1,13},{... | collective-permute-start | bytes 442376 | tf_op jit(solution)/shard_map/ppermute | solution.py:448
  58.6 16.3 %collective-permute-start.19 = (bf16[3,4,3,16,128]{4,3,2,1,0:T(8,128)(2,1)S(1)}, bf16[3,4,3,16,128]{4,3,2,1,0:T(8,128)(2,1)S(1)}, u32[]{:S(2)}, u32[]{:S(2)}) collective-permute-start(bf16[3,4,3,16,128]{4,3,2,1,0:T(8,128)(2,1)S(1)} %get-tuple-element.59), channel_id=1, source_target_pairs={{0,8},{4,12},{8,0},{12,4},{16,24},{20,28},{24,16},{28,20},{1,9},{5... | collective-permute-start | bytes 442376 | tf_op jit(solution)/shard_map/ppermute | solution.py:448
  70.6 5.8 %collective-permute-start.20 = (bf16[3,4,3,16,128]{4,3,2,1,0:T(8,128)(2,1)S(1)}, bf16[3,4,3,16,128]{4,3,2,1,0:T(8,128)(2,1)S(1)}, u32[]{:S(2)}, u32[]{:S(2)}) collective-permute-start(bf16[3,4,3,16,128]{4,3,2,1,0:T(8,128)(2,1)S(1)} %get-tuple-element.60), channel_id=1, source_target_pairs={{0,4},{4,0},{8,12},{12,8},{16,20},{20,16},{24,28},{28,24},{1,5},{5... | collective-permute-start | bytes 442376 | tf_op jit(solution)/shard_map/ppermute | solution.py:448

commit v4 on v3

--- a/solution.py
+++ b/solution.py
@@ -11,9 +11,10 @@
 HBM = pl.BlockSpec(memory_space=pltpu.HBM)
 VMEM = pl.BlockSpec(memory_space=pltpu.VMEM)
 MIB = 1024 * 1024
-SLOTS = (7, 4, 6, 5, 3, 2, 1, 0)
-FAR = (7, 4, 6, 5)
-ROUNDS = (0, 1, 4, 5, 6, 7, 2, 3)
+SLOTS = (6, 7, 4, 5, 3, 2, 1, 0)
+LATE = (4, 5)
+FAR = (7, 6, 4, 5)
+ROUNDS = (0, 1, 6, 7, 4, 5, 2, 3)
 GROUPS = 4
 
 
@@ -176,36 +177,36 @@
     )(*(pltpu.with_memory_space_constraint(x, pltpu.HBM) for x in q_k_v))
 
 
-def unpack_kernel(slots, *refs):
-    n_tm = len(slots)
-    grads, outs, sems = refs[:n_tm], refs[n_tm : n_tm + 3], refs[n_tm + 3]
+def unpack_kernel(ks, *refs):
+    grads, outs, sems = refs[: len(ks)], refs[-4:-1], refs[-1]
     me = lax.axis_index("tm")
     _, _, g_heads, p_rows, _ = grads[0].shape
     copies = []
-    for j, k in enumerate(slots):
+    for j, k in enumerate(ks):
         there = me ^ k
         heads = pl.ds(group_of(there) * g_heads, g_heads)
         rows = pl.ds(pl.multiple_of(part_of(there) * p_rows, p_rows), p_rows)
         for a, ref in enumerate(outs):
             copies.append(
-                pltpu.make_async_copy(grads[j].at[a], ref.at[:, heads, rows], sems.at[3 * j + a])
+                pltpu.make_async_copy(grads[j].at[a], ref.at[:, heads, rows], sems.at[j, a])
             )
     copy_all(copies)
 
 
-def unpack(grads, slots, pos_dev):
-    n_tm = len(grads)
+def unpack(grads, ks, pos_dev, before=()):
     _, frames_dev, g_heads, _, head_size = grads[0].shape
     shape = (frames_dev, g_heads * GROUPS, pos_dev, head_size)
-    return pl.pallas_call(
-        functools.partial(unpack_kernel, slots),
+    n = len(ks)
+    return pl.pallas_call(
+        functools.partial(unpack_kernel, ks),
         out_shape=[jax.ShapeDtypeStruct(shape, grads[0].dtype)] * 3,
-        in_specs=[ANY] * n_tm,
+        in_specs=[ANY] * n + [HBM] * len(before),
         out_specs=[HBM] * 3,
-        scratch_shapes=[pltpu.SemaphoreType.DMA((3 * n_tm,))],
+        scratch_shapes=[pltpu.SemaphoreType.DMA((n, 3))],
+        input_output_aliases={n + a: a for a in range(len(before))},
         compiler_params=pltpu.CompilerParams(vmem_limit_bytes=1 * MIB),
         name="unpack",
-    )(*grads)
+    )(*grads, *before)
 
 
 def project_into(res, at, w, out):
@@ -479,7 +480,11 @@
     gin = [round_of(m, r) for r, m in zip(ROUNDS, messages)]
     grads = grads_of(gin, probs_of(far_qkv, near_qkv, far), slots, far_qkv[0].shape)
     grads = [send(g, k) for g, k in zip(grads, slots)]
-    return tuple(heads_out(g) for g in unpack(grads, slots, pos_dev))
+    grads = dict(zip(slots, grads))
+    early = tuple(k for k in slots if k not in LATE)
+    outs = unpack([grads[k] for k in early], early, pos_dev)
+    outs = unpack([grads[k] for k in LATE], LATE, pos_dev, outs)
+    return tuple(heads_out(g) for g in outs)
 
 
 def solution(mesh):

time: 77.9 us -> 74 us (0.950)
  waiting for transfers between devices: 9.85 us -> 7.3 us
  starting transfers between devices: 52.6 us -> 50.2 us
    ppermute x11, waiting for transfers between devices: 9.23 us -> 4.74 us  [send(): lax.ppermute(message, 'tm', [(i, i ^ k) for i in range(n_tm)])]
    ppermute x8, starting transfers between devices: 18.8 us -> 15.7 us  [round_of(): return lax.ppermute(message, ('tm', 'fsdp'), pairs)]
    ppermute x8, waiting for transfers between devices: 0.61 us -> 2.54 us  [round_of(): return lax.ppermute(message, ('tm', 'fsdp'), pairs)]
    all_to_all x1, starting transfers between devices: 3.49 us -> 4.66 us  [body_permutes(): lax.all_to_all(near_message, 'tm', split_axis=0, concat_axis=0, axis_inde...]
    pallas_call x1 -> x2, Pallas kernels: 1.2 us -> 1.83 us  [unpack(): pl.pallas_call(functools.partial(unpack_kernel, ks), out_shape=[jax.Shape...]
  transfers between devices with their start and end apart: 22 -> 22, of which waited for: 5 -> 6; matrix products, arithmetic and copies ran while one was open for 0% -> 0% of each run, Pallas kernels for 15% -> 17%
where the time goes in v4:
time: 74 us; the launch traced here: 73.2 us
  starting transfers between devices  50.2 us (68%)
  Pallas kernels  15 us (20%)
  waiting for transfers between devices  7.3 us (10%)
  between operations  0.76 us (1%)
    ppermute x11, starting transfers between devices, send(): lax.ppermute(message, 'tm', [(i, i ^ k) for i in range(n_tm)])  26.7 us
    ppermute x8, starting transfers between devices, round_of(): return lax.ppermute(message, ('tm', 'fsdp'), pairs)  15.7 us
    ppermute x11, waiting for transfers between devices, send(): lax.ppermute(message, 'tm', [(i, i ^ k) for i in range(n_tm)])  4.74 us
    all_to_all x1, starting transfers between devices, body_permutes(): lax.all_to_all(near_message, 'tm', split_axis=0, concat_axis=0, axis_inde...  4.66 us
    pallas_call x1, Pallas kernels, project_own(): pl.pallas_call(project_own_kernel, out_shape=[jax.ShapeDtypeStruct((2, 1,...  3.92 us
    ppermute x2, starting transfers between devices, swap(): return lax.ppermute(x, 'fsdp', [(i, i ^ bit) for i in range(n_fsdp)])  3.09 us
    ppermute x8, waiting for transfers between devices, round_of(): return lax.ppermute(message, ('tm', 'fsdp'), pairs)  2.54 us
    pallas_call x1, Pallas kernels, pack_near(): pl.pallas_call(pack_near_kernel, out_shape=jax.ShapeDtypeStruct(shape, q_...  2.04 us
  transfers between devices with their start and end apart: 22, of which 6 were waited for; matrix products, arithmetic and copies ran while one was open for 0% of the time, Pallas kernels for 17%

profile of v4, /device:TPU:0, one launch (start us, length us, event | category | flops | bytes accessed | tf_op | source)
XLA Modules:
  0.0 73.2 jit_solution(902570367195747789)
XLA Ops:
  0.6 0.5 collective-permute-start.1
  1.1 2.6 %collective-permute-start = (bf16[4,32,3072]{2,1,0:T(8,128)(2,1)}, bf16[4,32,3072]{2,1,0:T(8,128)(2,1)S(1)}, u32[]{:S(2)}, u32[]{:S(2)}) collective-permute-start(bf16[4,32,3072]{2,1,0:T(8,128)(2,1)} %own_ref.1), channel_id=1, source_target_pairs={{0,2},{1,3},{2,0},{3,1},{4,6},{5,7},{6,4},{7,5},{8,10},{9,11},{10,... | collective-permute-start | bytes 2359304 | tf_op jit(solution)/shard_map/ppermute | solution.py:446
  3.7 1.8 %pack_far.1 = (bf16[3,4,3,16,128]{4,3,2,1,0:T(8,128)(2,1)S(1)}, bf16[3,4,3,16,128]{4,3,2,1,0:T(8,128)(2,1)S(1)}, bf16[3,4,3,16,128]{4,3,2,1,0:T(8,128)(2,1)S(1)}, bf16[3,4,3,16,128]{4,3,2,1,0:T(8,128)(2,1)S(1)}) custom-call(bf16[4,12,32,128]{3,2,1,0:T(8,128)(2,1)} %bitcast.6, bf16[4,12,32,128]{3,2,1,0:T(8,128)(2,1)} %bitcast.8, bf16[4,12,32,128]{3,2,1,0:T(8,128)(2,1)} %bitcast.10), custom_call_target="tpu_custom_call" | custom-call | tf_op jit(solution)/shard_map/pack_far/pallas_call | solution.py:149
  5.5 4.6 %collective-permute-start.10 = (bf16[3,4,3,16,128]{4,3,2,1,0:T(8,128)(2,1)S(1)}, bf16[3,4,3,16,128]{4,3,2,1,0:T(8,128)(2,1)S(1)}, u32[]{:S(2)}, u32[]{:S(2)}) collective-permute-start(bf16[3,4,3,16,128]{4,3,2,1,0:T(8,128)(2,1)S(1)} %get-tuple-element.49), channel_id=1, source_target_pairs={{0,28},{4,24},{8,20},{12,16},{16,12},{20,8},{24,4},{28,0},{1,29},{... | collective-permute-start | bytes 442376 | tf_op jit(solution)/shard_map/ppermute | solution.py:449
  10.1 0.2 collective-permute-start.11
  10.3 0.8 %collective-permute-start.12 = (bf16[3,4,3,16,128]{4,3,2,1,0:T(8,128)(2,1)S(1)}, bf16[3,4,3,16,128]{4,3,2,1,0:T(8,128)(2,1)S(1)}, u32[]{:S(2)}, u32[]{:S(2)}) collective-permute-start(bf16[3,4,3,16,128]{4,3,2,1,0:T(8,128)(2,1)S(1)} %get-tuple-element.51), channel_id=1, source_target_pairs={{0,16},{4,20},{8,24},{12,28},{16,0},{20,4},{24,8},{28,12},{1,17},{... | collective-permute-start | bytes 442376 | tf_op jit(solution)/shard_map/ppermute | solution.py:449
  11.1 2.0 %pack_near.1 = bf16[4,3,4,3,16,128]{5,4,3,2,1,0:T(8,128)(2,1)} custom-call(bf16[4,12,32,128]{3,2,1,0:T(8,128)(2,1)} %bitcast.7, bf16[4,12,32,128]{3,2,1,0:T(8,128)(2,1)} %bitcast.9, bf16[4,12,32,128]{3,2,1,0:T(8,128)(2,1)} %bitcast.11), custom_call_target="tpu_custom_call" | custom-call | tf_op jit(solution)/shard_map/pack_near/pallas_call | solution.py:166
  13.2 4.7 %all-to-all-start = ((bf16[4,3,4,3,16,128]{5,4,3,2,1,0:T(8,128)(2,1)}), bf16[4,3,4,3,16,128]{5,4,3,2,1,0:T(8,128)(2,1)S(1)}, u32[]{:S(2)}, u32[]{:S(2)}) async-start(bf16[4,3,4,3,16,128]{5,4,3,2,1,0:T(8,128)(2,1)} %pack_near.1), calls=%async_computation | async-start | bytes 1179648 | tf_op jit(solution)/shard_map/all_to_all | solution.py:470
  17.8 0.0 collective-permute-done.1.w_other_ref
  17.8 2.4 %collective-permute-start.13 = (bf16[3,4,3,16,128]{4,3,2,1,0:T(8,128)(2,1)S(1)}, bf16[3,4,3,16,128]{4,3,2,1,0:T(8,128)(2,1)S(1)}, u32[]{:S(2)}, u32[]{:S(2)}) collective-permute-start(bf16[3,4,3,16,128]{4,3,2,1,0:T(8,128)(2,1)S(1)} %get-tuple-element.52), channel_id=1, source_target_pairs={{0,20},{4,16},{8,28},{12,24},{16,4},{20,0},{24,12},{28,8},{1,21},{... | collective-permute-start | bytes 442376 | tf_op jit(solution)/shard_map/ppermute | solution.py:449
  20.2 3.9 %project_own.1 = (bf16[2,1,3,4,32,128]{5,4,3,2,1,0:T(8,128)(2,1)S(1)}, bf16[2,384,3072]{2,1,0:T(8,128)(2,1)S(1)}) custom-call(bf16[4,32,3072]{2,1,0:T(8,128)(2,1)} %own_ref.1, bf16[384,3072]{1,0:T(8,128)(2,1)} %w_own_ref.1, bf16[384,3072]{1,0:T(8,128)(2,1)} %collective-permute-done.1.w_other_ref), custom_call_target="tpu_custom_call" | custom-call | flops 603979776 | bytes 5505024 | tf_op jit(solution)/shard_map/project_own/pallas_call | solution.py:278
  24.2 0.0 collective-permute-done.other_ref
  24.2 1.7 %project_other.1 = (bf16[3,4,16,128]{3,2,1,0:T(8,128)(2,1)S(1)}, bf16[3,4,16,128]{3,2,1,0:T(8,128)(2,1)S(1)}, bf16[3,4,16,128]{3,2,1,0:T(8,128)(2,1)S(1)}, bf16[...) custom-call(bf16[4,32,3072]{2,1,0:T(8,128)(2,1)S(1)} %collective-per, ...), custom_call_target="tpu_custom_call" | custom-call | flops 9663676416 | bytes 5505024 | tf_op jit(solution)/shard_map/project_other/pallas_call | solution.py:301
  25.8 0.7 collective-permute-start.2
  26.5 0.0 collective-permute-done.10.refs_0_
  26.5 2.9 %collective-permute-start.3 = (bf16[3,4,16,128]{3,2,1,0:T(8,128)(2,1)S(1)}, bf16[3,4,16,128]{3,2,1,0:T(8,128)(2,1)S(1)}, u32[]{:S(2)}, u32[]{:S(2)}) collective-permute-start(bf16[3,4,16,128]{3,2,1,0:T(8,128)(2,1)S(1)} %get-tuple-element.42), channel_id=1, source_target_pairs={{0,2},{1,3},{2,6},{3,7},{4,0},{5,1},{6,4},{7,5},{8,10},{9,11},{10,... | collective-permute-start | bytes 147464 | tf_op jit(solution)/shard_map/ppermute | solution.py:459
  29.4 0.0 collective-permute-done.11.refs_1_
  29.4 3.6 %collective-permute-start.4 = (bf16[3,4,16,128]{3,2,1,0:T(8,128)(2,1)S(1)}, bf16[3,4,16,128]{3,2,1,0:T(8,128)(2,1)S(1)}, u32[]{:S(2)}, u32[]{:S(2)}) collective-permute-start(bf16[3,4,16,128]{3,2,1,0:T(8,128)(2,1)S(1)} %get-tuple-element.43), channel_id=1, source_target_pairs={{0,24},{1,25},{2,28},{3,29},{4,26},{5,27},{6,30},{7,31},{8,16},{9,... | collective-permute-start | bytes 147464 | tf_op jit(solution)/shard_map/ppermute | solution.py:459
  33.0 0.8 %collective-permute-done.12.refs_2_ = bf16[3,4,3,16,128]{4,3,2,1,0:T(8,128)(2,1)S(1)} collective-permute-done((bf16[3,4,3,16,128]{4,3,2,1,0:T(8,128)(2,1)S(1)}, bf16[3,4,3,16,128]{4,3,2,1,0:T(8,128)(2,1)S(1)}, u32[]{:S(2)}, u32[]{:S(2)}) %collective-permute-start.12) | collective-permute-done | bytes 147488 | tf_op jit(solution)/shard_map/ppermute | solution.py:449
  33.8 1.8 %collective-permute-start.5 = (bf16[3,4,16,128]{3,2,1,0:T(8,128)(2,1)S(1)}, bf16[3,4,16,128]{3,2,1,0:T(8,128)(2,1)S(1)}, u32[]{:S(2)}, u32[]{:S(2)}) collective-permute-start(bf16[3,4,16,128]{3,2,1,0:T(8,128)(2,1)S(1)} %get-tuple-element.44), channel_id=1, source_target_pairs={{0,26},{1,27},{2,30},{3,31},{4,24},{5,25},{6,28},{7,29},{8,18},{9,... | collective-permute-start | bytes 147464 | tf_op jit(solution)/shard_map/ppermute | solution.py:459
  35.6 0.0 collective-permute-done.2.refs_0_
  35.6 0.0 collective-permute-start.6
  35.6 0.0 collective-permute-done.3.refs_1_
  35.6 4.7 %collective-permute-start.7 = (bf16[3,4,16,128]{3,2,1,0:T(8,128)(2,1)S(1)}, bf16[3,4,16,128]{3,2,1,0:T(8,128)(2,1)S(1)}, u32[]{:S(2)}, u32[]{:S(2)}) collective-permute-start(bf16[3,4,16,128]{3,2,1,0:T(8,128)(2,1)S(1)} %get-tuple-element.46), channel_id=1, source_target_pairs={{0,18},{1,19},{2,22},{3,23},{4,16},{5,17},{6,20},{7,21},{8,26},{9,... | collective-permute-start | bytes 147464 | tf_op jit(solution)/shard_map/ppermute | solution.py:459
  40.4 0.0 collective-permute-done.4.refs_2_
  40.4 1.5 %collective-permute-start.8 = (bf16[3,4,16,128]{3,2,1,0:T(8,128)(2,1)S(1)}, bf16[3,4,16,128]{3,2,1,0:T(8,128)(2,1)S(1)}, u32[]{:S(2)}, u32[]{:S(2)}) collective-permute-start(bf16[3,4,16,128]{3,2,1,0:T(8,128)(2,1)S(1)} %get-tuple-element.47), channel_id=1, source_target_pairs={{0,8},{1,9},{2,12},{3,13},{4,10},{5,11},{6,14},{7,15},{8,0},{9,1},... | collective-permute-start | bytes 147464 | tf_op jit(solution)/shard_map/ppermute | solution.py:459
  41.9 0.0 collective-permute-done.13.refs_3_
  41.9 0.5 collective-permute-start.9
  42.4 1.9 %probs.1 = (bf16[12,128,128]{2,1,0:T(8,128)(2,1)S(1)}, bf16[12,128,128]{2,1,0:T(8,128)(2,1)S(1)}, bf16[12,128,128]{2,1,0:T(8,128)(2,1)S(1)}, f32[12,128,128]{2,1,0:T(8,128)S(1)}) custom-call(bf16[3,4,3,16,128]{4,3,2,1,0:T(8,128)(2,1)S(1)} %collective-permute-done.10.refs_0_, bf16[3,4,3,16,128]{4,3,2,1,0:T(8,128)(2,1)S(1)} %collective-permute-done.11.refs_1_, ...), custom_call_target="tpu_custom_call" | custom-call | tf_op jit(solution)/shard_map/probs/pallas_call | solution.py:405
  44.3 0.0 collective-permute-done.6.refs_4_
  44.3 0.0 collective-permute-done.7.refs_5_
  44.3 0.4 collective-permute-done.8.refs_6_
  44.8 2.1 %collective-permute-done.9.refs_7_ = bf16[3,4,16,128]{3,2,1,0:T(8,128)(2,1)S(1)} collective-permute-done((bf16[3,4,16,128]{3,2,1,0:T(8,128)(2,1)S(1)}, bf16[3,4,16,128]{3,2,1,0:T(8,128)(2,1)S(1)}, u32[]{:S(2)}, u32[]{:S(2)}) %collective-permute-start.9) | collective-permute-done | bytes 49184 | tf_op jit(solution)/shard_map/ppermute | solution.py:459
  46.9 1.9 %grads.1 = (bf16[3,4,3,16,128]{4,3,2,1,0:T(8,128)(2,1)S(1)}, bf16[3,4,3,16,128]{4,3,2,1,0:T(8,128)(2,1)S(1)}, bf16[3,4,3,16,128]{4,3,2,1,0:T(8,128)(2,1)S(1)}, b...) custom-call(bf16[3,4,16,128]{3,2,1,0:T(8,128)(2,1)S(1)} %collective-, ...), custom_call_target="tpu_custom_call" | custom-call | tf_op jit(solution)/shard_map/grads/pallas_call | solution.py:421
  48.8 2.3 %collective-permute-start.16 = (bf16[3,4,3,16,128]{4,3,2,1,0:T(8,128)(2,1)S(1)}, bf16[3,4,3,16,128]{4,3,2,1,0:T(8,128)(2,1)S(1)}, u32[]{:S(2)}, u32[]{:S(2)}) collective-permute-start(bf16[3,4,3,16,128]{4,3,2,1,0:T(8,128)(2,1)S(1)} %get-tuple-element.59), channel_id=1, source_target_pairs={{0,24},{4,28},{8,16},{12,20},{16,8},{20,12},{24,0},{28,4},{1,25},{... | collective-permute-start | bytes 442376 | tf_op jit(solution)/shard_map/ppermute | solution.py:449
  51.1 1.8 %collective-permute-start.17 = (bf16[3,4,3,16,128]{4,3,2,1,0:T(8,128)(2,1)S(1)}, bf16[3,4,3,16,128]{4,3,2,1,0:T(8,128)(2,1)S(1)}, u32[]{:S(2)}, u32[]{:S(2)}) collective-permute-start(bf16[3,4,3,16,128]{4,3,2,1,0:T(8,128)(2,1)S(1)} %get-tuple-element.60), channel_id=1, source_target_pairs={{0,28},{4,24},{8,20},{12,16},{16,12},{20,8},{24,4},{28,0},{1,29},{... | collective-permute-start | bytes 442376 | tf_op jit(solution)/shard_map/ppermute | solution.py:449
  52.9 2.7 %collective-permute-start.19 = (bf16[3,4,3,16,128]{4,3,2,1,0:T(8,128)(2,1)S(1)}, bf16[3,4,3,16,128]{4,3,2,1,0:T(8,128)(2,1)S(1)}, u32[]{:S(2)}, u32[]{:S(2)}) collective-permute-start(bf16[3,4,3,16,128]{4,3,2,1,0:T(8,128)(2,1)S(1)} %get-tuple-element.62), channel_id=1, source_target_pairs={{0,8},{4,12},{8,0},{12,4},{16,24},{20,28},{24,16},{28,20},{1,9},{5... | collective-permute-start | bytes 442376 | tf_op jit(solution)/shard_map/ppermute | solution.py:449
  55.6 0.8 %collective-permute-start.20 = (bf16[3,4,3,16,128]{4,3,2,1,0:T(8,128)(2,1)S(1)}, bf16[3,4,3,16,128]{4,3,2,1,0:T(8,128)(2,1)S(1)}, u32[]{:S(2)}, u32[]{:S(2)}) collective-permute-start(bf16[3,4,3,16,128]{4,3,2,1,0:T(8,128)(2,1)S(1)} %get-tuple-element.63), channel_id=1, source_target_pairs={{0,4},{4,0},{8,12},{12,8},{16,20},{20,16},{24,28},{28,24},{1,5},{5... | collective-permute-start | bytes 442376 | tf_op jit(solution)/shard_map/ppermute | solution.py:449
  56.4 1.0 %collective-permute-done.16.refs_0_ = bf16[3,4,3,16,128]{4,3,2,1,0:T(8,128)(2,1)S(1)} collective-permute-done((bf16[3,4,3,16,128]{4,3,2,1,0:T(8,128)(2,1)S(1)}, bf16[3,4,3,16,128]{4,3,2,1,0:T(8,128)(2,1)S(1)}, u32[]{:S(2)}, u32[]{:S(2)}) %collective-permute-start.16) | collective-permute-done | bytes 147488 | tf_op jit(solution)/shard_map/ppermute | solution.py:449
  57.4 4.7 %collective-permute-start.14 = (bf16[3,4,3,16,128]{4,3,2,1,0:T(8,128)(2,1)S(1)}, bf16[3,4,3,16,128]{4,3,2,1,0:T(8,128)(2,1)S(1)}, u32[]{:S(2)}, u32[]{:S(2)}) collective-permute-start(bf16[3,4,3,16,128]{4,3,2,1,0:T(8,128)(2,1)S(1)} %get-tuple-element.57), channel_id=1, source_target_pairs={{0,16},{4,20},{8,24},{12,28},{16,0},{20,4},{24,8},{28,12},{1,17},{... | collective-permute-start | bytes 442376 | tf_op jit(solution)/shard_map/ppermute | solution.py:449
  62.1 6.4 %collective-permute-start.15 = (bf16[3,4,3,16,128]{4,3,2,1,0:T(8,128)(2,1)S(1)}, bf16[3,4,3,16,128]{4,3,2,1,0:T(8,128)(2,1)S(1)}, u32[]{:S(2)}, u32[]{:S(2)}) collective-permute-start(bf16[3,4,3,16,128]{4,3,2,1,0:T(8,128)(2,1)S(1)} %get-tuple-element.58), channel_id=1, source_target_pairs={{0,20},{4,16},{8,28},{12,24},{16,4},{20,0},{24,12},{28,8},{1,21},{... | collective-permute-start | bytes 442376 | tf_op jit(solution)/shard_map/ppermute | solution.py:449
  68.5 0.0 collective-permute-done.18.refs_2_
  68.5 0.0 collective-permute-done.19.refs_3_
  68.5 0.0 collective-permute-done.20.refs_4_
  68.5 1.1 %unpack.2 = (bf16[4,12,32,128]{3,2,1,0:T(8,128)(2,1)}, bf16[4,12,32,128]{3,2,1,0:T(8,128)(2,1)}, bf16[4,12,32,128]{3,2,1,0:T(8,128)(2,1)}) custom-call(bf16[3,4,3,16,128]{4,3,2,1,0:T(8,128)(2,1)S(1)} %collective-permute-done.16.refs_0_, bf16[3,4,3,16,128]{4,3,2,1,0:T(8,128)(2,1)S(1)} %collective-permute-done.17.refs_1_, ...), custom_call_target="tpu_custom_call" | custom-call | tf_op jit(solution)/shard_map/unpack/pallas_call | solution.py:200
  69.6 0.5 collective-permute-done.14.refs_0_
  70.1 2.3 %collective-permute-done.15.refs_1_ = bf16[3,4,3,16,128]{4,3,2,1,0:T(8,128)(2,1)S(1)} collective-permute-done((bf16[3,4,3,16,128]{4,3,2,1,0:T(8,128)(2,1)S(1)}, bf16[3,4,3,16,128]{4,3,2,1,0:T(8,128)(2,1)S(1)}, u32[]{:S(2)}, u32[]{:S(2)}) %collective-permute-start.15) | collective-permute-done | bytes 147488 | tf_op jit(solution)/shard_map/ppermute | solution.py:449
  72.5 0.8 %unpack.3 = (bf16[4,12,32,128]{3,2,1,0:T(8,128)(2,1)}, bf16[4,12,32,128]{3,2,1,0:T(8,128)(2,1)}, bf16[4,12,32,128]{3,2,1,0:T(8,128)(2,1)}) custom-call(bf16[3,4,3,16,128]{4,3,2,1,0:T(8,128)(2,1)S(1)} %collective-permute-done.14.refs_0_, ...), custom_call_target="tpu_custom_call", output_to_operand_aliasing={{0}: (2, {}), {1}: (3, {}), {2}: (4, {})} | custom-call | tf_op jit(solution)/shard_map/unpack/pallas_call | solution.py:200
  (4 shorter events, 0.0 us)
Async XLA Ops:
  0.6 17.2 %collective-permute-start.1 = (bf16[384,3072]{1,0:T(8,128)(2,1)}, bf16[384,3072]{1,0:T(8,128)(2,1)}, u32[]{:S(2)}, u32[]{:S(2)}) collective-permute-start(bf16[384,3072]{1,0:T(8,128)(2,1)} %w_own_ref.1), channel_id=1, source_target_pairs={{0,1},{1,0},{2,3},{3,2},{4,5},{5,4},{6,7},{7,6},{8,9},{9,8},{10,11... | collective-permute-start | bytes 7077896 | tf_op jit(solution)/shard_map/ppermute | solution.py:446
  1.1 23.0 %collective-permute-start = (bf16[4,32,3072]{2,1,0:T(8,128)(2,1)}, bf16[4,32,3072]{2,1,0:T(8,128)(2,1)S(1)}, u32[]{:S(2)}, u32[]{:S(2)}) collective-permute-start(bf16[4,32,3072]{2,1,0:T(8,128)(2,1)} %own_ref.1), channel_id=1, source_target_pairs={{0,2},{1,3},{2,0},{3,1},{4,6},{5,7},{6,4},{7,5},{8,10},{9,11},{10,... | collective-permute-start | bytes 2359304 | tf_op jit(solution)/shard_map/ppermute | solution.py:446
  5.5 21.0 %collective-permute-start.10 = (bf16[3,4,3,16,128]{4,3,2,1,0:T(8,128)(2,1)S(1)}, bf16[3,4,3,16,128]{4,3,2,1,0:T(8,128)(2,1)S(1)}, u32[]{:S(2)}, u32[]{:S(2)}) collective-permute-start(bf16[3,4,3,16,128]{4,3,2,1,0:T(8,128)(2,1)S(1)} %get-tuple-element.49), channel_id=1, source_target_pairs={{0,28},{4,24},{8,20},{12,16},{16,12},{20,8},{24,4},{28,0},{1,29},{... | collective-permute-start | bytes 442376 | tf_op jit(solution)/shard_map/ppermute | solution.py:449
  10.1 19.3 %collective-permute-start.11 = (bf16[3,4,3,16,128]{4,3,2,1,0:T(8,128)(2,1)S(1)}, bf16[3,4,3,16,128]{4,3,2,1,0:T(8,128)(2,1)S(1)}, u32[]{:S(2)}, u32[]{:S(2)}) collective-permute-start(bf16[3,4,3,16,128]{4,3,2,1,0:T(8,128)(2,1)S(1)} %get-tuple-element.50), channel_id=1, source_target_pairs={{0,24},{4,28},{8,16},{12,20},{16,8},{20,12},{24,0},{28,4},{1,25},{... | collective-permute-start | bytes 442376 | tf_op jit(solution)/shard_map/ppermute | solution.py:449
  10.3 23.5 %collective-permute-start.12 = (bf16[3,4,3,16,128]{4,3,2,1,0:T(8,128)(2,1)S(1)}, bf16[3,4,3,16,128]{4,3,2,1,0:T(8,128)(2,1)S(1)}, u32[]{:S(2)}, u32[]{:S(2)}) collective-permute-start(bf16[3,4,3,16,128]{4,3,2,1,0:T(8,128)(2,1)S(1)} %get-tuple-element.51), channel_id=1, source_target_pairs={{0,16},{4,20},{8,24},{12,28},{16,0},{20,4},{24,8},{28,12},{1,17},{... | collective-permute-start | bytes 442376 | tf_op jit(solution)/shard_map/ppermute | solution.py:449
  13.2 29.2 %all-to-all-start = ((bf16[4,3,4,3,16,128]{5,4,3,2,1,0:T(8,128)(2,1)}), bf16[4,3,4,3,16,128]{5,4,3,2,1,0:T(8,128)(2,1)S(1)}, u32[]{:S(2)}, u32[]{:S(2)}) async-start(bf16[4,3,4,3,16,128]{5,4,3,2,1,0:T(8,128)(2,1)} %pack_near.1), calls=%async_computation | async-start | bytes 1179648 | tf_op jit(solution)/shard_map/all_to_all | solution.py:470
  17.8 24.1 %collective-permute-start.13 = (bf16[3,4,3,16,128]{4,3,2,1,0:T(8,128)(2,1)S(1)}, bf16[3,4,3,16,128]{4,3,2,1,0:T(8,128)(2,1)S(1)}, u32[]{:S(2)}, u32[]{:S(2)}) collective-permute-start(bf16[3,4,3,16,128]{4,3,2,1,0:T(8,128)(2,1)S(1)} %get-tuple-element.52), channel_id=1, source_target_pairs={{0,20},{4,16},{8,28},{12,24},{16,4},{20,0},{24,12},{28,8},{1,21},{... | collective-permute-start | bytes 442376 | tf_op jit(solution)/shard_map/ppermute | solution.py:449
  25.8 9.8 %collective-permute-start.2 = (bf16[3,4,16,128]{3,2,1,0:T(8,128)(2,1)S(1)}, bf16[3,4,16,128]{3,2,1,0:T(8,128)(2,1)S(1)}, u32[]{:S(2)}, u32[]{:S(2)}) collective-permute-start(bf16[3,4,16,128]{3,2,1,0:T(8,128)(2,1)S(1)} %get-tuple-element.41), channel_id=1, source_target_pairs={{0,0},{1,1},{2,4},{3,5},{4,2},{5,3},{6,6},{7,7},{8,8},{9,9},{10,12... | collective-permute-start | bytes 147464 | tf_op jit(solution)/shard_map/ppermute | solution.py:459
  26.5 9.1 %collective-permute-start.3 = (bf16[3,4,16,128]{3,2,1,0:T(8,128)(2,1)S(1)}, bf16[3,4,16,128]{3,2,1,0:T(8,128)(2,1)S(1)}, u32[]{:S(2)}, u32[]{:S(2)}) collective-permute-start(bf16[3,4,16,128]{3,2,1,0:T(8,128)(2,1)S(1)} %get-tuple-element.42), channel_id=1, source_target_pairs={{0,2},{1,3},{2,6},{3,7},{4,0},{5,1},{6,4},{7,5},{8,10},{9,11},{10,... | collective-permute-start | bytes 147464 | tf_op jit(solution)/shard_map/ppermute | solution.py:459
  29.4 11.0 %collective-permute-start.4 = (bf16[3,4,16,128]{3,2,1,0:T(8,128)(2,1)S(1)}, bf16[3,4,16,128]{3,2,1,0:T(8,128)(2,1)S(1)}, u32[]{:S(2)}, u32[]{:S(2)}) collective-permute-start(bf16[3,4,16,128]{3,2,1,0:T(8,128)(2,1)S(1)} %get-tuple-element.43), channel_id=1, source_target_pairs={{0,24},{1,25},{2,28},{3,29},{4,26},{5,27},{6,30},{7,31},{8,16},{9,... | collective-permute-start | bytes 147464 | tf_op jit(solution)/shard_map/ppermute | solution.py:459
  33.8 10.5 %collective-permute-start.5 = (bf16[3,4,16,128]{3,2,1,0:T(8,128)(2,1)S(1)}, bf16[3,4,16,128]{3,2,1,0:T(8,128)(2,1)S(1)}, u32[]{:S(2)}, u32[]{:S(2)}) collective-permute-start(bf16[3,4,16,128]{3,2,1,0:T(8,128)(2,1)S(1)} %get-tuple-element.44), channel_id=1, source_target_pairs={{0,26},{1,27},{2,30},{3,31},{4,24},{5,25},{6,28},{7,29},{8,18},{9,... | collective-permute-start | bytes 147464 | tf_op jit(solution)/shard_map/ppermute | solution.py:459
  35.6 8.7 %collective-permute-start.6 = (bf16[3,4,16,128]{3,2,1,0:T(8,128)(2,1)S(1)}, bf16[3,4,16,128]{3,2,1,0:T(8,128)(2,1)S(1)}, u32[]{:S(2)}, u32[]{:S(2)}) collective-permute-start(bf16[3,4,16,128]{3,2,1,0:T(8,128)(2,1)S(1)} %get-tuple-element.45), channel_id=1, source_target_pairs={{0,16},{1,17},{2,20},{3,21},{4,18},{5,19},{6,22},{7,23},{8,24},{9,... | collective-permute-start | bytes 147464 | tf_op jit(solution)/shard_map/ppermute | solution.py:459
  35.6 8.7 %collective-permute-start.7 = (bf16[3,4,16,128]{3,2,1,0:T(8,128)(2,1)S(1)}, bf16[3,4,16,128]{3,2,1,0:T(8,128)(2,1)S(1)}, u32[]{:S(2)}, u32[]{:S(2)}) collective-permute-start(bf16[3,4,16,128]{3,2,1,0:T(8,128)(2,1)S(1)} %get-tuple-element.46), channel_id=1, source_target_pairs={{0,18},{1,19},{2,22},{3,23},{4,16},{5,17},{6,20},{7,21},{8,26},{9,... | collective-permute-start | bytes 147464 | tf_op jit(solution)/shard_map/ppermute | solution.py:459
  40.4 4.4 %collective-permute-start.8 = (bf16[3,4,16,128]{3,2,1,0:T(8,128)(2,1)S(1)}, bf16[3,4,16,128]{3,2,1,0:T(8,128)(2,1)S(1)}, u32[]{:S(2)}, u32[]{:S(2)}) collective-permute-start(bf16[3,4,16,128]{3,2,1,0:T(8,128)(2,1)S(1)} %get-tuple-element.47), channel_id=1, source_target_pairs={{0,8},{1,9},{2,12},{3,13},{4,10},{5,11},{6,14},{7,15},{8,0},{9,1},... | collective-permute-start | bytes 147464 | tf_op jit(solution)/shard_map/ppermute | solution.py:459
  41.9 5.0 %collective-permute-start.9 = (bf16[3,4,16,128]{3,2,1,0:T(8,128)(2,1)S(1)}, bf16[3,4,16,128]{3,2,1,0:T(8,128)(2,1)S(1)}, u32[]{:S(2)}, u32[]{:S(2)}) collective-permute-start(bf16[3,4,16,128]{3,2,1,0:T(8,128)(2,1)S(1)} %get-tuple-element.48), channel_id=1, source_target_pairs={{0,10},{1,11},{2,14},{3,15},{4,8},{5,9},{6,12},{7,13},{8,2},{9,3},... | collective-permute-start | bytes 147464 | tf_op jit(solution)/shard_map/ppermute | solution.py:459
  48.8 8.6 %collective-permute-start.16 = (bf16[3,4,3,16,128]{4,3,2,1,0:T(8,128)(2,1)S(1)}, bf16[3,4,3,16,128]{4,3,2,1,0:T(8,128)(2,1)S(1)}, u32[]{:S(2)}, u32[]{:S(2)}) collective-permute-start(bf16[3,4,3,16,128]{4,3,2,1,0:T(8,128)(2,1)S(1)} %get-tuple-element.59), channel_id=1, source_target_pairs={{0,24},{4,28},{8,16},{12,20},{16,8},{20,12},{24,0},{28,4},{1,25},{... | collective-permute-start | bytes 442376 | tf_op jit(solution)/shard_map/ppermute | solution.py:449
  51.1 11.0 %collective-permute-start.17 = (bf16[3,4,3,16,128]{4,3,2,1,0:T(8,128)(2,1)S(1)}, bf16[3,4,3,16,128]{4,3,2,1,0:T(8,128)(2,1)S(1)}, u32[]{:S(2)}, u32[]{:S(2)}) collective-permute-start(bf16[3,4,3,16,128]{4,3,2,1,0:T(8,128)(2,1)S(1)} %get-tuple-element.60), channel_id=1, source_target_pairs={{0,28},{4,24},{8,20},{12,16},{16,12},{20,8},{24,4},{28,0},{1,29},{... | collective-permute-start | bytes 442376 | tf_op jit(solution)/shard_map/ppermute | solution.py:449
  52.9 15.6 %collective-permute-start.18 = (bf16[3,4,3,16,128]{4,3,2,1,0:T(8,128)(2,1)S(1)}, bf16[3,4,3,16,128]{4,3,2,1,0:T(8,128)(2,1)S(1)}, u32[]{:S(2)}, u32[]{:S(2)}) collective-permute-start(bf16[3,4,3,16,128]{4,3,2,1,0:T(8,128)(2,1)S(1)} %get-tuple-element.61), channel_id=1, source_target_pairs={{0,12},{4,8},{8,4},{12,0},{16,28},{20,24},{24,20},{28,16},{1,13},{... | collective-permute-start | bytes 442376 | tf_op jit(solution)/shard_map/ppermute | solution.py:449
  52.9 15.6 %collective-permute-start.19 = (bf16[3,4,3,16,128]{4,3,2,1,0:T(8,128)(2,1)S(1)}, bf16[3,4,3,16,128]{4,3,2,1,0:T(8,128)(2,1)S(1)}, u32[]{:S(2)}, u32[]{:S(2)}) collective-permute-start(bf16[3,4,3,16,128]{4,3,2,1,0:T(8,128)(2,1)S(1)} %get-tuple-element.62), channel_id=1, source_target_pairs={{0,8},{4,12},{8,0},{12,4},{16,24},{20,28},{24,16},{28,20},{1,9},{5... | collective-permute-start | bytes 442376 | tf_op jit(solution)/shard_map/ppermute | solution.py:449
  55.6 12.9 %collective-permute-start.20 = (bf16[3,4,3,16,128]{4,3,2,1,0:T(8,128)(2,1)S(1)}, bf16[3,4,3,16,128]{4,3,2,1,0:T(8,128)(2,1)S(1)}, u32[]{:S(2)}, u32[]{:S(2)}) collective-permute-start(bf16[3,4,3,16,128]{4,3,2,1,0:T(8,128)(2,1)S(1)} %get-tuple-element.63), channel_id=1, source_target_pairs={{0,4},{4,0},{8,12},{12,8},{16,20},{20,16},{24,28},{28,24},{1,5},{5... | collective-permute-start | bytes 442376 | tf_op jit(solution)/shard_map/ppermute | solution.py:449
  57.4 12.8 %collective-permute-start.14 = (bf16[3,4,3,16,128]{4,3,2,1,0:T(8,128)(2,1)S(1)}, bf16[3,4,3,16,128]{4,3,2,1,0:T(8,128)(2,1)S(1)}, u32[]{:S(2)}, u32[]{:S(2)}) collective-permute-start(bf16[3,4,3,16,128]{4,3,2,1,0:T(8,128)(2,1)S(1)} %get-tuple-element.57), channel_id=1, source_target_pairs={{0,16},{4,20},{8,24},{12,28},{16,0},{20,4},{24,8},{28,12},{1,17},{... | collective-permute-start | bytes 442376 | tf_op jit(solution)/shard_map/ppermute | solution.py:449
  62.1 10.4 %collective-permute-start.15 = (bf16[3,4,3,16,128]{4,3,2,1,0:T(8,128)(2,1)S(1)}, bf16[3,4,3,16,128]{4,3,2,1,0:T(8,128)(2,1)S(1)}, u32[]{:S(2)}, u32[]{:S(2)}) collective-permute-start(bf16[3,4,3,16,128]{4,3,2,1,0:T(8,128)(2,1)S(1)} %get-tuple-element.58), channel_id=1, source_target_pairs={{0,20},{4,16},{8,28},{12,24},{16,4},{20,0},{24,12},{28,8},{1,21},{... | collective-permute-start | bytes 442376 | tf_op jit(solution)/shard_map/ppermute | solution.py:449

commit v5 on v4

--- a/solution.py
+++ b/solution.py
@@ -12,7 +12,7 @@
 VMEM = pl.BlockSpec(memory_space=pltpu.VMEM)
 MIB = 1024 * 1024
 SLOTS = (6, 7, 4, 5, 3, 2, 1, 0)
-LATE = (4, 5)
+LATE = (5, 4)
 FAR = (7, 6, 4, 5)
 ROUNDS = (0, 1, 6, 7, 4, 5, 2, 3)
 GROUPS = 4

time: 74 us -> 73 us (0.986)
  starting transfers between devices: 50.2 us -> 47.6 us
  waiting for transfers between devices: 7.3 us -> 9.12 us
    ppermute x11, starting transfers between devices: 26.7 us -> 24.1 us  [send(): lax.ppermute(message, 'tm', [(i, i ^ k) for i in range(n_tm)])]
    ppermute x11, waiting for transfers between devices: 4.74 us -> 6.57 us  [send(): lax.ppermute(message, 'tm', [(i, i ^ k) for i in range(n_tm)])]
  transfers between devices with their start and end apart: 22 -> 22, of which waited for: 6 -> 7; matrix products, arithmetic and copies ran while one was open for 0% -> 0% of each run, Pallas kernels for 17% -> 17%
where the time goes in v5:
time: 73 us; the launch traced here: 72.5 us
  starting transfers between devices  47.6 us (65%)
  Pallas kernels  15 us (21%)
  waiting for transfers between devices  9.12 us (12%)
  between operations  0.76 us (1%)
    ppermute x11, starting transfers between devices, send(): lax.ppermute(message, 'tm', [(i, i ^ k) for i in range(n_tm)])  24.1 us
    ppermute x8, starting transfers between devices, round_of(): return lax.ppermute(message, ('tm', 'fsdp'), pairs)  15.7 us
    ppermute x11, waiting for transfers between devices, send(): lax.ppermute(message, 'tm', [(i, i ^ k) for i in range(n_tm)])  6.57 us
    all_to_all x1, starting transfers between devices, body_permutes(): lax.all_to_all(near_message, 'tm', split_axis=0, concat_axis=0, axis_inde...  4.66 us
    pallas_call x1, Pallas kernels, project_own(): pl.pallas_call(project_own_kernel, out_shape=[jax.ShapeDtypeStruct((2, 1,...  3.92 us
    ppermute x2, starting transfers between devices, swap(): return lax.ppermute(x, 'fsdp', [(i, i ^ bit) for i in range(n_fsdp)])  3.09 us
    ppermute x8, waiting for transfers between devices, round_of(): return lax.ppermute(message, ('tm', 'fsdp'), pairs)  2.54 us
    pallas_call x1, Pallas kernels, pack_near(): pl.pallas_call(pack_near_kernel, out_shape=jax.ShapeDtypeStruct(shape, q_...  2.04 us
  transfers between devices with their start and end apart: 22, of which 7 were waited for; matrix products, arithmetic and copies ran while one was open for 0% of the time, Pallas kernels for 17%

profile of v5, /device:TPU:0, one launch (start us, length us, event | category | flops | bytes accessed | tf_op | source)
XLA Modules:
  0.0 72.5 jit_solution(8200039033525485390)
XLA Ops:
  0.6 0.5 collective-permute-start.1
  1.1 2.6 %collective-permute-start = (bf16[4,32,3072]{2,1,0:T(8,128)(2,1)}, bf16[4,32,3072]{2,1,0:T(8,128)(2,1)S(1)}, u32[]{:S(2)}, u32[]{:S(2)}) collective-permute-start(bf16[4,32,3072]{2,1,0:T(8,128)(2,1)} %own_ref.1), channel_id=1, source_target_pairs={{0,2},{1,3},{2,0},{3,1},{4,6},{5,7},{6,4},{7,5},{8,10},{9,11},{10,... | collective-permute-start | bytes 2359304 | tf_op jit(solution)/shard_map/ppermute | solution.py:446
  3.7 1.8 %pack_far.1 = (bf16[3,4,3,16,128]{4,3,2,1,0:T(8,128)(2,1)S(1)}, bf16[3,4,3,16,128]{4,3,2,1,0:T(8,128)(2,1)S(1)}, bf16[3,4,3,16,128]{4,3,2,1,0:T(8,128)(2,1)S(1)}, bf16[3,4,3,16,128]{4,3,2,1,0:T(8,128)(2,1)S(1)}) custom-call(bf16[4,12,32,128]{3,2,1,0:T(8,128)(2,1)} %bitcast.6, bf16[4,12,32,128]{3,2,1,0:T(8,128)(2,1)} %bitcast.8, bf16[4,12,32,128]{3,2,1,0:T(8,128)(2,1)} %bitcast.10), custom_call_target="tpu_custom_call" | custom-call | tf_op jit(solution)/shard_map/pack_far/pallas_call | solution.py:149
  5.5 4.6 %collective-permute-start.10 = (bf16[3,4,3,16,128]{4,3,2,1,0:T(8,128)(2,1)S(1)}, bf16[3,4,3,16,128]{4,3,2,1,0:T(8,128)(2,1)S(1)}, u32[]{:S(2)}, u32[]{:S(2)}) collective-permute-start(bf16[3,4,3,16,128]{4,3,2,1,0:T(8,128)(2,1)S(1)} %get-tuple-element.49), channel_id=1, source_target_pairs={{0,28},{4,24},{8,20},{12,16},{16,12},{20,8},{24,4},{28,0},{1,29},{... | collective-permute-start | bytes 442376 | tf_op jit(solution)/shard_map/ppermute | solution.py:449
  10.1 0.2 collective-permute-start.11
  10.3 0.8 %collective-permute-start.12 = (bf16[3,4,3,16,128]{4,3,2,1,0:T(8,128)(2,1)S(1)}, bf16[3,4,3,16,128]{4,3,2,1,0:T(8,128)(2,1)S(1)}, u32[]{:S(2)}, u32[]{:S(2)}) collective-permute-start(bf16[3,4,3,16,128]{4,3,2,1,0:T(8,128)(2,1)S(1)} %get-tuple-element.51), channel_id=1, source_target_pairs={{0,16},{4,20},{8,24},{12,28},{16,0},{20,4},{24,8},{28,12},{1,17},{... | collective-permute-start | bytes 442376 | tf_op jit(solution)/shard_map/ppermute | solution.py:449
  11.1 2.0 %pack_near.1 = bf16[4,3,4,3,16,128]{5,4,3,2,1,0:T(8,128)(2,1)} custom-call(bf16[4,12,32,128]{3,2,1,0:T(8,128)(2,1)} %bitcast.7, bf16[4,12,32,128]{3,2,1,0:T(8,128)(2,1)} %bitcast.9, bf16[4,12,32,128]{3,2,1,0:T(8,128)(2,1)} %bitcast.11), custom_call_target="tpu_custom_call" | custom-call | tf_op jit(solution)/shard_map/pack_near/pallas_call | solution.py:166
  13.2 4.7 %all-to-all-start = ((bf16[4,3,4,3,16,128]{5,4,3,2,1,0:T(8,128)(2,1)}), bf16[4,3,4,3,16,128]{5,4,3,2,1,0:T(8,128)(2,1)S(1)}, u32[]{:S(2)}, u32[]{:S(2)}) async-start(bf16[4,3,4,3,16,128]{5,4,3,2,1,0:T(8,128)(2,1)} %pack_near.1), calls=%async_computation | async-start | bytes 1179648 | tf_op jit(solution)/shard_map/all_to_all | solution.py:470
  17.8 0.0 collective-permute-done.1.w_other_ref
  17.8 2.4 %collective-permute-start.13 = (bf16[3,4,3,16,128]{4,3,2,1,0:T(8,128)(2,1)S(1)}, bf16[3,4,3,16,128]{4,3,2,1,0:T(8,128)(2,1)S(1)}, u32[]{:S(2)}, u32[]{:S(2)}) collective-permute-start(bf16[3,4,3,16,128]{4,3,2,1,0:T(8,128)(2,1)S(1)} %get-tuple-element.52), channel_id=1, source_target_pairs={{0,20},{4,16},{8,28},{12,24},{16,4},{20,0},{24,12},{28,8},{1,21},{... | collective-permute-start | bytes 442376 | tf_op jit(solution)/shard_map/ppermute | solution.py:449
  20.2 3.9 %project_own.1 = (bf16[2,1,3,4,32,128]{5,4,3,2,1,0:T(8,128)(2,1)S(1)}, bf16[2,384,3072]{2,1,0:T(8,128)(2,1)S(1)}) custom-call(bf16[4,32,3072]{2,1,0:T(8,128)(2,1)} %own_ref.1, bf16[384,3072]{1,0:T(8,128)(2,1)} %w_own_ref.1, bf16[384,3072]{1,0:T(8,128)(2,1)} %collective-permute-done.1.w_other_ref), custom_call_target="tpu_custom_call" | custom-call | flops 603979776 | bytes 5505024 | tf_op jit(solution)/shard_map/project_own/pallas_call | solution.py:278
  24.2 0.0 collective-permute-done.other_ref
  24.2 1.7 %project_other.1 = (bf16[3,4,16,128]{3,2,1,0:T(8,128)(2,1)S(1)}, bf16[3,4,16,128]{3,2,1,0:T(8,128)(2,1)S(1)}, bf16[3,4,16,128]{3,2,1,0:T(8,128)(2,1)S(1)}, bf16[...) custom-call(bf16[4,32,3072]{2,1,0:T(8,128)(2,1)S(1)} %collective-per, ...), custom_call_target="tpu_custom_call" | custom-call | flops 9663676416 | bytes 5505024 | tf_op jit(solution)/shard_map/project_other/pallas_call | solution.py:301
  25.8 0.7 collective-permute-start.2
  26.5 2.9 %collective-permute-start.3 = (bf16[3,4,16,128]{3,2,1,0:T(8,128)(2,1)S(1)}, bf16[3,4,16,128]{3,2,1,0:T(8,128)(2,1)S(1)}, u32[]{:S(2)}, u32[]{:S(2)}) collective-permute-start(bf16[3,4,16,128]{3,2,1,0:T(8,128)(2,1)S(1)} %get-tuple-element.42), channel_id=1, source_target_pairs={{0,2},{1,3},{2,6},{3,7},{4,0},{5,1},{6,4},{7,5},{8,10},{9,11},{10,... | collective-permute-start | bytes 147464 | tf_op jit(solution)/shard_map/ppermute | solution.py:459
  29.4 0.0 collective-permute-done.11.refs_1_
  29.4 3.6 %collective-permute-start.4 = (bf16[3,4,16,128]{3,2,1,0:T(8,128)(2,1)S(1)}, bf16[3,4,16,128]{3,2,1,0:T(8,128)(2,1)S(1)}, u32[]{:S(2)}, u32[]{:S(2)}) collective-permute-start(bf16[3,4,16,128]{3,2,1,0:T(8,128)(2,1)S(1)} %get-tuple-element.43), channel_id=1, source_target_pairs={{0,24},{1,25},{2,28},{3,29},{4,26},{5,27},{6,30},{7,31},{8,16},{9,... | collective-permute-start | bytes 147464 | tf_op jit(solution)/shard_map/ppermute | solution.py:459
  33.0 0.8 %collective-permute-done.12.refs_2_ = bf16[3,4,3,16,128]{4,3,2,1,0:T(8,128)(2,1)S(1)} collective-permute-done((bf16[3,4,3,16,128]{4,3,2,1,0:T(8,128)(2,1)S(1)}, bf16[3,4,3,16,128]{4,3,2,1,0:T(8,128)(2,1)S(1)}, u32[]{:S(2)}, u32[]{:S(2)}) %collective-permute-start.12) | collective-permute-done | bytes 147488 | tf_op jit(solution)/shard_map/ppermute | solution.py:449
  33.8 1.8 %collective-permute-start.5 = (bf16[3,4,16,128]{3,2,1,0:T(8,128)(2,1)S(1)}, bf16[3,4,16,128]{3,2,1,0:T(8,128)(2,1)S(1)}, u32[]{:S(2)}, u32[]{:S(2)}) collective-permute-start(bf16[3,4,16,128]{3,2,1,0:T(8,128)(2,1)S(1)} %get-tuple-element.44), channel_id=1, source_target_pairs={{0,26},{1,27},{2,30},{3,31},{4,24},{5,25},{6,28},{7,29},{8,18},{9,... | collective-permute-start | bytes 147464 | tf_op jit(solution)/shard_map/ppermute | solution.py:459
  35.6 0.0 collective-permute-done.2.refs_0_
  35.6 0.0 collective-permute-start.6
  35.6 0.0 collective-permute-done.3.refs_1_
  35.6 4.7 %collective-permute-start.7 = (bf16[3,4,16,128]{3,2,1,0:T(8,128)(2,1)S(1)}, bf16[3,4,16,128]{3,2,1,0:T(8,128)(2,1)S(1)}, u32[]{:S(2)}, u32[]{:S(2)}) collective-permute-start(bf16[3,4,16,128]{3,2,1,0:T(8,128)(2,1)S(1)} %get-tuple-element.46), channel_id=1, source_target_pairs={{0,18},{1,19},{2,22},{3,23},{4,16},{5,17},{6,20},{7,21},{8,26},{9,... | collective-permute-start | bytes 147464 | tf_op jit(solution)/shard_map/ppermute | solution.py:459
  40.4 0.0 collective-permute-done.4.refs_2_
  40.4 1.5 %collective-permute-start.8 = (bf16[3,4,16,128]{3,2,1,0:T(8,128)(2,1)S(1)}, bf16[3,4,16,128]{3,2,1,0:T(8,128)(2,1)S(1)}, u32[]{:S(2)}, u32[]{:S(2)}) collective-permute-start(bf16[3,4,16,128]{3,2,1,0:T(8,128)(2,1)S(1)} %get-tuple-element.47), channel_id=1, source_target_pairs={{0,8},{1,9},{2,12},{3,13},{4,10},{5,11},{6,14},{7,15},{8,0},{9,1},... | collective-permute-start | bytes 147464 | tf_op jit(solution)/shard_map/ppermute | solution.py:459
  41.9 0.5 collective-permute-start.9
  42.4 0.0 all-to-all-done.refs_4_
  42.4 1.9 %probs.1 = (bf16[12,128,128]{2,1,0:T(8,128)(2,1)S(1)}, bf16[12,128,128]{2,1,0:T(8,128)(2,1)S(1)}, bf16[12,128,128]{2,1,0:T(8,128)(2,1)S(1)}, f32[12,128,128]{2,1,0:T(8,128)S(1)}) custom-call(bf16[3,4,3,16,128]{4,3,2,1,0:T(8,128)(2,1)S(1)} %collective-permute-done.10.refs_0_, bf16[3,4,3,16,128]{4,3,2,1,0:T(8,128)(2,1)S(1)} %collective-permute-done.11.refs_1_, ...), custom_call_target="tpu_custom_call" | custom-call | tf_op jit(solution)/shard_map/probs/pallas_call | solution.py:405
  44.3 0.0 collective-permute-done.5.refs_3_
  44.3 0.0 collective-permute-done.7.refs_5_
  44.3 0.4 collective-permute-done.8.refs_6_
  44.8 2.1 %collective-permute-done.9.refs_7_ = bf16[3,4,16,128]{3,2,1,0:T(8,128)(2,1)S(1)} collective-permute-done((bf16[3,4,16,128]{3,2,1,0:T(8,128)(2,1)S(1)}, bf16[3,4,16,128]{3,2,1,0:T(8,128)(2,1)S(1)}, u32[]{:S(2)}, u32[]{:S(2)}) %collective-permute-start.9) | collective-permute-done | bytes 49184 | tf_op jit(solution)/shard_map/ppermute | solution.py:459
  46.9 1.9 %grads.1 = (bf16[3,4,3,16,128]{4,3,2,1,0:T(8,128)(2,1)S(1)}, bf16[3,4,3,16,128]{4,3,2,1,0:T(8,128)(2,1)S(1)}, bf16[3,4,3,16,128]{4,3,2,1,0:T(8,128)(2,1)S(1)}, b...) custom-call(bf16[3,4,16,128]{3,2,1,0:T(8,128)(2,1)S(1)} %collective-, ...), custom_call_target="tpu_custom_call" | custom-call | tf_op jit(solution)/shard_map/grads/pallas_call | solution.py:421
  48.8 2.3 %collective-permute-start.16 = (bf16[3,4,3,16,128]{4,3,2,1,0:T(8,128)(2,1)S(1)}, bf16[3,4,3,16,128]{4,3,2,1,0:T(8,128)(2,1)S(1)}, u32[]{:S(2)}, u32[]{:S(2)}) collective-permute-start(bf16[3,4,3,16,128]{4,3,2,1,0:T(8,128)(2,1)S(1)} %get-tuple-element.59), channel_id=1, source_target_pairs={{0,24},{4,28},{8,16},{12,20},{16,8},{20,12},{24,0},{28,4},{1,25},{... | collective-permute-start | bytes 442376 | tf_op jit(solution)/shard_map/ppermute | solution.py:449
  51.1 1.8 %collective-permute-start.17 = (bf16[3,4,3,16,128]{4,3,2,1,0:T(8,128)(2,1)S(1)}, bf16[3,4,3,16,128]{4,3,2,1,0:T(8,128)(2,1)S(1)}, u32[]{:S(2)}, u32[]{:S(2)}) collective-permute-start(bf16[3,4,3,16,128]{4,3,2,1,0:T(8,128)(2,1)S(1)} %get-tuple-element.60), channel_id=1, source_target_pairs={{0,28},{4,24},{8,20},{12,16},{16,12},{20,8},{24,4},{28,0},{1,29},{... | collective-permute-start | bytes 442376 | tf_op jit(solution)/shard_map/ppermute | solution.py:449
  52.9 0.0 collective-permute-start.18
  52.9 2.7 %collective-permute-start.19 = (bf16[3,4,3,16,128]{4,3,2,1,0:T(8,128)(2,1)S(1)}, bf16[3,4,3,16,128]{4,3,2,1,0:T(8,128)(2,1)S(1)}, u32[]{:S(2)}, u32[]{:S(2)}) collective-permute-start(bf16[3,4,3,16,128]{4,3,2,1,0:T(8,128)(2,1)S(1)} %get-tuple-element.62), channel_id=1, source_target_pairs={{0,8},{4,12},{8,0},{12,4},{16,24},{20,28},{24,16},{28,20},{1,9},{5... | collective-permute-start | bytes 442376 | tf_op jit(solution)/shard_map/ppermute | solution.py:449
  55.6 0.8 %collective-permute-start.20 = (bf16[3,4,3,16,128]{4,3,2,1,0:T(8,128)(2,1)S(1)}, bf16[3,4,3,16,128]{4,3,2,1,0:T(8,128)(2,1)S(1)}, u32[]{:S(2)}, u32[]{:S(2)}) collective-permute-start(bf16[3,4,3,16,128]{4,3,2,1,0:T(8,128)(2,1)S(1)} %get-tuple-element.63), channel_id=1, source_target_pairs={{0,4},{4,0},{8,12},{12,8},{16,20},{20,16},{24,28},{28,24},{1,5},{5... | collective-permute-start | bytes 442376 | tf_op jit(solution)/shard_map/ppermute | solution.py:449
  56.4 1.0 %collective-permute-done.16.refs_0_ = bf16[3,4,3,16,128]{4,3,2,1,0:T(8,128)(2,1)S(1)} collective-permute-done((bf16[3,4,3,16,128]{4,3,2,1,0:T(8,128)(2,1)S(1)}, bf16[3,4,3,16,128]{4,3,2,1,0:T(8,128)(2,1)S(1)}, u32[]{:S(2)}, u32[]{:S(2)}) %collective-permute-start.16) | collective-permute-done | bytes 147488 | tf_op jit(solution)/shard_map/ppermute | solution.py:449
  57.4 1.8 %collective-permute-start.14 = (bf16[3,4,3,16,128]{4,3,2,1,0:T(8,128)(2,1)S(1)}, bf16[3,4,3,16,128]{4,3,2,1,0:T(8,128)(2,1)S(1)}, u32[]{:S(2)}, u32[]{:S(2)}) collective-permute-start(bf16[3,4,3,16,128]{4,3,2,1,0:T(8,128)(2,1)S(1)} %get-tuple-element.57), channel_id=1, source_target_pairs={{0,20},{4,16},{8,28},{12,24},{16,4},{20,0},{24,12},{28,8},{1,21},{... | collective-permute-start | bytes 442376 | tf_op jit(solution)/shard_map/ppermute | solution.py:449
  59.2 1.5 %collective-permute-done.17.refs_1_ = bf16[3,4,3,16,128]{4,3,2,1,0:T(8,128)(2,1)S(1)} collective-permute-done((bf16[3,4,3,16,128]{4,3,2,1,0:T(8,128)(2,1)S(1)}, bf16[3,4,3,16,128]{4,3,2,1,0:T(8,128)(2,1)S(1)}, u32[]{:S(2)}, u32[]{:S(2)}) %collective-permute-start.17) | collective-permute-done | bytes 147488 | tf_op jit(solution)/shard_map/ppermute | solution.py:449
  60.7 6.7 %collective-permute-start.15 = (bf16[3,4,3,16,128]{4,3,2,1,0:T(8,128)(2,1)S(1)}, bf16[3,4,3,16,128]{4,3,2,1,0:T(8,128)(2,1)S(1)}, u32[]{:S(2)}, u32[]{:S(2)}) collective-permute-start(bf16[3,4,3,16,128]{4,3,2,1,0:T(8,128)(2,1)S(1)} %get-tuple-element.58), channel_id=1, source_target_pairs={{0,16},{4,20},{8,24},{12,28},{16,0},{20,4},{24,8},{28,12},{1,17},{... | collective-permute-start | bytes 442376 | tf_op jit(solution)/shard_map/ppermute | solution.py:449
  67.4 0.0 collective-permute-done.19.refs_3_
  67.4 0.0 collective-permute-done.20.refs_4_
  67.4 1.1 %unpack.2 = (bf16[4,12,32,128]{3,2,1,0:T(8,128)(2,1)}, bf16[4,12,32,128]{3,2,1,0:T(8,128)(2,1)}, bf16[4,12,32,128]{3,2,1,0:T(8,128)(2,1)}) custom-call(bf16[3,4,3,16,128]{4,3,2,1,0:T(8,128)(2,1)S(1)} %collective-permute-done.16.refs_0_, bf16[3,4,3,16,128]{4,3,2,1,0:T(8,128)(2,1)S(1)} %collective-permute-done.17.refs_1_, ...), custom_call_target="tpu_custom_call" | custom-call | tf_op jit(solution)/shard_map/unpack/pallas_call | solution.py:200
  68.5 2.3 %collective-permute-done.14.refs_0_ = bf16[3,4,3,16,128]{4,3,2,1,0:T(8,128)(2,1)S(1)} collective-permute-done((bf16[3,4,3,16,128]{4,3,2,1,0:T(8,128)(2,1)S(1)}, bf16[3,4,3,16,128]{4,3,2,1,0:T(8,128)(2,1)S(1)}, u32[]{:S(2)}, u32[]{:S(2)}) %collective-permute-start.14) | collective-permute-done | bytes 147488 | tf_op jit(solution)/shard_map/ppermute | solution.py:449
  70.8 0.9 %collective-permute-done.15.refs_1_ = bf16[3,4,3,16,128]{4,3,2,1,0:T(8,128)(2,1)S(1)} collective-permute-done((bf16[3,4,3,16,128]{4,3,2,1,0:T(8,128)(2,1)S(1)}, bf16[3,4,3,16,128]{4,3,2,1,0:T(8,128)(2,1)S(1)}, u32[]{:S(2)}, u32[]{:S(2)}) %collective-permute-start.15) | collective-permute-done | bytes 147488 | tf_op jit(solution)/shard_map/ppermute | solution.py:449
  71.7 0.8 %unpack.3 = (bf16[4,12,32,128]{3,2,1,0:T(8,128)(2,1)}, bf16[4,12,32,128]{3,2,1,0:T(8,128)(2,1)}, bf16[4,12,32,128]{3,2,1,0:T(8,128)(2,1)}) custom-call(bf16[3,4,3,16,128]{4,3,2,1,0:T(8,128)(2,1)S(1)} %collective-permute-done.14.refs_0_, ...), custom_call_target="tpu_custom_call", output_to_operand_aliasing={{0}: (2, {}), {1}: (3, {}), {2}: (4, {})} | custom-call | tf_op jit(solution)/shard_map/unpack/pallas_call | solution.py:200
  (4 shorter events, 0.0 us)
Async XLA Ops:
  0.6 17.2 %collective-permute-start.1 = (bf16[384,3072]{1,0:T(8,128)(2,1)}, bf16[384,3072]{1,0:T(8,128)(2,1)}, u32[]{:S(2)}, u32[]{:S(2)}) collective-permute-start(bf16[384,3072]{1,0:T(8,128)(2,1)} %w_own_ref.1), channel_id=1, source_target_pairs={{0,1},{1,0},{2,3},{3,2},{4,5},{5,4},{6,7},{7,6},{8,9},{9,8},{10,11... | collective-permute-start | bytes 7077896 | tf_op jit(solution)/shard_map/ppermute | solution.py:446
  1.1 23.0 %collective-permute-start = (bf16[4,32,3072]{2,1,0:T(8,128)(2,1)}, bf16[4,32,3072]{2,1,0:T(8,128)(2,1)S(1)}, u32[]{:S(2)}, u32[]{:S(2)}) collective-permute-start(bf16[4,32,3072]{2,1,0:T(8,128)(2,1)} %own_ref.1), channel_id=1, source_target_pairs={{0,2},{1,3},{2,0},{3,1},{4,6},{5,7},{6,4},{7,5},{8,10},{9,11},{10,... | collective-permute-start | bytes 2359304 | tf_op jit(solution)/shard_map/ppermute | solution.py:446
  5.5 21.0 %collective-permute-start.10 = (bf16[3,4,3,16,128]{4,3,2,1,0:T(8,128)(2,1)S(1)}, bf16[3,4,3,16,128]{4,3,2,1,0:T(8,128)(2,1)S(1)}, u32[]{:S(2)}, u32[]{:S(2)}) collective-permute-start(bf16[3,4,3,16,128]{4,3,2,1,0:T(8,128)(2,1)S(1)} %get-tuple-element.49), channel_id=1, source_target_pairs={{0,28},{4,24},{8,20},{12,16},{16,12},{20,8},{24,4},{28,0},{1,29},{... | collective-permute-start | bytes 442376 | tf_op jit(solution)/shard_map/ppermute | solution.py:449
  10.1 19.3 %collective-permute-start.11 = (bf16[3,4,3,16,128]{4,3,2,1,0:T(8,128)(2,1)S(1)}, bf16[3,4,3,16,128]{4,3,2,1,0:T(8,128)(2,1)S(1)}, u32[]{:S(2)}, u32[]{:S(2)}) collective-permute-start(bf16[3,4,3,16,128]{4,3,2,1,0:T(8,128)(2,1)S(1)} %get-tuple-element.50), channel_id=1, source_target_pairs={{0,24},{4,28},{8,16},{12,20},{16,8},{20,12},{24,0},{28,4},{1,25},{... | collective-permute-start | bytes 442376 | tf_op jit(solution)/shard_map/ppermute | solution.py:449
  10.3 23.5 %collective-permute-start.12 = (bf16[3,4,3,16,128]{4,3,2,1,0:T(8,128)(2,1)S(1)}, bf16[3,4,3,16,128]{4,3,2,1,0:T(8,128)(2,1)S(1)}, u32[]{:S(2)}, u32[]{:S(2)}) collective-permute-start(bf16[3,4,3,16,128]{4,3,2,1,0:T(8,128)(2,1)S(1)} %get-tuple-element.51), channel_id=1, source_target_pairs={{0,16},{4,20},{8,24},{12,28},{16,0},{20,4},{24,8},{28,12},{1,17},{... | collective-permute-start | bytes 442376 | tf_op jit(solution)/shard_map/ppermute | solution.py:449
  13.2 29.2 %all-to-all-start = ((bf16[4,3,4,3,16,128]{5,4,3,2,1,0:T(8,128)(2,1)}), bf16[4,3,4,3,16,128]{5,4,3,2,1,0:T(8,128)(2,1)S(1)}, u32[]{:S(2)}, u32[]{:S(2)}) async-start(bf16[4,3,4,3,16,128]{5,4,3,2,1,0:T(8,128)(2,1)} %pack_near.1), calls=%async_computation | async-start | bytes 1179648 | tf_op jit(solution)/shard_map/all_to_all | solution.py:470
  17.8 24.1 %collective-permute-start.13 = (bf16[3,4,3,16,128]{4,3,2,1,0:T(8,128)(2,1)S(1)}, bf16[3,4,3,16,128]{4,3,2,1,0:T(8,128)(2,1)S(1)}, u32[]{:S(2)}, u32[]{:S(2)}) collective-permute-start(bf16[3,4,3,16,128]{4,3,2,1,0:T(8,128)(2,1)S(1)} %get-tuple-element.52), channel_id=1, source_target_pairs={{0,20},{4,16},{8,28},{12,24},{16,4},{20,0},{24,12},{28,8},{1,21},{... | collective-permute-start | bytes 442376 | tf_op jit(solution)/shard_map/ppermute | solution.py:449
  25.8 9.8 %collective-permute-start.2 = (bf16[3,4,16,128]{3,2,1,0:T(8,128)(2,1)S(1)}, bf16[3,4,16,128]{3,2,1,0:T(8,128)(2,1)S(1)}, u32[]{:S(2)}, u32[]{:S(2)}) collective-permute-start(bf16[3,4,16,128]{3,2,1,0:T(8,128)(2,1)S(1)} %get-tuple-element.41), channel_id=1, source_target_pairs={{0,0},{1,1},{2,4},{3,5},{4,2},{5,3},{6,6},{7,7},{8,8},{9,9},{10,12... | collective-permute-start | bytes 147464 | tf_op jit(solution)/shard_map/ppermute | solution.py:459
  26.5 9.1 %collective-permute-start.3 = (bf16[3,4,16,128]{3,2,1,0:T(8,128)(2,1)S(1)}, bf16[3,4,16,128]{3,2,1,0:T(8,128)(2,1)S(1)}, u32[]{:S(2)}, u32[]{:S(2)}) collective-permute-start(bf16[3,4,16,128]{3,2,1,0:T(8,128)(2,1)S(1)} %get-tuple-element.42), channel_id=1, source_target_pairs={{0,2},{1,3},{2,6},{3,7},{4,0},{5,1},{6,4},{7,5},{8,10},{9,11},{10,... | collective-permute-start | bytes 147464 | tf_op jit(solution)/shard_map/ppermute | solution.py:459
  29.4 11.0 %collective-permute-start.4 = (bf16[3,4,16,128]{3,2,1,0:T(8,128)(2,1)S(1)}, bf16[3,4,16,128]{3,2,1,0:T(8,128)(2,1)S(1)}, u32[]{:S(2)}, u32[]{:S(2)}) collective-permute-start(bf16[3,4,16,128]{3,2,1,0:T(8,128)(2,1)S(1)} %get-tuple-element.43), channel_id=1, source_target_pairs={{0,24},{1,25},{2,28},{3,29},{4,26},{5,27},{6,30},{7,31},{8,16},{9,... | collective-permute-start | bytes 147464 | tf_op jit(solution)/shard_map/ppermute | solution.py:459
  33.8 10.5 %collective-permute-start.5 = (bf16[3,4,16,128]{3,2,1,0:T(8,128)(2,1)S(1)}, bf16[3,4,16,128]{3,2,1,0:T(8,128)(2,1)S(1)}, u32[]{:S(2)}, u32[]{:S(2)}) collective-permute-start(bf16[3,4,16,128]{3,2,1,0:T(8,128)(2,1)S(1)} %get-tuple-element.44), channel_id=1, source_target_pairs={{0,26},{1,27},{2,30},{3,31},{4,24},{5,25},{6,28},{7,29},{8,18},{9,... | collective-permute-start | bytes 147464 | tf_op jit(solution)/shard_map/ppermute | solution.py:459
  35.6 8.7 %collective-permute-start.6 = (bf16[3,4,16,128]{3,2,1,0:T(8,128)(2,1)S(1)}, bf16[3,4,16,128]{3,2,1,0:T(8,128)(2,1)S(1)}, u32[]{:S(2)}, u32[]{:S(2)}) collective-permute-start(bf16[3,4,16,128]{3,2,1,0:T(8,128)(2,1)S(1)} %get-tuple-element.45), channel_id=1, source_target_pairs={{0,16},{1,17},{2,20},{3,21},{4,18},{5,19},{6,22},{7,23},{8,24},{9,... | collective-permute-start | bytes 147464 | tf_op jit(solution)/shard_map/ppermute | solution.py:459
  35.6 8.7 %collective-permute-start.7 = (bf16[3,4,16,128]{3,2,1,0:T(8,128)(2,1)S(1)}, bf16[3,4,16,128]{3,2,1,0:T(8,128)(2,1)S(1)}, u32[]{:S(2)}, u32[]{:S(2)}) collective-permute-start(bf16[3,4,16,128]{3,2,1,0:T(8,128)(2,1)S(1)} %get-tuple-element.46), channel_id=1, source_target_pairs={{0,18},{1,19},{2,22},{3,23},{4,16},{5,17},{6,20},{7,21},{8,26},{9,... | collective-permute-start | bytes 147464 | tf_op jit(solution)/shard_map/ppermute | solution.py:459
  40.4 4.4 %collective-permute-start.8 = (bf16[3,4,16,128]{3,2,1,0:T(8,128)(2,1)S(1)}, bf16[3,4,16,128]{3,2,1,0:T(8,128)(2,1)S(1)}, u32[]{:S(2)}, u32[]{:S(2)}) collective-permute-start(bf16[3,4,16,128]{3,2,1,0:T(8,128)(2,1)S(1)} %get-tuple-element.47), channel_id=1, source_target_pairs={{0,8},{1,9},{2,12},{3,13},{4,10},{5,11},{6,14},{7,15},{8,0},{9,1},... | collective-permute-start | bytes 147464 | tf_op jit(solution)/shard_map/ppermute | solution.py:459
  41.9 5.0 %collective-permute-start.9 = (bf16[3,4,16,128]{3,2,1,0:T(8,128)(2,1)S(1)}, bf16[3,4,16,128]{3,2,1,0:T(8,128)(2,1)S(1)}, u32[]{:S(2)}, u32[]{:S(2)}) collective-permute-start(bf16[3,4,16,128]{3,2,1,0:T(8,128)(2,1)S(1)} %get-tuple-element.48), channel_id=1, source_target_pairs={{0,10},{1,11},{2,14},{3,15},{4,8},{5,9},{6,12},{7,13},{8,2},{9,3},... | collective-permute-start | bytes 147464 | tf_op jit(solution)/shard_map/ppermute | solution.py:459
  48.8 8.6 %collective-permute-start.16 = (bf16[3,4,3,16,128]{4,3,2,1,0:T(8,128)(2,1)S(1)}, bf16[3,4,3,16,128]{4,3,2,1,0:T(8,128)(2,1)S(1)}, u32[]{:S(2)}, u32[]{:S(2)}) collective-permute-start(bf16[3,4,3,16,128]{4,3,2,1,0:T(8,128)(2,1)S(1)} %get-tuple-element.59), channel_id=1, source_target_pairs={{0,24},{4,28},{8,16},{12,20},{16,8},{20,12},{24,0},{28,4},{1,25},{... | collective-permute-start | bytes 442376 | tf_op jit(solution)/shard_map/ppermute | solution.py:449
  51.1 9.7 %collective-permute-start.17 = (bf16[3,4,3,16,128]{4,3,2,1,0:T(8,128)(2,1)S(1)}, bf16[3,4,3,16,128]{4,3,2,1,0:T(8,128)(2,1)S(1)}, u32[]{:S(2)}, u32[]{:S(2)}) collective-permute-start(bf16[3,4,3,16,128]{4,3,2,1,0:T(8,128)(2,1)S(1)} %get-tuple-element.60), channel_id=1, source_target_pairs={{0,28},{4,24},{8,20},{12,16},{16,12},{20,8},{24,4},{28,0},{1,29},{... | collective-permute-start | bytes 442376 | tf_op jit(solution)/shard_map/ppermute | solution.py:449
  52.9 14.6 %collective-permute-start.18 = (bf16[3,4,3,16,128]{4,3,2,1,0:T(8,128)(2,1)S(1)}, bf16[3,4,3,16,128]{4,3,2,1,0:T(8,128)(2,1)S(1)}, u32[]{:S(2)}, u32[]{:S(2)}) collective-permute-start(bf16[3,4,3,16,128]{4,3,2,1,0:T(8,128)(2,1)S(1)} %get-tuple-element.61), channel_id=1, source_target_pairs={{0,12},{4,8},{8,4},{12,0},{16,28},{20,24},{24,20},{28,16},{1,13},{... | collective-permute-start | bytes 442376 | tf_op jit(solution)/shard_map/ppermute | solution.py:449
  52.9 14.6 %collective-permute-start.19 = (bf16[3,4,3,16,128]{4,3,2,1,0:T(8,128)(2,1)S(1)}, bf16[3,4,3,16,128]{4,3,2,1,0:T(8,128)(2,1)S(1)}, u32[]{:S(2)}, u32[]{:S(2)}) collective-permute-start(bf16[3,4,3,16,128]{4,3,2,1,0:T(8,128)(2,1)S(1)} %get-tuple-element.62), channel_id=1, source_target_pairs={{0,8},{4,12},{8,0},{12,4},{16,24},{20,28},{24,16},{28,20},{1,9},{5... | collective-permute-start | bytes 442376 | tf_op jit(solution)/shard_map/ppermute | solution.py:449
  55.6 11.9 %collective-permute-start.20 = (bf16[3,4,3,16,128]{4,3,2,1,0:T(8,128)(2,1)S(1)}, bf16[3,4,3,16,128]{4,3,2,1,0:T(8,128)(2,1)S(1)}, u32[]{:S(2)}, u32[]{:S(2)}) collective-permute-start(bf16[3,4,3,16,128]{4,3,2,1,0:T(8,128)(2,1)S(1)} %get-tuple-element.63), channel_id=1, source_target_pairs={{0,4},{4,0},{8,12},{12,8},{16,20},{20,16},{24,28},{28,24},{1,5},{5... | collective-permute-start | bytes 442376 | tf_op jit(solution)/shard_map/ppermute | solution.py:449
  57.4 13.4 %collective-permute-start.14 = (bf16[3,4,3,16,128]{4,3,2,1,0:T(8,128)(2,1)S(1)}, bf16[3,4,3,16,128]{4,3,2,1,0:T(8,128)(2,1)S(1)}, u32[]{:S(2)}, u32[]{:S(2)}) collective-permute-start(bf16[3,4,3,16,128]{4,3,2,1,0:T(8,128)(2,1)S(1)} %get-tuple-element.57), channel_id=1, source_target_pairs={{0,20},{4,16},{8,28},{12,24},{16,4},{20,0},{24,12},{28,8},{1,21},{... | collective-permute-start | bytes 442376 | tf_op jit(solution)/shard_map/ppermute | solution.py:449
  60.7 11.0 %collective-permute-start.15 = (bf16[3,4,3,16,128]{4,3,2,1,0:T(8,128)(2,1)S(1)}, bf16[3,4,3,16,128]{4,3,2,1,0:T(8,128)(2,1)S(1)}, u32[]{:S(2)}, u32[]{:S(2)}) collective-permute-start(bf16[3,4,3,16,128]{4,3,2,1,0:T(8,128)(2,1)S(1)} %get-tuple-element.58), channel_id=1, source_target_pairs={{0,16},{4,20},{8,24},{12,28},{16,0},{20,4},{24,8},{28,12},{1,17},{... | collective-permute-start | bytes 442376 | tf_op jit(solution)/shard_map/ppermute | solution.py:449

commit v6 on v5

--- a/solution.py
+++ b/solution.py
@@ -242,25 +242,32 @@
     outs, res, sems = refs[:n_tm], refs[n_tm], refs[n_tm + 1]
     me, fs = lax.axis_index("tm"), lax.axis_index("fsdp")
     half, core = fs // 2, lax.rem(fs, 2)
+    p_rows = outs[0].shape[2]
+    y, z = lax.rem(me, 2), me // 2
+    own, other = [], []
+    for j, r in enumerate(ROUNDS):
+        there_z = z ^ (r // 2)
+        part = pl.ds(pl.multiple_of((there_z // 2) * p_rows, p_rows), p_rows)
+        at = lax.rem(there_z, 2)
+        own.append(
+            pltpu.make_async_copy(own_ref.at[at, 0, :, :, part], outs[j], sems.at[j])
+        )
+        other.append(pltpu.make_async_copy(res.at[at, :, :, part], outs[j], sems.at[j]))
+    mine = [half == y ^ (r % 2) for r in ROUNDS]
+    for copy, here in zip(own, mine):
+        pl.when(here)(copy.start)
     rows = flat(other_ref)
     for i in range(2):
-        project_into(res, 1, core ^ i, dot(rows, w_ref[i], NT).astype(jnp.bfloat16))
-    for i in range(2):
-        res[i, 0] = own_ref[i, 0]
-    p_rows = outs[0].shape[2]
-    y, z = lax.rem(me, 2), me // 2
-    copies = []
-    for j, r in enumerate(ROUNDS):
-        there_z, there_x = z ^ (r // 2), y ^ (r % 2)
-        part = pl.ds(pl.multiple_of((there_z // 2) * p_rows, p_rows), p_rows)
-        copies.append(
-            pltpu.make_async_copy(
-                res.at[lax.rem(there_z, 2), half ^ there_x, :, :, part],
-                outs[j],
-                sems.at[j],
+        out = dot(rows, w_ref[i], NT).astype(jnp.bfloat16)
+        g_heads, frames_dev, pos_dev, head_size = res.shape[1:]
+        for h in range(g_heads):
+            res[core ^ i, h] = out[:, h * head_size : (h + 1) * head_size].reshape(
+                frames_dev, pos_dev, head_size
             )
-        )
-    copy_all(copies)
+    for copy, here in zip(other, mine):
+        pl.when(jnp.logical_not(here))(copy.start)
+    for copy in other:
+        copy.wait()
 
 
 def project_cost(own, w_own, weight):
@@ -304,7 +311,7 @@
         in_specs=[VMEM] * 3,
         out_specs=[ANY] * n_tm,
         scratch_shapes=[
-            pltpu.VMEM((2, 2) + res_own.shape[2:], jnp.bfloat16),
+            pltpu.VMEM((2,) + res_own.shape[2:], jnp.bfloat16),
             pltpu.SemaphoreType.DMA((n_tm,)),
         ],
         compiler_params=pltpu.CompilerParams(vmem_limit_bytes=14 * MIB),

time: 73 us -> 73 us (level)
  no operation moved by 1% of the time
where the time goes in v6:
time: 73 us; the launch traced here: 72.5 us
  starting transfers between devices  47.5 us (65%)
  Pallas kernels  15.1 us (21%)
  waiting for transfers between devices  9.19 us (13%)
  between operations  0.76 us (1%)
    ppermute x11, starting transfers between devices, send(): lax.ppermute(message, 'tm', [(i, i ^ k) for i in range(n_tm)])  24.1 us
    ppermute x8, starting transfers between devices, round_of(): return lax.ppermute(message, ('tm', 'fsdp'), pairs)  15.7 us
    ppermute x11, waiting for transfers between devices, send(): lax.ppermute(message, 'tm', [(i, i ^ k) for i in range(n_tm)])  6.61 us
    all_to_all x1, starting transfers between devices, body_permutes(): lax.all_to_all(near_message, 'tm', split_axis=0, concat_axis=0, axis_inde...  4.66 us
    pallas_call x1, Pallas kernels, project_own(): pl.pallas_call(project_own_kernel, out_shape=[jax.ShapeDtypeStruct((2, 1,...  3.92 us
    ppermute x2, starting transfers between devices, swap(): return lax.ppermute(x, 'fsdp', [(i, i ^ bit) for i in range(n_fsdp)])  3.09 us
    ppermute x8, waiting for transfers between devices, round_of(): return lax.ppermute(message, ('tm', 'fsdp'), pairs)  2.58 us
    pallas_call x1, Pallas kernels, pack_near(): pl.pallas_call(pack_near_kernel, out_shape=jax.ShapeDtypeStruct(shape, q_...  2.04 us
  transfers between devices with their start and end apart: 22, of which 7 were waited for; matrix products, arithmetic and copies ran while one was open for 0% of the time, Pallas kernels for 17%

profile of v6, /device:TPU:0, one launch (start us, length us, event | category | flops | bytes accessed | tf_op | source)
XLA Modules:
  0.0 72.5 jit_solution(10032955592783713244)
XLA Ops:
  0.6 0.5 collective-permute-start.1
  1.1 2.6 %collective-permute-start = (bf16[4,32,3072]{2,1,0:T(8,128)(2,1)}, bf16[4,32,3072]{2,1,0:T(8,128)(2,1)S(1)}, u32[]{:S(2)}, u32[]{:S(2)}) collective-permute-start(bf16[4,32,3072]{2,1,0:T(8,128)(2,1)} %own_ref.1), channel_id=1, source_target_pairs={{0,2},{1,3},{2,0},{3,1},{4,6},{5,7},{6,4},{7,5},{8,10},{9,11},{10,... | collective-permute-start | bytes 2359304 | tf_op jit(solution)/shard_map/ppermute | solution.py:453
  3.7 1.8 %pack_far.1 = (bf16[3,4,3,16,128]{4,3,2,1,0:T(8,128)(2,1)S(1)}, bf16[3,4,3,16,128]{4,3,2,1,0:T(8,128)(2,1)S(1)}, bf16[3,4,3,16,128]{4,3,2,1,0:T(8,128)(2,1)S(1)}, bf16[3,4,3,16,128]{4,3,2,1,0:T(8,128)(2,1)S(1)}) custom-call(bf16[4,12,32,128]{3,2,1,0:T(8,128)(2,1)} %bitcast.6, bf16[4,12,32,128]{3,2,1,0:T(8,128)(2,1)} %bitcast.8, bf16[4,12,32,128]{3,2,1,0:T(8,128)(2,1)} %bitcast.10), custom_call_target="tpu_custom_call" | custom-call | tf_op jit(solution)/shard_map/pack_far/pallas_call | solution.py:149
  5.5 4.6 %collective-permute-start.10 = (bf16[3,4,3,16,128]{4,3,2,1,0:T(8,128)(2,1)S(1)}, bf16[3,4,3,16,128]{4,3,2,1,0:T(8,128)(2,1)S(1)}, u32[]{:S(2)}, u32[]{:S(2)}) collective-permute-start(bf16[3,4,3,16,128]{4,3,2,1,0:T(8,128)(2,1)S(1)} %get-tuple-element.49), channel_id=1, source_target_pairs={{0,28},{4,24},{8,20},{12,16},{16,12},{20,8},{24,4},{28,0},{1,29},{... | collective-permute-start | bytes 442376 | tf_op jit(solution)/shard_map/ppermute | solution.py:456
  10.1 0.2 collective-permute-start.11
  10.3 0.8 %collective-permute-start.12 = (bf16[3,4,3,16,128]{4,3,2,1,0:T(8,128)(2,1)S(1)}, bf16[3,4,3,16,128]{4,3,2,1,0:T(8,128)(2,1)S(1)}, u32[]{:S(2)}, u32[]{:S(2)}) collective-permute-start(bf16[3,4,3,16,128]{4,3,2,1,0:T(8,128)(2,1)S(1)} %get-tuple-element.51), channel_id=1, source_target_pairs={{0,16},{4,20},{8,24},{12,28},{16,0},{20,4},{24,8},{28,12},{1,17},{... | collective-permute-start | bytes 442376 | tf_op jit(solution)/shard_map/ppermute | solution.py:456
  11.1 2.0 %pack_near.1 = bf16[4,3,4,3,16,128]{5,4,3,2,1,0:T(8,128)(2,1)} custom-call(bf16[4,12,32,128]{3,2,1,0:T(8,128)(2,1)} %bitcast.7, bf16[4,12,32,128]{3,2,1,0:T(8,128)(2,1)} %bitcast.9, bf16[4,12,32,128]{3,2,1,0:T(8,128)(2,1)} %bitcast.11), custom_call_target="tpu_custom_call" | custom-call | tf_op jit(solution)/shard_map/pack_near/pallas_call | solution.py:166
  13.2 4.7 %all-to-all-start = ((bf16[4,3,4,3,16,128]{5,4,3,2,1,0:T(8,128)(2,1)}), bf16[4,3,4,3,16,128]{5,4,3,2,1,0:T(8,128)(2,1)S(1)}, u32[]{:S(2)}, u32[]{:S(2)}) async-start(bf16[4,3,4,3,16,128]{5,4,3,2,1,0:T(8,128)(2,1)} %pack_near.1), calls=%async_computation | async-start | bytes 1179648 | tf_op jit(solution)/shard_map/all_to_all | solution.py:477
  17.8 0.0 collective-permute-done.1.w_other_ref
  17.8 2.4 %collective-permute-start.13 = (bf16[3,4,3,16,128]{4,3,2,1,0:T(8,128)(2,1)S(1)}, bf16[3,4,3,16,128]{4,3,2,1,0:T(8,128)(2,1)S(1)}, u32[]{:S(2)}, u32[]{:S(2)}) collective-permute-start(bf16[3,4,3,16,128]{4,3,2,1,0:T(8,128)(2,1)S(1)} %get-tuple-element.52), channel_id=1, source_target_pairs={{0,20},{4,16},{8,28},{12,24},{16,4},{20,0},{24,12},{28,8},{1,21},{... | collective-permute-start | bytes 442376 | tf_op jit(solution)/shard_map/ppermute | solution.py:456
  20.2 3.9 %project_own.1 = (bf16[2,1,3,4,32,128]{5,4,3,2,1,0:T(8,128)(2,1)S(1)}, bf16[2,384,3072]{2,1,0:T(8,128)(2,1)S(1)}) custom-call(bf16[4,32,3072]{2,1,0:T(8,128)(2,1)} %own_ref.1, bf16[384,3072]{1,0:T(8,128)(2,1)} %w_own_ref.1, bf16[384,3072]{1,0:T(8,128)(2,1)} %collective-permute-done.1.w_other_ref), custom_call_target="tpu_custom_call" | custom-call | flops 603979776 | bytes 5505024 | tf_op jit(solution)/shard_map/project_own/pallas_call | solution.py:285
  24.2 0.0 collective-permute-done.other_ref
  24.2 1.7 %project_other.1 = (bf16[3,4,16,128]{3,2,1,0:T(8,128)(2,1)S(1)}, bf16[3,4,16,128]{3,2,1,0:T(8,128)(2,1)S(1)}, bf16[3,4,16,128]{3,2,1,0:T(8,128)(2,1)S(1)}, bf16[...) custom-call(bf16[4,32,3072]{2,1,0:T(8,128)(2,1)S(1)} %collective-per, ...), custom_call_target="tpu_custom_call" | custom-call | flops 9663676416 | bytes 5505024 | tf_op jit(solution)/shard_map/project_other/pallas_call | solution.py:308
  25.9 0.7 collective-permute-start.2
  26.6 0.0 collective-permute-done.10.refs_0_
  26.6 2.9 %collective-permute-start.3 = (bf16[3,4,16,128]{3,2,1,0:T(8,128)(2,1)S(1)}, bf16[3,4,16,128]{3,2,1,0:T(8,128)(2,1)S(1)}, u32[]{:S(2)}, u32[]{:S(2)}) collective-permute-start(bf16[3,4,16,128]{3,2,1,0:T(8,128)(2,1)S(1)} %get-tuple-element.42), channel_id=1, source_target_pairs={{0,2},{1,3},{2,6},{3,7},{4,0},{5,1},{6,4},{7,5},{8,10},{9,11},{10,... | collective-permute-start | bytes 147464 | tf_op jit(solution)/shard_map/ppermute | solution.py:466
  29.5 0.0 collective-permute-done.11.refs_1_
  29.5 3.6 %collective-permute-start.4 = (bf16[3,4,16,128]{3,2,1,0:T(8,128)(2,1)S(1)}, bf16[3,4,16,128]{3,2,1,0:T(8,128)(2,1)S(1)}, u32[]{:S(2)}, u32[]{:S(2)}) collective-permute-start(bf16[3,4,16,128]{3,2,1,0:T(8,128)(2,1)S(1)} %get-tuple-element.43), channel_id=1, source_target_pairs={{0,24},{1,25},{2,28},{3,29},{4,26},{5,27},{6,30},{7,31},{8,16},{9,... | collective-permute-start | bytes 147464 | tf_op jit(solution)/shard_map/ppermute | solution.py:466
  33.0 0.8 %collective-permute-done.12.refs_2_ = bf16[3,4,3,16,128]{4,3,2,1,0:T(8,128)(2,1)S(1)} collective-permute-done((bf16[3,4,3,16,128]{4,3,2,1,0:T(8,128)(2,1)S(1)}, bf16[3,4,3,16,128]{4,3,2,1,0:T(8,128)(2,1)S(1)}, u32[]{:S(2)}, u32[]{:S(2)}) %collective-permute-start.12) | collective-permute-done | bytes 147488 | tf_op jit(solution)/shard_map/ppermute | solution.py:456
  33.8 1.8 %collective-permute-start.5 = (bf16[3,4,16,128]{3,2,1,0:T(8,128)(2,1)S(1)}, bf16[3,4,16,128]{3,2,1,0:T(8,128)(2,1)S(1)}, u32[]{:S(2)}, u32[]{:S(2)}) collective-permute-start(bf16[3,4,16,128]{3,2,1,0:T(8,128)(2,1)S(1)} %get-tuple-element.44), channel_id=1, source_target_pairs={{0,26},{1,27},{2,30},{3,31},{4,24},{5,25},{6,28},{7,29},{8,18},{9,... | collective-permute-start | bytes 147464 | tf_op jit(solution)/shard_map/ppermute | solution.py:466
  35.6 0.0 collective-permute-done.2.refs_0_
  35.6 0.0 collective-permute-start.6
  35.6 0.0 collective-permute-done.3.refs_1_
  35.6 4.7 %collective-permute-start.7 = (bf16[3,4,16,128]{3,2,1,0:T(8,128)(2,1)S(1)}, bf16[3,4,16,128]{3,2,1,0:T(8,128)(2,1)S(1)}, u32[]{:S(2)}, u32[]{:S(2)}) collective-permute-start(bf16[3,4,16,128]{3,2,1,0:T(8,128)(2,1)S(1)} %get-tuple-element.46), channel_id=1, source_target_pairs={{0,18},{1,19},{2,22},{3,23},{4,16},{5,17},{6,20},{7,21},{8,26},{9,... | collective-permute-start | bytes 147464 | tf_op jit(solution)/shard_map/ppermute | solution.py:466
  40.4 0.0 collective-permute-done.4.refs_2_
  40.4 1.5 %collective-permute-start.8 = (bf16[3,4,16,128]{3,2,1,0:T(8,128)(2,1)S(1)}, bf16[3,4,16,128]{3,2,1,0:T(8,128)(2,1)S(1)}, u32[]{:S(2)}, u32[]{:S(2)}) collective-permute-start(bf16[3,4,16,128]{3,2,1,0:T(8,128)(2,1)S(1)} %get-tuple-element.47), channel_id=1, source_target_pairs={{0,8},{1,9},{2,12},{3,13},{4,10},{5,11},{6,14},{7,15},{8,0},{9,1},... | collective-permute-start | bytes 147464 | tf_op jit(solution)/shard_map/ppermute | solution.py:466
  41.9 0.0 collective-permute-done.13.refs_3_
  41.9 0.5 collective-permute-start.9
  42.4 0.0 all-to-all-done.refs_4_
  42.4 1.9 %probs.1 = (bf16[12,128,128]{2,1,0:T(8,128)(2,1)S(1)}, bf16[12,128,128]{2,1,0:T(8,128)(2,1)S(1)}, bf16[12,128,128]{2,1,0:T(8,128)(2,1)S(1)}, f32[12,128,128]{2,1,0:T(8,128)S(1)}) custom-call(bf16[3,4,3,16,128]{4,3,2,1,0:T(8,128)(2,1)S(1)} %collective-permute-done.10.refs_0_, bf16[3,4,3,16,128]{4,3,2,1,0:T(8,128)(2,1)S(1)} %collective-permute-done.11.refs_1_, ...), custom_call_target="tpu_custom_call" | custom-call | tf_op jit(solution)/shard_map/probs/pallas_call | solution.py:412
  44.3 0.0 collective-permute-done.5.refs_3_
  44.3 0.0 collective-permute-done.6.refs_4_
  44.3 0.0 collective-permute-done.7.refs_5_
  44.3 0.4 collective-permute-done.8.refs_6_
  44.8 2.1 %collective-permute-done.9.refs_7_ = bf16[3,4,16,128]{3,2,1,0:T(8,128)(2,1)S(1)} collective-permute-done((bf16[3,4,16,128]{3,2,1,0:T(8,128)(2,1)S(1)}, bf16[3,4,16,128]{3,2,1,0:T(8,128)(2,1)S(1)}, u32[]{:S(2)}, u32[]{:S(2)}) %collective-permute-start.9) | collective-permute-done | bytes 49184 | tf_op jit(solution)/shard_map/ppermute | solution.py:466
  46.9 1.9 %grads.1 = (bf16[3,4,3,16,128]{4,3,2,1,0:T(8,128)(2,1)S(1)}, bf16[3,4,3,16,128]{4,3,2,1,0:T(8,128)(2,1)S(1)}, bf16[3,4,3,16,128]{4,3,2,1,0:T(8,128)(2,1)S(1)}, b...) custom-call(bf16[3,4,16,128]{3,2,1,0:T(8,128)(2,1)S(1)} %collective-, ...), custom_call_target="tpu_custom_call" | custom-call | tf_op jit(solution)/shard_map/grads/pallas_call | solution.py:428
  48.8 2.3 %collective-permute-start.16 = (bf16[3,4,3,16,128]{4,3,2,1,0:T(8,128)(2,1)S(1)}, bf16[3,4,3,16,128]{4,3,2,1,0:T(8,128)(2,1)S(1)}, u32[]{:S(2)}, u32[]{:S(2)}) collective-permute-start(bf16[3,4,3,16,128]{4,3,2,1,0:T(8,128)(2,1)S(1)} %get-tuple-element.59), channel_id=1, source_target_pairs={{0,24},{4,28},{8,16},{12,20},{16,8},{20,12},{24,0},{28,4},{1,25},{... | collective-permute-start | bytes 442376 | tf_op jit(solution)/shard_map/ppermute | solution.py:456
  51.1 1.8 %collective-permute-start.17 = (bf16[3,4,3,16,128]{4,3,2,1,0:T(8,128)(2,1)S(1)}, bf16[3,4,3,16,128]{4,3,2,1,0:T(8,128)(2,1)S(1)}, u32[]{:S(2)}, u32[]{:S(2)}) collective-permute-start(bf16[3,4,3,16,128]{4,3,2,1,0:T(8,128)(2,1)S(1)} %get-tuple-element.60), channel_id=1, source_target_pairs={{0,28},{4,24},{8,20},{12,16},{16,12},{20,8},{24,4},{28,0},{1,29},{... | collective-permute-start | bytes 442376 | tf_op jit(solution)/shard_map/ppermute | solution.py:456
  52.9 2.7 %collective-permute-start.19 = (bf16[3,4,3,16,128]{4,3,2,1,0:T(8,128)(2,1)S(1)}, bf16[3,4,3,16,128]{4,3,2,1,0:T(8,128)(2,1)S(1)}, u32[]{:S(2)}, u32[]{:S(2)}) collective-permute-start(bf16[3,4,3,16,128]{4,3,2,1,0:T(8,128)(2,1)S(1)} %get-tuple-element.62), channel_id=1, source_target_pairs={{0,8},{4,12},{8,0},{12,4},{16,24},{20,28},{24,16},{28,20},{1,9},{5... | collective-permute-start | bytes 442376 | tf_op jit(solution)/shard_map/ppermute | solution.py:456
  55.6 0.8 %collective-permute-start.20 = (bf16[3,4,3,16,128]{4,3,2,1,0:T(8,128)(2,1)S(1)}, bf16[3,4,3,16,128]{4,3,2,1,0:T(8,128)(2,1)S(1)}, u32[]{:S(2)}, u32[]{:S(2)}) collective-permute-start(bf16[3,4,3,16,128]{4,3,2,1,0:T(8,128)(2,1)S(1)} %get-tuple-element.63), channel_id=1, source_target_pairs={{0,4},{4,0},{8,12},{12,8},{16,20},{20,16},{24,28},{28,24},{1,5},{5... | collective-permute-start | bytes 442376 | tf_op jit(solution)/shard_map/ppermute | solution.py:456
  56.4 1.0 %collective-permute-done.16.refs_0_ = bf16[3,4,3,16,128]{4,3,2,1,0:T(8,128)(2,1)S(1)} collective-permute-done((bf16[3,4,3,16,128]{4,3,2,1,0:T(8,128)(2,1)S(1)}, bf16[3,4,3,16,128]{4,3,2,1,0:T(8,128)(2,1)S(1)}, u32[]{:S(2)}, u32[]{:S(2)}) %collective-permute-start.16) | collective-permute-done | bytes 147488 | tf_op jit(solution)/shard_map/ppermute | solution.py:456
  57.4 1.8 %collective-permute-start.14 = (bf16[3,4,3,16,128]{4,3,2,1,0:T(8,128)(2,1)S(1)}, bf16[3,4,3,16,128]{4,3,2,1,0:T(8,128)(2,1)S(1)}, u32[]{:S(2)}, u32[]{:S(2)}) collective-permute-start(bf16[3,4,3,16,128]{4,3,2,1,0:T(8,128)(2,1)S(1)} %get-tuple-element.57), channel_id=1, source_target_pairs={{0,20},{4,16},{8,28},{12,24},{16,4},{20,0},{24,12},{28,8},{1,21},{... | collective-permute-start | bytes 442376 | tf_op jit(solution)/shard_map/ppermute | solution.py:456
  59.2 1.5 %collective-permute-done.17.refs_1_ = bf16[3,4,3,16,128]{4,3,2,1,0:T(8,128)(2,1)S(1)} collective-permute-done((bf16[3,4,3,16,128]{4,3,2,1,0:T(8,128)(2,1)S(1)}, bf16[3,4,3,16,128]{4,3,2,1,0:T(8,128)(2,1)S(1)}, u32[]{:S(2)}, u32[]{:S(2)}) %collective-permute-start.17) | collective-permute-done | bytes 147488 | tf_op jit(solution)/shard_map/ppermute | solution.py:456
  60.7 6.7 %collective-permute-start.15 = (bf16[3,4,3,16,128]{4,3,2,1,0:T(8,128)(2,1)S(1)}, bf16[3,4,3,16,128]{4,3,2,1,0:T(8,128)(2,1)S(1)}, u32[]{:S(2)}, u32[]{:S(2)}) collective-permute-start(bf16[3,4,3,16,128]{4,3,2,1,0:T(8,128)(2,1)S(1)} %get-tuple-element.58), channel_id=1, source_target_pairs={{0,16},{4,20},{8,24},{12,28},{16,0},{20,4},{24,8},{28,12},{1,17},{... | collective-permute-start | bytes 442376 | tf_op jit(solution)/shard_map/ppermute | solution.py:456
  67.4 1.1 %unpack.2 = (bf16[4,12,32,128]{3,2,1,0:T(8,128)(2,1)}, bf16[4,12,32,128]{3,2,1,0:T(8,128)(2,1)}, bf16[4,12,32,128]{3,2,1,0:T(8,128)(2,1)}) custom-call(bf16[3,4,3,16,128]{4,3,2,1,0:T(8,128)(2,1)S(1)} %collective-permute-done.16.refs_0_, bf16[3,4,3,16,128]{4,3,2,1,0:T(8,128)(2,1)S(1)} %collective-permute-done.17.refs_1_, ...), custom_call_target="tpu_custom_call" | custom-call | tf_op jit(solution)/shard_map/unpack/pallas_call | solution.py:200
  68.5 2.3 %collective-permute-done.14.refs_0_ = bf16[3,4,3,16,128]{4,3,2,1,0:T(8,128)(2,1)S(1)} collective-permute-done((bf16[3,4,3,16,128]{4,3,2,1,0:T(8,128)(2,1)S(1)}, bf16[3,4,3,16,128]{4,3,2,1,0:T(8,128)(2,1)S(1)}, u32[]{:S(2)}, u32[]{:S(2)}) %collective-permute-start.14) | collective-permute-done | bytes 147488 | tf_op jit(solution)/shard_map/ppermute | solution.py:456
  70.8 1.0 %collective-permute-done.15.refs_1_ = bf16[3,4,3,16,128]{4,3,2,1,0:T(8,128)(2,1)S(1)} collective-permute-done((bf16[3,4,3,16,128]{4,3,2,1,0:T(8,128)(2,1)S(1)}, bf16[3,4,3,16,128]{4,3,2,1,0:T(8,128)(2,1)S(1)}, u32[]{:S(2)}, u32[]{:S(2)}) %collective-permute-start.15) | collective-permute-done | bytes 147488 | tf_op jit(solution)/shard_map/ppermute | solution.py:456
  71.8 0.8 %unpack.3 = (bf16[4,12,32,128]{3,2,1,0:T(8,128)(2,1)}, bf16[4,12,32,128]{3,2,1,0:T(8,128)(2,1)}, bf16[4,12,32,128]{3,2,1,0:T(8,128)(2,1)}) custom-call(bf16[3,4,3,16,128]{4,3,2,1,0:T(8,128)(2,1)S(1)} %collective-permute-done.14.refs_0_, ...), custom_call_target="tpu_custom_call", output_to_operand_aliasing={{0}: (2, {}), {1}: (3, {}), {2}: (4, {})} | custom-call | tf_op jit(solution)/shard_map/unpack/pallas_call | solution.py:200
  (4 shorter events, 0.0 us)
Async XLA Ops:
  0.6 17.2 %collective-permute-start.1 = (bf16[384,3072]{1,0:T(8,128)(2,1)}, bf16[384,3072]{1,0:T(8,128)(2,1)}, u32[]{:S(2)}, u32[]{:S(2)}) collective-permute-start(bf16[384,3072]{1,0:T(8,128)(2,1)} %w_own_ref.1), channel_id=1, source_target_pairs={{0,1},{1,0},{2,3},{3,2},{4,5},{5,4},{6,7},{7,6},{8,9},{9,8},{10,11... | collective-permute-start | bytes 7077896 | tf_op jit(solution)/shard_map/ppermute | solution.py:453
  1.1 23.0 %collective-permute-start = (bf16[4,32,3072]{2,1,0:T(8,128)(2,1)}, bf16[4,32,3072]{2,1,0:T(8,128)(2,1)S(1)}, u32[]{:S(2)}, u32[]{:S(2)}) collective-permute-start(bf16[4,32,3072]{2,1,0:T(8,128)(2,1)} %own_ref.1), channel_id=1, source_target_pairs={{0,2},{1,3},{2,0},{3,1},{4,6},{5,7},{6,4},{7,5},{8,10},{9,11},{10,... | collective-permute-start | bytes 2359304 | tf_op jit(solution)/shard_map/ppermute | solution.py:453
  5.5 21.1 %collective-permute-start.10 = (bf16[3,4,3,16,128]{4,3,2,1,0:T(8,128)(2,1)S(1)}, bf16[3,4,3,16,128]{4,3,2,1,0:T(8,128)(2,1)S(1)}, u32[]{:S(2)}, u32[]{:S(2)}) collective-permute-start(bf16[3,4,3,16,128]{4,3,2,1,0:T(8,128)(2,1)S(1)} %get-tuple-element.49), channel_id=1, source_target_pairs={{0,28},{4,24},{8,20},{12,16},{16,12},{20,8},{24,4},{28,0},{1,29},{... | collective-permute-start | bytes 442376 | tf_op jit(solution)/shard_map/ppermute | solution.py:456
  10.1 19.3 %collective-permute-start.11 = (bf16[3,4,3,16,128]{4,3,2,1,0:T(8,128)(2,1)S(1)}, bf16[3,4,3,16,128]{4,3,2,1,0:T(8,128)(2,1)S(1)}, u32[]{:S(2)}, u32[]{:S(2)}) collective-permute-start(bf16[3,4,3,16,128]{4,3,2,1,0:T(8,128)(2,1)S(1)} %get-tuple-element.50), channel_id=1, source_target_pairs={{0,24},{4,28},{8,16},{12,20},{16,8},{20,12},{24,0},{28,4},{1,25},{... | collective-permute-start | bytes 442376 | tf_op jit(solution)/shard_map/ppermute | solution.py:456
  10.3 23.5 %collective-permute-start.12 = (bf16[3,4,3,16,128]{4,3,2,1,0:T(8,128)(2,1)S(1)}, bf16[3,4,3,16,128]{4,3,2,1,0:T(8,128)(2,1)S(1)}, u32[]{:S(2)}, u32[]{:S(2)}) collective-permute-start(bf16[3,4,3,16,128]{4,3,2,1,0:T(8,128)(2,1)S(1)} %get-tuple-element.51), channel_id=1, source_target_pairs={{0,16},{4,20},{8,24},{12,28},{16,0},{20,4},{24,8},{28,12},{1,17},{... | collective-permute-start | bytes 442376 | tf_op jit(solution)/shard_map/ppermute | solution.py:456
  13.2 29.2 %all-to-all-start = ((bf16[4,3,4,3,16,128]{5,4,3,2,1,0:T(8,128)(2,1)}), bf16[4,3,4,3,16,128]{5,4,3,2,1,0:T(8,128)(2,1)S(1)}, u32[]{:S(2)}, u32[]{:S(2)}) async-start(bf16[4,3,4,3,16,128]{5,4,3,2,1,0:T(8,128)(2,1)} %pack_near.1), calls=%async_computation | async-start | bytes 1179648 | tf_op jit(solution)/shard_map/all_to_all | solution.py:477
  17.8 24.1 %collective-permute-start.13 = (bf16[3,4,3,16,128]{4,3,2,1,0:T(8,128)(2,1)S(1)}, bf16[3,4,3,16,128]{4,3,2,1,0:T(8,128)(2,1)S(1)}, u32[]{:S(2)}, u32[]{:S(2)}) collective-permute-start(bf16[3,4,3,16,128]{4,3,2,1,0:T(8,128)(2,1)S(1)} %get-tuple-element.52), channel_id=1, source_target_pairs={{0,20},{4,16},{8,28},{12,24},{16,4},{20,0},{24,12},{28,8},{1,21},{... | collective-permute-start | bytes 442376 | tf_op jit(solution)/shard_map/ppermute | solution.py:456
  25.9 9.7 %collective-permute-start.2 = (bf16[3,4,16,128]{3,2,1,0:T(8,128)(2,1)S(1)}, bf16[3,4,16,128]{3,2,1,0:T(8,128)(2,1)S(1)}, u32[]{:S(2)}, u32[]{:S(2)}) collective-permute-start(bf16[3,4,16,128]{3,2,1,0:T(8,128)(2,1)S(1)} %get-tuple-element.41), channel_id=1, source_target_pairs={{0,0},{1,1},{2,4},{3,5},{4,2},{5,3},{6,6},{7,7},{8,8},{9,9},{10,12... | collective-permute-start | bytes 147464 | tf_op jit(solution)/shard_map/ppermute | solution.py:466
  26.6 9.1 %collective-permute-start.3 = (bf16[3,4,16,128]{3,2,1,0:T(8,128)(2,1)S(1)}, bf16[3,4,16,128]{3,2,1,0:T(8,128)(2,1)S(1)}, u32[]{:S(2)}, u32[]{:S(2)}) collective-permute-start(bf16[3,4,16,128]{3,2,1,0:T(8,128)(2,1)S(1)} %get-tuple-element.42), channel_id=1, source_target_pairs={{0,2},{1,3},{2,6},{3,7},{4,0},{5,1},{6,4},{7,5},{8,10},{9,11},{10,... | collective-permute-start | bytes 147464 | tf_op jit(solution)/shard_map/ppermute | solution.py:466
  29.5 10.9 %collective-permute-start.4 = (bf16[3,4,16,128]{3,2,1,0:T(8,128)(2,1)S(1)}, bf16[3,4,16,128]{3,2,1,0:T(8,128)(2,1)S(1)}, u32[]{:S(2)}, u32[]{:S(2)}) collective-permute-start(bf16[3,4,16,128]{3,2,1,0:T(8,128)(2,1)S(1)} %get-tuple-element.43), channel_id=1, source_target_pairs={{0,24},{1,25},{2,28},{3,29},{4,26},{5,27},{6,30},{7,31},{8,16},{9,... | collective-permute-start | bytes 147464 | tf_op jit(solution)/shard_map/ppermute | solution.py:466
  33.8 10.5 %collective-permute-start.5 = (bf16[3,4,16,128]{3,2,1,0:T(8,128)(2,1)S(1)}, bf16[3,4,16,128]{3,2,1,0:T(8,128)(2,1)S(1)}, u32[]{:S(2)}, u32[]{:S(2)}) collective-permute-start(bf16[3,4,16,128]{3,2,1,0:T(8,128)(2,1)S(1)} %get-tuple-element.44), channel_id=1, source_target_pairs={{0,26},{1,27},{2,30},{3,31},{4,24},{5,25},{6,28},{7,29},{8,18},{9,... | collective-permute-start | bytes 147464 | tf_op jit(solution)/shard_map/ppermute | solution.py:466
  35.6 8.7 %collective-permute-start.6 = (bf16[3,4,16,128]{3,2,1,0:T(8,128)(2,1)S(1)}, bf16[3,4,16,128]{3,2,1,0:T(8,128)(2,1)S(1)}, u32[]{:S(2)}, u32[]{:S(2)}) collective-permute-start(bf16[3,4,16,128]{3,2,1,0:T(8,128)(2,1)S(1)} %get-tuple-element.45), channel_id=1, source_target_pairs={{0,16},{1,17},{2,20},{3,21},{4,18},{5,19},{6,22},{7,23},{8,24},{9,... | collective-permute-start | bytes 147464 | tf_op jit(solution)/shard_map/ppermute | solution.py:466
  35.6 8.7 %collective-permute-start.7 = (bf16[3,4,16,128]{3,2,1,0:T(8,128)(2,1)S(1)}, bf16[3,4,16,128]{3,2,1,0:T(8,128)(2,1)S(1)}, u32[]{:S(2)}, u32[]{:S(2)}) collective-permute-start(bf16[3,4,16,128]{3,2,1,0:T(8,128)(2,1)S(1)} %get-tuple-element.46), channel_id=1, source_target_pairs={{0,18},{1,19},{2,22},{3,23},{4,16},{5,17},{6,20},{7,21},{8,26},{9,... | collective-permute-start | bytes 147464 | tf_op jit(solution)/shard_map/ppermute | solution.py:466
  40.4 4.4 %collective-permute-start.8 = (bf16[3,4,16,128]{3,2,1,0:T(8,128)(2,1)S(1)}, bf16[3,4,16,128]{3,2,1,0:T(8,128)(2,1)S(1)}, u32[]{:S(2)}, u32[]{:S(2)}) collective-permute-start(bf16[3,4,16,128]{3,2,1,0:T(8,128)(2,1)S(1)} %get-tuple-element.47), channel_id=1, source_target_pairs={{0,8},{1,9},{2,12},{3,13},{4,10},{5,11},{6,14},{7,15},{8,0},{9,1},... | collective-permute-start | bytes 147464 | tf_op jit(solution)/shard_map/ppermute | solution.py:466
  41.9 5.0 %collective-permute-start.9 = (bf16[3,4,16,128]{3,2,1,0:T(8,128)(2,1)S(1)}, bf16[3,4,16,128]{3,2,1,0:T(8,128)(2,1)S(1)}, u32[]{:S(2)}, u32[]{:S(2)}) collective-permute-start(bf16[3,4,16,128]{3,2,1,0:T(8,128)(2,1)S(1)} %get-tuple-element.48), channel_id=1, source_target_pairs={{0,10},{1,11},{2,14},{3,15},{4,8},{5,9},{6,12},{7,13},{8,2},{9,3},... | collective-permute-start | bytes 147464 | tf_op jit(solution)/shard_map/ppermute | solution.py:466
  48.8 8.6 %collective-permute-start.16 = (bf16[3,4,3,16,128]{4,3,2,1,0:T(8,128)(2,1)S(1)}, bf16[3,4,3,16,128]{4,3,2,1,0:T(8,128)(2,1)S(1)}, u32[]{:S(2)}, u32[]{:S(2)}) collective-permute-start(bf16[3,4,3,16,128]{4,3,2,1,0:T(8,128)(2,1)S(1)} %get-tuple-element.59), channel_id=1, source_target_pairs={{0,24},{4,28},{8,16},{12,20},{16,8},{20,12},{24,0},{28,4},{1,25},{... | collective-permute-start | bytes 442376 | tf_op jit(solution)/shard_map/ppermute | solution.py:456
  51.1 9.7 %collective-permute-start.17 = (bf16[3,4,3,16,128]{4,3,2,1,0:T(8,128)(2,1)S(1)}, bf16[3,4,3,16,128]{4,3,2,1,0:T(8,128)(2,1)S(1)}, u32[]{:S(2)}, u32[]{:S(2)}) collective-permute-start(bf16[3,4,3,16,128]{4,3,2,1,0:T(8,128)(2,1)S(1)} %get-tuple-element.60), channel_id=1, source_target_pairs={{0,28},{4,24},{8,20},{12,16},{16,12},{20,8},{24,4},{28,0},{1,29},{... | collective-permute-start | bytes 442376 | tf_op jit(solution)/shard_map/ppermute | solution.py:456
  52.9 14.5 %collective-permute-start.18 = (bf16[3,4,3,16,128]{4,3,2,1,0:T(8,128)(2,1)S(1)}, bf16[3,4,3,16,128]{4,3,2,1,0:T(8,128)(2,1)S(1)}, u32[]{:S(2)}, u32[]{:S(2)}) collective-permute-start(bf16[3,4,3,16,128]{4,3,2,1,0:T(8,128)(2,1)S(1)} %get-tuple-element.61), channel_id=1, source_target_pairs={{0,12},{4,8},{8,4},{12,0},{16,28},{20,24},{24,20},{28,16},{1,13},{... | collective-permute-start | bytes 442376 | tf_op jit(solution)/shard_map/ppermute | solution.py:456
  52.9 14.5 %collective-permute-start.19 = (bf16[3,4,3,16,128]{4,3,2,1,0:T(8,128)(2,1)S(1)}, bf16[3,4,3,16,128]{4,3,2,1,0:T(8,128)(2,1)S(1)}, u32[]{:S(2)}, u32[]{:S(2)}) collective-permute-start(bf16[3,4,3,16,128]{4,3,2,1,0:T(8,128)(2,1)S(1)} %get-tuple-element.62), channel_id=1, source_target_pairs={{0,8},{4,12},{8,0},{12,4},{16,24},{20,28},{24,16},{28,20},{1,9},{5... | collective-permute-start | bytes 442376 | tf_op jit(solution)/shard_map/ppermute | solution.py:456
  55.6 11.8 %collective-permute-start.20 = (bf16[3,4,3,16,128]{4,3,2,1,0:T(8,128)(2,1)S(1)}, bf16[3,4,3,16,128]{4,3,2,1,0:T(8,128)(2,1)S(1)}, u32[]{:S(2)}, u32[]{:S(2)}) collective-permute-start(bf16[3,4,3,16,128]{4,3,2,1,0:T(8,128)(2,1)S(1)} %get-tuple-element.63), channel_id=1, source_target_pairs={{0,4},{4,0},{8,12},{12,8},{16,20},{20,16},{24,28},{28,24},{1,5},{5... | collective-permute-start | bytes 442376 | tf_op jit(solution)/shard_map/ppermute | solution.py:456
  57.4 13.4 %collective-permute-start.14 = (bf16[3,4,3,16,128]{4,3,2,1,0:T(8,128)(2,1)S(1)}, bf16[3,4,3,16,128]{4,3,2,1,0:T(8,128)(2,1)S(1)}, u32[]{:S(2)}, u32[]{:S(2)}) collective-permute-start(bf16[3,4,3,16,128]{4,3,2,1,0:T(8,128)(2,1)S(1)} %get-tuple-element.57), channel_id=1, source_target_pairs={{0,20},{4,16},{8,28},{12,24},{16,4},{20,0},{24,12},{28,8},{1,21},{... | collective-permute-start | bytes 442376 | tf_op jit(solution)/shard_map/ppermute | solution.py:456
  60.7 11.1 %collective-permute-start.15 = (bf16[3,4,3,16,128]{4,3,2,1,0:T(8,128)(2,1)S(1)}, bf16[3,4,3,16,128]{4,3,2,1,0:T(8,128)(2,1)S(1)}, u32[]{:S(2)}, u32[]{:S(2)}) collective-permute-start(bf16[3,4,3,16,128]{4,3,2,1,0:T(8,128)(2,1)S(1)} %get-tuple-element.58), channel_id=1, source_target_pairs={{0,16},{4,20},{8,24},{12,28},{16,0},{20,4},{24,8},{28,12},{1,17},{... | collective-permute-start | bytes 442376 | tf_op jit(solution)/shard_map/ppermute | solution.py:456
